TPU v7x, 1024 devices: a whole 8x8x8 slice. The times are simulated.
1024 devices in a mesh: member: 8 (over y), lat: 32 (over z, x_hi), lon: 4 (over x_lo, core).
Axes of the slice: x: 8 (x_hi: 4, x_lo: 2; x = x_hi * 2 + x_lo), y: 8, z: 8, core: 2. Of those that a mesh axis runs over, the one named last changes fastest.
Arguments:
- members: bfloat16 [8, 16, 768, 1024], P('member', None, 'lat', 'lon'), may hold values from -9 to 9, as said below
- observed: bfloat16 [16, 768, 1024], P(None, 'lat', 'lon'), may hold values from -6 to 6
- scales: float32 [16], replicated, may hold values from 0.5 to 2
Outputs:
- cell_grad: float32 [8, 16, 768, 1024], P('member', None, 'lat', 'lon')
Inputs may be any that keep to these rules, and one draw needn't show every extreme that they name: `members`: each member is a zonal pattern of its own plus a field that varies from cell to cell.
All inputs are finite; a program needn't handle non-finite values.
Results may differ from a plain program's by a relative error of at most 0.0003.
Values may be sent and summed in bfloat16 or wider, within the bound.
No kernel may reach another device: no remote copies, remote signals or barrier semaphores. Data moves between devices by JAX's collectives and lax.ppermute only.
A program may use at most 32 MiB of HBM per device.

v0:
```python
import jax
import jax.numpy as jnp
from jax import lax
from jax.sharding import PartitionSpec as P

BAND = 1.0


def lat_weights(count):
    index = jnp.arange(count).astype(jnp.float32)
    angle = (-90.0 + (index + 0.5) * 180.0 / count) * (jnp.pi / 180.0)
    return jnp.cos(angle)


def per_device(members, observed, scales):
    me_index = lax.axis_index("member")
    member_count = lax.axis_size("member")
    own = members[0].astype(jnp.float32)
    obsf = observed.astype(jnp.float32)
    channels, rows, columns = own.shape
    total_rows = rows * lax.axis_size("lat")
    lon_count = columns * lax.axis_size("lon")
    weights_all = lat_weights(total_rows)
    sumw = jnp.sum(weights_all)
    local_w = lax.dynamic_slice_in_dim(weights_all, lax.axis_index("lat") * rows, rows)
    inv_sq = 1.0 / (scales * scales)
    field_wgt = local_w[None, :, None] * inv_sq[:, None, None] / (channels * lon_count * sumw)
    obs_part = jnp.sum(field_wgt * (own - obsf) ** 2)
    zonal_x, zonal_y = lax.psum((jnp.sum(own, axis=2), jnp.sum(obsf, axis=2)), "lon")
    zonal = zonal_x / lon_count
    zobs = zonal_y / lon_count
    zonal_all = lax.all_gather(zonal[None], "member", axis=0, tiled=True)
    zonal_wgt = local_w[None, :] * inv_sq[:, None] / (channels * sumw)
    leading = (lax.axis_index("lon") == 0).astype(jnp.float32)
    zonal_part = jnp.sum(zonal_wgt[None] * (zonal[None] - zonal_all) ** 2, axis=(1, 2)) * leading
    zobs_part = jnp.sum(zonal_wgt * (zonal - zobs) ** 2) * leading
    gathered = lax.all_gather(members, "member", axis=0, tiled=True)
    field_part = jnp.sum(
        field_wgt[None] * (own[None] - gathered.astype(jnp.float32)) ** 2, axis=(1, 2, 3)
    )
    dist, dobs, zdist, zdobs = lax.psum(
        (field_part, obs_part, zonal_part, zobs_part), ("lat", "lon")
    )
    offdiag = (jnp.arange(member_count) != me_index).astype(jnp.float32)
    pair_norm = member_count * (member_count - 1) * BAND
    acoef = jnp.exp(-dist / (2.0 * BAND)) / pair_norm * offdiag
    bcoef = jnp.exp(-dobs / (2.0 * BAND)) / (member_count * BAND)
    zacoef = jnp.exp(-zdist / (2.0 * BAND)) / pair_norm * offdiag
    zbcoef = jnp.exp(-zdobs / (2.0 * BAND)) / (member_count * BAND)
    mixed = jnp.einsum(
        "n,nclw->clw", acoef, gathered.astype(jnp.float32), precision=lax.Precision.HIGHEST
    )
    field_term = -jnp.sum(acoef) * own + mixed + bcoef * (own - obsf)
    zmixed = jnp.einsum("n,ncl->cl", zacoef, zonal_all, precision=lax.Precision.HIGHEST)
    zonal_term = -jnp.sum(zacoef) * zonal + zmixed + zbcoef * (zonal - zobs)
    factor = total_rows * local_w[None, :, None] * inv_sq[:, None, None] / sumw
    return (factor * (field_term + zonal_term[:, :, None]))[None]


def solution(mesh):
    placed = (P("member", None, "lat", "lon"), P(None, "lat", "lon"), P())
    return jax.shard_map(
        per_device,
        mesh=mesh,
        in_specs=placed,
        out_specs=P("member", None, "lat", "lon"),
        check_vma=False,
    )
```

profile of v0, /device:TPU:1, one launch (start us, length us, event | category | flops | bytes accessed | tf_op | source)
XLA Modules:
  0.0 332.8 jit_solution(12978687488487251777)
XLA Ops:
  6.5 0.0 all-gather.3.cloned.1.call-start
  6.5 0.7 all-gather.3.cloned.1.call-update
  7.3 0.6 fusion.8
  9.3 0.1 broadcast_multiply_fusion.2
  9.3 1.0 convert_reduce_fusion
  10.4 0.7 multiply_divide_fusion.3
  11.1 0.1 multiply_divide_fusion.1
  11.1 1.9 multiply_reduce_fusion.1
  13.0 22.0 %all-reduce.1 = (f32[16,24]{1,0:T(8,128)S(1)}, f32[16,24]{1,0:T(8,128)S(1)}) all-reduce(f32[16,24]{1,0:T(8,128)S(1)} %convert_reduce_fusion, f32[16,24]{1,0:T(8,128)S(1)} %get-tuple-element.6), channel_id=1, replica_groups=mesh['member'=8,'lat'=32,'lon'=4] {'lon'}, use_global_device_ids=true, to_apply=%region_7.0 | all-reduce | flops 768 | bytes 6144 | tf_op jit(solution)/shard_map/psum | solution.py:29
  35.0 1.4 multiply_reduce_fusion.3
  37.0 19.7 %all-gather = f32[128,24]{1,0:T(8,128)S(1)} all-gather(f32[16,24]{1,0:T(8,128)S(1)} %get-tuple-element.16), channel_id=2, replica_groups=mesh['member'=8,'lat'=32,'lon'=4] {'member'}, dimensions={0}, use_global_device_ids=true | all-gather | bytes 13824 | tf_op jit(solution)/shard_map/all_gather | solution.py:32
  56.6 0.1 multiply_reduce_fusion.2
  56.8 1.0 convert_bitcast_fusion
  57.8 0.0 copy-start.1
  57.8 0.0 copy-start.2
  57.8 5.7 %all-gather.3.cloned.1.call-done = bf16[8,16,24,256]{3,2,1,0:T(8,128)(2,1)} async-done(((bf16[1,16,24,256]{3,2,1,0:T(8,128)(2,1)}), bf16[8,16,24,256]{3,2,1,0:T(8,128)(2,1)}) %all-gather.3.cloned.1.call-update) | async-done | bytes 1572880 | tf_op jit(solution)/shard_map/all_gather | solution.py:37
  63.5 2.2 multiply_reduce_fusion
  65.6 253.9 %all-reduce = (f32[8]{0:T(128)S(1)}, f32[8]{0:T(128)S(1)}, f32[]{:T(128)}, f32[]{:T(128)}) all-reduce(f32[8]{0:T(128)S(1)} %multiply_reduce_fusion, f32[8]{0:T(128)S(1)} %broadcast_multiply_fusion.1, f32[]{:T(128)S(6)} %mul.174, f32[]{:T(128)} %get-tuple-element.5), channel_id=1, replica_groups=mesh['member'=8,'lat'=32,'lon'=4] {'lat','lon'}, use_global_device_ids=true, to_apply=%region_2.0 | all-reduce | flops 18 | bytes 144 | tf_op jit(solution)/shard_map/psum | solution.py:41
  320.3 0.2 fusion.6
  320.5 0.6 fusion.11
  323.1 0.0 copy-done
  323.1 1.9 fusion
  325.0 0.0 copy-done.1
  325.0 0.9 fusion.5
  (5 shorter events, 0.1 us)
Async XLA Ops:
  6.5 56.9 %all-gather.3.cloned.1.call-start = ((), (), s32[]{:S(2)}) async-start(), calls=%async_computation | async-start | bytes 1769472 | tf_op jit(solution)/shard_map/all_gather | solution.py:37
  57.8 267.2 %copy-start.1 = (bf16[1,16,24,256]{3,2,1,0:T(8,128)(2,1)S(1)}, bf16[1,16,24,256]{3,2,1,0:T(8,128)(2,1)}, u32[]{:S(2)}) copy-start(bf16[1,16,24,256]{3,2,1,0:T(8,128)(2,1)} %param.3) | copy-start | bytes 589828
  57.8 267.2 %copy-start.2 = (bf16[16,24,256]{2,1,0:T(8,128)(2,1)S(1)}, bf16[16,24,256]{2,1,0:T(8,128)(2,1)}, u32[]{:S(2)}) copy-start(bf16[16,24,256]{2,1,0:T(8,128)(2,1)} %param.4) | copy-start | bytes 589828
  63.5 259.6 %copy-start = (bf16[8,16,24,256]{3,2,1,0:T(8,128)(2,1)S(1)}, bf16[8,16,24,256]{3,2,1,0:T(8,128)(2,1)}, u32[]{:S(2)}) copy-start(bf16[8,16,24,256]{3,2,1,0:T(8,128)(2,1)} %all-gather.3.cloned.1.call-done) | copy-start | bytes 4718596
Sparse Core Ops, SparseCore 0:
  10.0 53.3 all-gather.2
where the time goes:
time: 333 us
  blocking collectives  296 us (89%)
  between operations  18.1 us (5%)
  other arithmetic  10.7 us (3%)
  waiting for transfers between devices  6.38 us (2%)
    psum x1, blocking collectives, per_device(): lax.psum((field_part, obs_part, zonal_part, zobs_part), ('lat', 'lon'))  254 us
    psum x1, blocking collectives, per_device(): lax.psum((jnp.sum(own, axis=2), jnp.sum(obsf, axis=2)), 'lon')  22 us
    all_gather x1, blocking collectives, per_device(): zonal_all = lax.all_gather(zonal[None], 'member', axis=0, tiled=True)  19.7 us
  transfers between devices with their start and end apart: 1, of which 1 were waited for; matrix products, arithmetic and copies ran while one was open for 2% of the time, Pallas kernels for 0%

commit v1 on v0

v1 whole, which is shorter than its diff:
```python
import functools

import jax
import jax.numpy as jnp
import numpy as np
from jax import lax
from jax.experimental import pallas as pl
from jax.experimental.pallas import tpu as pltpu
from jax.sharding import Mesh
from jax.sharding import PartitionSpec as P

BAND = 1.0
F32 = jnp.float32
BF16 = jnp.bfloat16
C, M, LAT, LON = 16, 8, 768, 1024
ROWS, COLS = 24, 256
CELLS = C * ROWS
GROUP = 32
HIGHEST = lax.Precision.HIGHEST


def total_weight():
    index = np.arange(LAT).astype(np.float32)
    angle = (np.float32(-90.0) + (index + np.float32(0.5)) * np.float32(180.0) / np.float32(LAT)) * np.float32(
        np.pi / 180.0
    )
    return float(np.sum(np.cos(angle.astype(np.float32)).astype(np.float64)))


SUMW = total_weight()


def row_weight(index):
    angle = (-90.0 + (index.astype(F32) + 0.5) * 180.0 / LAT) * np.float32(np.pi / 180.0)
    return jnp.cos(angle)


def iota(shape, axis):
    return lax.broadcasted_iota(jnp.int32, shape, axis)


def lat_index():
    return lax.axis_index("z") * 4 + lax.axis_index("xh")


def tile_weights(shape):
    return row_weight(lat_index() * ROWS + iota(shape, 0))


def inverse_square(scales_ref, c):
    s = scales_ref[c]
    return 1.0 / (s * s)


def lanes_sum(x):
    ones = jnp.ones((8, COLS), BF16)
    flat = x.reshape(CELLS, COLS).astype(BF16)
    return lax.dot_general(ones, flat, (((1,), (1,)), ((), ())), preferred_element_type=F32)


def part_of(part, block, lane):
    flat = block * 128 + lane
    return (flat >= part * (CELLS // M)) & (flat < (part + 1) * (CELLS // M))


def pack_kernel(own_ref, obs_ref, pay_ref):
    me = lax.axis_index("y")
    x = own_ref[0].astype(F32)
    zx = lanes_sum(x)
    zy = lanes_sum(obs_ref[...].astype(F32))
    row, lane = iota((8, 128), 0), iota((8, 128), 1)

    def high(v):
        return v.astype(BF16).astype(F32)

    part = jnp.zeros((8, 128), F32)
    extra = jnp.zeros((8, 128), F32)
    for k in range(3):
        part = jnp.where(part_of(me, k, lane), zy[:, k * 128 : (k + 1) * 128], part)
        zk = zx[:, k * 128 : (k + 1) * 128]
        extra = jnp.where(row == k, high(zk), extra)
        extra = jnp.where(row == k + 3, zk - high(zk), extra)
    extra = jnp.where(row == 6, high(part), extra)
    extra = jnp.where(row == 7, part - high(part), extra)
    for d in range(GROUP):
        h = d % 2
        pay_ref[d] = jnp.concatenate([x[d // 2, :, h * 128 : (h + 1) * 128], extra], axis=0).astype(BF16)


def local_kernel(scales_ref, own_ref, obs_ref, aux_ref):
    w = tile_weights((ROWS, 128))
    total = jnp.zeros((ROWS, 128), F32)
    for c in range(C):
        d = own_ref[0, c].astype(F32) - obs_ref[c].astype(F32)
        d = d * d
        total = total + (d[:, :128] + d[:, 128:]) * inverse_square(scales_ref, c)
    total = total * w
    aux_ref[0:8] = (total[0:8] + total[8:16] + total[16:24]) * np.float32(1.0 / (C * LON * SUMW))
    flat = iota((8, 128), 0) * 128 + iota((8, 128), 1)
    channel = lax.shift_right_logical(flat * 2731, 16)
    weight = row_weight(lat_index() * ROWS + flat - channel * ROWS)
    inv = jnp.zeros((8, 128), F32)
    for c in range(C):
        inv = jnp.where(channel == c, inverse_square(scales_ref, c), inv)
    aux_ref[8:16] = weight * inv * np.float32(1.0 / (C * SUMW * GROUP))


def distance_kernel(scales_ref, recv_ref, aux_ref, msg_ref, zall_ref, rows_ref):
    me = lax.axis_index("y")
    inv = inverse_square(scales_ref, me * 2 + lax.axis_index("xl"))
    w = tile_weights((ROWS, 128)) * (inv * np.float32(1.0 / (C * LON * SUMW)))
    row, lane = iota((8, 128), 0), iota((8, 128), 1)
    got = [recv_ref[s].astype(F32) for s in range(GROUP)]
    rows_ref[...] = jnp.zeros((128, 128), F32)
    pairs = [(k, m, (m - k) % M) for k in (1, 2, 3, 4) for m in range(M) if k < 4 or m < 4]

    def put(at, value):
        rows_ref[at : at + 1] = jnp.sum(value, axis=0, keepdims=True)

    totals = [jnp.zeros((8, 128), F32) for _ in pairs]
    for t in range(3):
        rows8 = slice(t * 8, t * 8 + 8)
        for p, (_, m, n) in enumerate(pairs):
            acc = None
            for l in range(4):
                d = got[m * 4 + l][rows8] - got[n * 4 + l][rows8]
                acc = d * d if acc is None else acc + d * d
            totals[p] = totals[p] + acc * w[rows8]
    for p, (k, m, _) in enumerate(pairs):
        put((k - 1) * 8 + m, totals[p])
    rows_ref[32:40] = jnp.where(row == me, jnp.sum(aux_ref[0:8], axis=0, keepdims=True), 0.0)

    zw = aux_ref[8:16]
    real = row < 3
    zobs = jnp.zeros((8, 128), F32)
    zonal = []
    for m in range(M):
        s = sum(got[m * 4 + l][24:32] for l in range(4))
        z = jnp.where(real, s + jnp.concatenate([s[3:8], s[0:3]], axis=0), 0.0) * np.float32(1.0 / LON)
        zonal.append(z)
        zall_ref[m] = z
        part = s[6:7] + s[7:8]
        zobs = jnp.where(real & part_of(m, row, lane), part, zobs)
    zobs = zobs * np.float32(1.0 / LON)
    zall_ref[M] = zobs
    for k, m, n in pairs:
        d = zonal[m] - zonal[n]
        put(40 + (k - 1) * 8 + m, zw * d * d)
    for m in range(M):
        d = zonal[m] - zobs
        put(72 + m, zw * d * d)
    ones = jnp.ones((8, 128), F32)
    sums = lax.dot_general(
        ones, rows_ref[...], (((1,), (1,)), ((), ())), precision=HIGHEST, preferred_element_type=F32
    )
    for i in range(msg_ref.shape[0]):
        msg_ref[i] = sums[0:1]


def relay_kernel(in_ref, out_ref):
    total = jnp.sum(in_ref[...], axis=0)
    out_ref[...] = jnp.broadcast_to(total[None], out_ref.shape)


def mix_kernel(scales_ref, msg_ref, zall_ref, gat_ref, obs_ref, out_ref, coef_ref, zcol_ref):
    me = lax.axis_index("y")
    step = pl.program_id(0)
    per = out_ref.shape[1]

    @pl.when(step == 0)
    def _():
        dist = jnp.sum(msg_ref[...], axis=0)
        row, lane = iota((16, 128), 0), iota((16, 128), 1)
        j = row & 7
        k = j + 1
        at = jnp.where(
            k <= 3,
            j * 8 + ((me + k) & 7),
            jnp.where(k == 4, 24 + (me & 3), jnp.where(k <= 7, (7 - k) * 8 + me, 32 + me)),
        )
        at = at + jnp.where(row >= 8, 40, 0)
        e = jnp.broadcast_to(jnp.exp(dist * np.float32(-0.5 / BAND)), (16, 128))
        picked = jnp.sum(jnp.where(lane == at, e, 0.0), axis=1, keepdims=True)
        norm = jnp.where(row == 7, 1.0 / (M * BAND), jnp.where(row == 15, 1.0 / (M * BAND), 1.0 / (M * (M - 1) * BAND)))
        coef = jnp.broadcast_to(picked, (16, 128)) * norm
        coef_ref[...] = coef
        zme = zall_ref[me]
        z = coef[15:16] * (zme - zall_ref[M])
        for k in range(1, M):
            z = z + coef[7 + k : 8 + k] * (zall_ref[(me + k) & 7] - zme)
        for b in range(3):
            zcol_ref[b * 128 : (b + 1) * 128] = jnp.broadcast_to(z[b : b + 1], (128, 128)).T

    fac = tile_weights((ROWS, COLS)) * np.float32(LAT / SUMW)
    coef = coef_ref[...]
    own_b = coef[7:8]
    for i in range(per):
        c = step * per + i
        xm = gat_ref[me, i].astype(F32)
        acc = jnp.concatenate([own_b, own_b], axis=1) * (xm - obs_ref[i].astype(F32))
        for k in range(1, M):
            a = coef[k - 1 : k]
            acc = acc + jnp.concatenate([a, a], axis=1) * (gat_ref[(me + k) & 7, i].astype(F32) - xm)
        z = zcol_ref[pl.ds(pl.multiple_of(c * ROWS, 8), ROWS)]
        acc = acc + jnp.concatenate([z, z], axis=1)
        out_ref[0, i] = acc * (fac * inverse_square(scales_ref, c))


VMEM = pl.BlockSpec(memory_space=pltpu.VMEM)
SMEM = pl.BlockSpec(memory_space=pltpu.SMEM)


def call(kernel, out_shape, in_specs, cost, **kw):
    return pl.pallas_call(
        kernel,
        out_shape=out_shape,
        in_specs=in_specs,
        cost_estimate=pl.CostEstimate(flops=cost, bytes_accessed=cost, transcendentals=0),
        compiler_params=pltpu.CompilerParams(vmem_limit_bytes=32 * 1024 * 1024),
        **kw,
    )


def per_device(members, observed, scales):
    shape = jax.ShapeDtypeStruct
    gathered = lax.all_gather(members, "y", axis=0, tiled=True)
    pay = call(pack_kernel, shape((GROUP, 32, 128), BF16), [VMEM] * 2, 1 << 20, out_specs=VMEM)(members, observed)
    aux = call(local_kernel, shape((16, 128), F32), [SMEM, VMEM, VMEM], 1 << 20, out_specs=VMEM)(
        scales, members, observed
    )
    recv = lax.all_to_all(pay, ("y", "xl", "core"), 0, 0, tiled=True)
    msg, zall = call(
        distance_kernel,
        (shape((16, 1, 128), F32), shape((16, 8, 128), F32)),
        [SMEM, VMEM, VMEM],
        1 << 20,
        out_specs=(VMEM, VMEM),
        scratch_shapes=[pltpu.VMEM((128, 128), F32)],
    )(scales, recv, aux)
    msg = lax.all_to_all(msg, ("xh", "xl", "core"), 0, 0, tiled=True)
    msg = call(relay_kernel, shape((64, 1, 128), F32), [VMEM], 1 << 16, out_specs=VMEM)(msg)
    msg = lax.all_to_all(msg, ("y", "z"), 0, 0, tiled=True)
    steps = 4
    per = C // steps
    return call(
        mix_kernel,
        shape((1, C, ROWS, COLS), F32),
        [
            SMEM,
            pl.BlockSpec((64, 1, 128), lambda i: (0, 0, 0)),
            pl.BlockSpec((16, 8, 128), lambda i: (0, 0, 0)),
            pl.BlockSpec((M, per, ROWS, COLS), lambda i: (0, i, 0, 0)),
            pl.BlockSpec((per, ROWS, COLS), lambda i: (i, 0, 0)),
        ],
        1 << 22,
        grid=(steps,),
        out_specs=pl.BlockSpec((1, per, ROWS, COLS), lambda i: (0, i, 0, 0)),
        scratch_shapes=[pltpu.VMEM((16, 128), F32), pltpu.VMEM((CELLS, 128), F32)],
    )(scales, msg, zall, gathered, observed)


def solution(mesh):
    fine = Mesh(mesh.devices.reshape(8, 8, 4, 2, 2), ("y", "z", "xh", "xl", "core"))
    placed = P("y", None, ("z", "xh"), ("xl", "core"))
    return jax.shard_map(
        per_device,
        mesh=fine,
        in_specs=(placed, P(None, ("z", "xh"), ("xl", "core")), P()),
        out_specs=placed,
        check_vma=False,
    )
```

time: 333 us -> 86.2 us (0.26)
  blocking collectives: 296 us -> 34.8 us
  starting transfers between devices: 0.01 us -> 17.7 us
  other arithmetic: 10.7 us -> 0 us
  local copies, waits for them, and re-layouts: 0.02 us -> 5.77 us
  Pallas kernels: 0 us -> 5.56 us
  between operations: 18.1 us -> 13.4 us
    psum x2 -> x0, blocking collectives: 276 us -> none  [the longest x1 254 us: per_device(): lax.psum((field_part, obs_part, zonal_part, zobs_part), ('lat', 'lon'))]
    all_to_all x0 -> x2, blocking collectives: none -> 34.8 us  [the longest x1 23.6 us: per_device(): msg = lax.all_to_all(msg, ('y', 'z'), 0, 0, tiled=True)]
    all_gather x1 -> x0, blocking collectives: 19.7 us -> none  [per_device(): zonal_all = lax.all_gather(zonal[None], 'member', axis=0, tiled=True)]
    all_to_all x0 -> x1, starting transfers between devices: none -> 17.7 us  [per_device(): recv = lax.all_to_all(pay, ('y', 'xl', 'core'), 0, 0, tiled=True)]
    reduce_sum x7 -> x0, other arithmetic: 7.91 us -> none  [the longest x1 2.18 us: per_device(): jnp.sum(field_wgt[None] * (own[None] - gathered.astype(jnp.float32)) ** 2...]
    all_to_all x0 -> x1, waiting for transfers between devices: none -> 7.85 us  [per_device(): recv = lax.all_to_all(pay, ('y', 'xl', 'core'), 0, 0, tiled=True)]
    unnamed x6 -> x16, local copies, waits for them, and re-layouts: 0.02 us -> 5.77 us
    all_gather x1, waiting for transfers between devices: 5.67 us -> 0.01 us  [per_device(): gathered = lax.all_gather(members, 'y', axis=0, tiled=True)]
  transfers between devices with their start and end apart: 1 -> 2, of which waited for: 1 -> 1; matrix products, arithmetic and copies ran while one was open for 2% -> 0% of each run, Pallas kernels for 0% -> 3%
where the time goes in v1:
time: 86.2 us; the launch traced here: 85.8 us
  blocking collectives  34.8 us (40%)
  starting transfers between devices  17.7 us (21%)
  between operations  13.4 us (16%)
  waiting for transfers between devices  8.56 us (10%)
  local copies, waits for them, and re-layouts  5.77 us (7%)
  Pallas kernels  5.56 us (6%)
    all_to_all x1, blocking collectives, per_device(): msg = lax.all_to_all(msg, ('y', 'z'), 0, 0, tiled=True)  23.6 us
    all_to_all x1, starting transfers between devices, per_device(): recv = lax.all_to_all(pay, ('y', 'xl', 'core'), 0, 0, tiled=True)  17.7 us
    all_to_all x1, blocking collectives, per_device(): msg = lax.all_to_all(msg, ('xh', 'xl', 'core'), 0, 0, tiled=True)  11.2 us
    all_to_all x1, waiting for transfers between devices, per_device(): recv = lax.all_to_all(pay, ('y', 'xl', 'core'), 0, 0, tiled=True)  7.85 us
    unnamed x16, local copies, waits for them, and re-layouts  5.77 us
    pallas_call x1, Pallas kernels, per_device(): call(mix_kernel, shape((1, C, ROWS, COLS), F32), [SMEM, pl.BlockSpec((64,...  2.84 us
  transfers between devices with their start and end apart: 2, of which 1 were waited for; matrix products, arithmetic and copies ran while one was open for 0% of the time, Pallas kernels for 3%

profile of v1, /device:TPU:1, one launch (start us, length us, event | category | flops | bytes accessed | tf_op | source)
XLA Modules:
  0.0 85.8 jit_solution(13664750732612138822)
XLA Ops:
  6.5 0.0 copy-start.2
  6.5 0.0 all-gather.2.cloned.1.call-start
  6.5 0.7 all-gather.2.cloned.1.call-update
  7.3 0.0 copy-start
  7.3 0.9 %copy-done = bf16[16,24,256]{2,1,0:T(8,128)(2,1)S(1)} copy-done((bf16[16,24,256]{2,1,0:T(8,128)(2,1)S(1)}, bf16[16,24,256]{2,1,0:T(8,128)(2,1)}, u32[]{:S(2)}) %copy-start) | copy-done | bytes 196632
  8.2 0.0 copy-start.3
  8.2 0.9 %copy-done.3 = bf16[1,16,24,256]{3,2,1,0:T(8,128)(2,1)S(1)} copy-done((bf16[1,16,24,256]{3,2,1,0:T(8,128)(2,1)S(1)}, bf16[1,16,24,256]{3,2,1,0:T(8,128)(2,1)}, u32[]{:S(2)}) %copy-start.3) | copy-done | bytes 196632
  9.1 0.0 copy-start.7
  9.1 0.9 %shard_map.37 = bf16[32,32,128]{2,1,0:T(8,128)(2,1)} custom-call(bf16[1,16,24,256]{3,2,1,0:T(8,128)(2,1)S(1)} %copy-done.3, bf16[16,24,256]{2,1,0:T(8,128)(2,1)S(1)} %copy-done), custom_call_target="tpu_custom_call" | custom-call | flops 1048576 | bytes 1048576 | tf_op jit(solution)/shard_map/pallas_call | solution.py:227
  10.1 17.7 %all-to-all-start = ((bf16[32,32,128]{2,1,0:T(8,128)(2,1)}), bf16[32,32,128]{2,1,0:T(8,128)(2,1)S(1)}, u32[]{:S(2)}, u32[]{:S(2)}) async-start(bf16[32,32,128]{2,1,0:T(8,128)(2,1)} %shard_map.37), calls=%async_computation | async-start | bytes 524288 | tf_op jit(solution)/shard_map/all_to_all | solution.py:231
  27.7 0.0 copy-start.1
  27.7 0.9 %copy-done.1 = bf16[16,24,256]{2,1,0:T(8,128)(2,1)S(1)} copy-done((bf16[16,24,256]{2,1,0:T(8,128)(2,1)S(1)}, bf16[16,24,256]{2,1,0:T(8,128)(2,1)}, u32[]{:S(2)}) %copy-start.1) | copy-done | bytes 196632
  28.7 0.0 copy-start.4
  28.7 0.9 %copy-done.4 = bf16[1,16,24,256]{3,2,1,0:T(8,128)(2,1)S(1)} copy-done((bf16[1,16,24,256]{3,2,1,0:T(8,128)(2,1)S(1)}, bf16[1,16,24,256]{3,2,1,0:T(8,128)(2,1)}, u32[]{:S(2)}) %copy-start.4) | copy-done | bytes 196632
  29.6 0.7 copy-done.6
  30.2 0.7 shard_map.38.aux_ref
  31.0 7.8 %all-to-all-done.recv_ref = bf16[32,32,128]{2,1,0:T(8,128)(2,1)S(1)} async-done(((bf16[32,32,128]{2,1,0:T(8,128)(2,1)}), bf16[32,32,128]{2,1,0:T(8,128)(2,1)S(1)}, u32[]{:S(2)}, u32[]{:S(2)}) %all-to-all-start) | async-done | bytes 262176 | tf_op jit(solution)/shard_map/all_to_all | solution.py:231
  38.8 0.0 copy-done.7
  38.8 1.0 %shard_map.39 = (f32[16,1,128]{2,1,0:T(1,128)S(1)}, f32[16,8,128]{2,1,0:T(8,128)S(1)}) custom-call(f32[16]{0:T(128)S(1)} %copy-done.7, bf16[32,32,128]{2,1,0:T(8,128)(2,1)S(1)} %all-to-all-done.recv_ref, f32[16,128]{1,0:T(8,128)S(1)} %shard_map.38.aux_ref), custom_call_target="tpu_custom_call" | custom-call | flops 1048576 | bytes 1048576 | tf_op jit(solution)/shard_map/pallas_call | solution.py:232
  39.9 11.2 %all_to_all.15.in_ref = f32[16,1,128]{2,1,0:T(1,128)S(1)} all-to-all(f32[16,1,128]{2,1,0:T(1,128)S(1)} %get-tuple-element.7), channel_id=1, replica_groups=mesh['y'=8,'z'=8,'xh'=4,'xl'=2,'core'=2] {'xh','xl','core'}, dimensions={0} | all-to-all | bytes 16384 | tf_op jit(solution)/shard_map/all_to_all | solution.py:240
  51.1 23.6 %all_to_all.16.msg_ref = f32[64,1,128]{2,1,0:T(1,128)S(1)} all-to-all(f32[64,1,128]{2,1,0:T(1,128)S(1)} %shard_map.40), channel_id=1, replica_groups=mesh['y'=8,'z'=8,'xh'=4,'xl'=2,'core'=2] {'y','z'}, dimensions={0} | all-to-all | bytes 65536 | tf_op jit(solution)/shard_map/all_to_all | solution.py:242
  74.7 0.0 copy-done.2
  74.7 1.4 %copy-done.5 = bf16[8,16,24,256]{3,2,1,0:T(8,128)(2,1)S(1)} copy-done((bf16[8,16,24,256]{3,2,1,0:T(8,128)(2,1)S(1)}, bf16[8,16,24,256]{3,2,1,0:T(8,128)(2,1)}, u32[]{:S(2)}) %copy-start.5) | copy-done | bytes 1572888
  76.1 2.8 %shard_map.41 = f32[1,16,24,256]{3,2,1,0:T(8,128)} custom-call(f32[16]{0:T(128)S(1)} %copy-done.7, f32[64,1,128]{2,1,0:T(1,128)S(1)} %all_to_all.16.msg_ref, f32[16,8,128]{2,1,0:T(8,128)S(1)} %get-tuple-element.8.zall_ref, bf16[8,16,24,256]{3,2,1,0:T(8,128)(2,1)S(1)} %copy-done.5, bf16[16,24,256]{2,1,0:T(8,128)(2,1)S(1)} %copy-done.2), custom_call_target="tpu_custom_call" | custom-call | flops 4194304 | bytes 4194304 | tf_op jit(solution)/shard_map/pallas_call | solution.py:245
  (4 shorter events, 0.0 us)
Async XLA Ops:
  6.5 68.2 %copy-start.2 = (bf16[16,24,256]{2,1,0:T(8,128)(2,1)S(1)}, bf16[16,24,256]{2,1,0:T(8,128)(2,1)}, u32[]{:S(2)}) copy-start(bf16[16,24,256]{2,1,0:T(8,128)(2,1)} %obs_ref.5) | copy-start | bytes 589828
  6.5 68.2 %all-gather.2.cloned.1.call-start = ((), (), s32[]{:S(2)}) async-start(), calls=%async_computation.3 | async-start | bytes 1769472 | tf_op jit(solution)/shard_map/all_gather | solution.py:226
  7.3 0.9 %copy-start = (bf16[16,24,256]{2,1,0:T(8,128)(2,1)S(1)}, bf16[16,24,256]{2,1,0:T(8,128)(2,1)}, u32[]{:S(2)}) copy-start(bf16[16,24,256]{2,1,0:T(8,128)(2,1)} %obs_ref.5) | copy-start | bytes 589828
  8.2 0.9 %copy-start.3 = (bf16[1,16,24,256]{3,2,1,0:T(8,128)(2,1)S(1)}, bf16[1,16,24,256]{3,2,1,0:T(8,128)(2,1)}, u32[]{:S(2)}) copy-start(bf16[1,16,24,256]{3,2,1,0:T(8,128)(2,1)} %own_ref.3) | copy-start | bytes 589828
  9.1 29.7 %copy-start.7 = (f32[16]{0:T(128)S(1)}, f32[16]{0:T(128)}, u32[]{:S(2)}) copy-start(f32[16]{0:T(128)} %scales_ref.5) | copy-start | bytes 196
  10.1 28.8 %all-to-all-start = ((bf16[32,32,128]{2,1,0:T(8,128)(2,1)}), bf16[32,32,128]{2,1,0:T(8,128)(2,1)S(1)}, u32[]{:S(2)}, u32[]{:S(2)}) async-start(bf16[32,32,128]{2,1,0:T(8,128)(2,1)} %shard_map.37), calls=%async_computation | async-start | bytes 524288 | tf_op jit(solution)/shard_map/all_to_all | solution.py:231
  27.7 0.9 %copy-start.1 = (bf16[16,24,256]{2,1,0:T(8,128)(2,1)S(1)}, bf16[16,24,256]{2,1,0:T(8,128)(2,1)}, u32[]{:S(2)}) copy-start(bf16[16,24,256]{2,1,0:T(8,128)(2,1)} %obs_ref.5) | copy-start | bytes 589828
  28.7 0.9 %copy-start.4 = (bf16[1,16,24,256]{3,2,1,0:T(8,128)(2,1)S(1)}, bf16[1,16,24,256]{3,2,1,0:T(8,128)(2,1)}, u32[]{:S(2)}) copy-start(bf16[1,16,24,256]{3,2,1,0:T(8,128)(2,1)} %own_ref.3) | copy-start | bytes 589828
  29.6 0.7 copy-start.6
  74.7 1.4 %copy-start.5 = (bf16[8,16,24,256]{3,2,1,0:T(8,128)(2,1)S(1)}, bf16[8,16,24,256]{3,2,1,0:T(8,128)(2,1)}, u32[]{:S(2)}) copy-start(bf16[8,16,24,256]{3,2,1,0:T(8,128)(2,1)} %all-gather.2.cloned.1.call-done.gat_ref) | copy-start | bytes 4718596
Sparse Core Ops, SparseCore 0:
  10.0 53.2 all-gather.1

commit v2 on v1

--- a/solution.py
+++ b/solution.py
@@ -15,7 +15,9 @@
 C, M, LAT, LON = 16, 8, 768, 1024
 ROWS, COLS = 24, 256
 CELLS = C * ROWS
+PARTS = 8
 GROUP = 32
+LONG = 1 << 36
 HIGHEST = lax.Precision.HIGHEST
 
 
@@ -63,10 +65,16 @@
     return (flat >= part * (CELLS // M)) & (flat < (part + 1) * (CELLS // M))
 
 
-def pack_kernel(own_ref, obs_ref, pay_ref):
+def pack_kernel(own_hbm, obs_hbm, pay_ref, own_ref, obs_ref, sems):
     me = lax.axis_index("y")
+    get_own = pltpu.make_async_copy(own_hbm, own_ref, sems.at[0])
+    get_obs = pltpu.make_async_copy(obs_hbm, obs_ref, sems.at[1])
+    get_own.start()
+    get_obs.start()
+    get_own.wait()
     x = own_ref[0].astype(F32)
     zx = lanes_sum(x)
+    get_obs.wait()
     zy = lanes_sum(obs_ref[...].astype(F32))
     row, lane = iota((8, 128), 0), iota((8, 128), 1)
 
@@ -87,7 +95,8 @@
         pay_ref[d] = jnp.concatenate([x[d // 2, :, h * 128 : (h + 1) * 128], extra], axis=0).astype(BF16)
 
 
-def local_kernel(scales_ref, own_ref, obs_ref, aux_ref):
+def local_kernel(scales_ref, own_ref, obs_ref, pay_ref, aux_ref, copy_ref):
+    copy_ref[...] = own_ref[0]
     w = tile_weights((ROWS, 128))
     total = jnp.zeros((ROWS, 128), F32)
     for c in range(C):
@@ -162,101 +171,143 @@
     out_ref[...] = jnp.broadcast_to(total[None], out_ref.shape)
 
 
-def mix_kernel(scales_ref, msg_ref, zall_ref, gat_ref, obs_ref, out_ref, coef_ref, zcol_ref):
+def after_kernel(*refs):
+    pass
+
+
+def coefficient_kernel(msg_ref, zall_ref, coef_ref, zcol_ref):
     me = lax.axis_index("y")
-    step = pl.program_id(0)
-    per = out_ref.shape[1]
-
-    @pl.when(step == 0)
-    def _():
-        dist = jnp.sum(msg_ref[...], axis=0)
-        row, lane = iota((16, 128), 0), iota((16, 128), 1)
-        j = row & 7
-        k = j + 1
-        at = jnp.where(
-            k <= 3,
-            j * 8 + ((me + k) & 7),
-            jnp.where(k == 4, 24 + (me & 3), jnp.where(k <= 7, (7 - k) * 8 + me, 32 + me)),
-        )
-        at = at + jnp.where(row >= 8, 40, 0)
-        e = jnp.broadcast_to(jnp.exp(dist * np.float32(-0.5 / BAND)), (16, 128))
-        picked = jnp.sum(jnp.where(lane == at, e, 0.0), axis=1, keepdims=True)
-        norm = jnp.where(row == 7, 1.0 / (M * BAND), jnp.where(row == 15, 1.0 / (M * BAND), 1.0 / (M * (M - 1) * BAND)))
-        coef = jnp.broadcast_to(picked, (16, 128)) * norm
-        coef_ref[...] = coef
-        zme = zall_ref[me]
-        z = coef[15:16] * (zme - zall_ref[M])
-        for k in range(1, M):
-            z = z + coef[7 + k : 8 + k] * (zall_ref[(me + k) & 7] - zme)
-        for b in range(3):
-            zcol_ref[b * 128 : (b + 1) * 128] = jnp.broadcast_to(z[b : b + 1], (128, 128)).T
-
+    dist = jnp.sum(msg_ref[...], axis=0)
+    row, lane = iota((16, 128), 0), iota((16, 128), 1)
+    j = row & 7
+    k = j + 1
+    at = jnp.where(
+        k <= 3,
+        j * 8 + ((me + k) & 7),
+        jnp.where(k == 4, 24 + (me & 3), jnp.where(k <= 7, (7 - k) * 8 + me, 32 + me)),
+    )
+    at = at + jnp.where(row >= 8, 40, 0)
+    e = jnp.broadcast_to(jnp.exp(dist * np.float32(-0.5 / BAND)), (16, 128))
+    picked = jnp.sum(jnp.where(lane == at, e, 0.0), axis=1, keepdims=True)
+    norm = jnp.where(j == 7, 1.0 / (M * BAND), 1.0 / (M * (M - 1) * BAND))
+    coef = jnp.broadcast_to(picked, (16, 128)) * norm
+    coef_ref[...] = coef
+    zme = zall_ref[me]
+    z = coef[15:16] * (zme - zall_ref[M])
+    for k in range(1, M):
+        z = z + coef[7 + k : 8 + k] * (zall_ref[(me + k) & 7] - zme)
+    for b in range(3):
+        zcol_ref[b * 128 : (b + 1) * 128] = jnp.broadcast_to(z[b : b + 1], (128, 128)).T
+
+
+def mix_kernel(scales_ref, coef_ref, zcol_ref, obs_ref, *refs):
+    tiles, (out_hbm, out_ref, sems) = refs[:M], refs[M:]
     fac = tile_weights((ROWS, COLS)) * np.float32(LAT / SUMW)
     coef = coef_ref[...]
-    own_b = coef[7:8]
-    for i in range(per):
-        c = step * per + i
-        xm = gat_ref[me, i].astype(F32)
-        acc = jnp.concatenate([own_b, own_b], axis=1) * (xm - obs_ref[i].astype(F32))
+    coef = jnp.concatenate([coef, coef], axis=1)
+    per = C // PARTS
+    copies = []
+    for c in range(C):
+        xm = tiles[0][c].astype(F32)
+        acc = coef[7:8] * (xm - obs_ref[c].astype(F32))
         for k in range(1, M):
-            a = coef[k - 1 : k]
-            acc = acc + jnp.concatenate([a, a], axis=1) * (gat_ref[(me + k) & 7, i].astype(F32) - xm)
-        z = zcol_ref[pl.ds(pl.multiple_of(c * ROWS, 8), ROWS)]
+            acc = acc + coef[k - 1 : k] * (tiles[k][c].astype(F32) - xm)
+        z = zcol_ref[c * ROWS : (c + 1) * ROWS]
         acc = acc + jnp.concatenate([z, z], axis=1)
-        out_ref[0, i] = acc * (fac * inverse_square(scales_ref, c))
+        out_ref[c] = acc * (fac * inverse_square(scales_ref, c))
+        if c % per == per - 1:
+            part = pl.ds(c + 1 - per, per)
+            copies.append(pltpu.make_async_copy(out_ref.at[part], out_hbm.at[0, part], sems.at[c // per]))
+            copies[-1].start()
+    for copy in copies:
+        copy.wait()
 
 
 VMEM = pl.BlockSpec(memory_space=pltpu.VMEM)
 SMEM = pl.BlockSpec(memory_space=pltpu.SMEM)
 
 
-def call(kernel, out_shape, in_specs, cost, **kw):
+def call(kernel, out_shape, in_specs, cost, vmem=32, **kw):
     return pl.pallas_call(
         kernel,
         out_shape=out_shape,
         in_specs=in_specs,
         cost_estimate=pl.CostEstimate(flops=cost, bytes_accessed=cost, transcendentals=0),
-        compiler_params=pltpu.CompilerParams(vmem_limit_bytes=32 * 1024 * 1024),
+        compiler_params=pltpu.CompilerParams(vmem_limit_bytes=vmem * 1024 * 1024),
         **kw,
     )
+
+
+def after(arrays, made):
+    spec = pl.BlockSpec(memory_space=pl.ANY)
+    return call(
+        after_kernel,
+        [jax.ShapeDtypeStruct(a.shape, a.dtype) for a in arrays],
+        [spec] * (len(arrays) + 1),
+        1 << 22,
+        out_specs=[spec] * len(arrays),
+        input_output_aliases={i: i for i in range(len(arrays))},
+    )(*arrays, made)
+
+
+def from_ahead(tile, k):
+    return lax.ppermute(tile, "y", [((i + k) % M, i) for i in range(M)])
 
 
 def per_device(members, observed, scales):
     shape = jax.ShapeDtypeStruct
-    gathered = lax.all_gather(members, "y", axis=0, tiled=True)
-    pay = call(pack_kernel, shape((GROUP, 32, 128), BF16), [VMEM] * 2, 1 << 20, out_specs=VMEM)(members, observed)
-    aux = call(local_kernel, shape((16, 128), F32), [SMEM, VMEM, VMEM], 1 << 20, out_specs=VMEM)(
-        scales, members, observed
-    )
+    tile = shape((C, ROWS, COLS), BF16)
+    anywhere = pl.BlockSpec(memory_space=pl.ANY)
+    hbm = pl.BlockSpec(memory_space=pltpu.HBM)
+    pay = call(
+        pack_kernel,
+        shape((GROUP, 32, 128), BF16),
+        [hbm] * 2,
+        1 << 20,
+        vmem=60,
+        out_specs=VMEM,
+        scratch_shapes=[
+            pltpu.VMEM((1, C, ROWS, COLS), BF16),
+            pltpu.VMEM((C, ROWS, COLS), BF16),
+            pltpu.SemaphoreType.DMA((2,)),
+        ],
+    )(members, observed)
+    aux, own = call(
+        local_kernel, (shape((16, 128), F32), tile), [SMEM, VMEM, VMEM, anywhere], 1 << 20, out_specs=(VMEM, VMEM)
+    )(scales, members, observed, pay)
+    tiles = [own] + [None] * 7
     recv = lax.all_to_all(pay, ("y", "xl", "core"), 0, 0, tiled=True)
+    tiles[1], tiles[7] = from_ahead(own, 1), from_ahead(own, -1)
     msg, zall = call(
         distance_kernel,
         (shape((16, 1, 128), F32), shape((16, 8, 128), F32)),
         [SMEM, VMEM, VMEM],
-        1 << 20,
+        LONG,
         out_specs=(VMEM, VMEM),
         scratch_shapes=[pltpu.VMEM((128, 128), F32)],
     )(scales, recv, aux)
+    tiles[1], tiles[7] = after([tiles[1], tiles[7]], msg)
     msg = lax.all_to_all(msg, ("xh", "xl", "core"), 0, 0, tiled=True)
-    msg = call(relay_kernel, shape((64, 1, 128), F32), [VMEM], 1 << 16, out_specs=VMEM)(msg)
+    tiles[2], tiles[6] = from_ahead(tiles[1], 1), from_ahead(tiles[7], -1)
+    msg = call(relay_kernel, shape((64, 1, 128), F32), [VMEM], LONG, out_specs=VMEM)(msg)
+    tiles[2], tiles[6] = after([tiles[2], tiles[6]], msg)
     msg = lax.all_to_all(msg, ("y", "z"), 0, 0, tiled=True)
-    steps = 4
-    per = C // steps
+    tiles[3], tiles[5], tiles[4] = from_ahead(tiles[2], 1), from_ahead(tiles[6], -1), from_ahead(tiles[2], 2)
+    coef, zcol = call(
+        coefficient_kernel,
+        (shape((16, 128), F32), shape((CELLS, 128), F32)),
+        [VMEM] * 2,
+        LONG,
+        out_specs=(VMEM, VMEM),
+    )(msg, zall)
     return call(
         mix_kernel,
         shape((1, C, ROWS, COLS), F32),
-        [
-            SMEM,
-            pl.BlockSpec((64, 1, 128), lambda i: (0, 0, 0)),
-            pl.BlockSpec((16, 8, 128), lambda i: (0, 0, 0)),
-            pl.BlockSpec((M, per, ROWS, COLS), lambda i: (0, i, 0, 0)),
-            pl.BlockSpec((per, ROWS, COLS), lambda i: (i, 0, 0)),
-        ],
+        [SMEM] + [VMEM] * (3 + M),
         1 << 22,
-        grid=(steps,),
-        out_specs=pl.BlockSpec((1, per, ROWS, COLS), lambda i: (0, i, 0, 0)),
-        scratch_shapes=[pltpu.VMEM((16, 128), F32), pltpu.VMEM((CELLS, 128), F32)],
-    )(scales, msg, zall, gathered, observed)
+        out_specs=hbm,
+        scratch_shapes=[pltpu.VMEM((C, ROWS, COLS), F32), pltpu.SemaphoreType.DMA((PARTS,))],
+    )(scales, coef, zcol, observed, *tiles)
 
 
 def solution(mesh):

time: 86.2 us -> 78.8 us (0.914)
  starting transfers between devices: 17.7 us -> 58.1 us
  blocking collectives: 34.8 us -> 0 us
  between operations: 13.4 us -> 0.19 us
  local copies, waits for them, and re-layouts: 5.77 us -> 0.02 us
  waiting for transfers between devices: 8.56 us -> 12.7 us
  Pallas kernels: 5.56 us -> 7.25 us
    all_to_all x2 -> x0, blocking collectives: 34.8 us -> none  [the longest x1 23.6 us: per_device(): msg = lax.all_to_all(msg, ('y', 'z'), 0, 0, tiled=True)]
    ppermute x0 -> x7, starting transfers between devices: none -> 22.4 us  [from_ahead(): return lax.ppermute(tile, 'y', [((i + k) % M, i) for i in range(M)])]
    all_to_all x0 -> x2, starting transfers between devices: none -> 17.9 us  [the longest x1 12.7 us: per_device(): msg = lax.all_to_all(msg, ('y', 'z'), 0, 0, tiled=True)]
    ppermute x0 -> x7, waiting for transfers between devices: none -> 7.2 us  [from_ahead(): return lax.ppermute(tile, 'y', [((i + k) % M, i) for i in range(M)])]
    unnamed x16 -> x8, local copies, waits for them, and re-layouts: 5.77 us -> 0.02 us
    all_to_all x1, waiting for transfers between devices: 7.85 us -> 3.7 us  [per_device(): recv = lax.all_to_all(pay, ('y', 'xl', 'core'), 0, 0, tiled=True)]
    all_to_all x0 -> x2, waiting for transfers between devices: none -> 1.85 us  [the longest x1 1.66 us: per_device(): msg = lax.all_to_all(msg, ('xh', 'xl', 'core'), 0, 0, tiled=True)]
    pallas_call x4 -> x7, Pallas kernels: 4.53 us -> 5.58 us  [the longest x1 2.1 us: per_device(): call(pack_kernel, shape((GROUP, 32, 128), BF16), [hbm] * 2, 1 << 20, vmem...]
  transfers between devices with their start and end apart: 2 -> 10, of which waited for: 1 -> 5; matrix products, arithmetic and copies ran while one was open for 0% -> 0% of each run, Pallas kernels for 3% -> 4%
where the time goes in v2:
time: 78.8 us; the launch traced here: 78.3 us
  starting transfers between devices  58.1 us (74%)
  waiting for transfers between devices  12.7 us (16%)
  Pallas kernels  7.25 us (9%)
    ppermute x7, starting transfers between devices, from_ahead(): return lax.ppermute(tile, 'y', [((i + k) % M, i) for i in range(M)])  22.4 us
    all_to_all x1, starting transfers between devices, per_device(): recv = lax.all_to_all(pay, ('y', 'xl', 'core'), 0, 0, tiled=True)  17.8 us
    all_to_all x1, starting transfers between devices, per_device(): msg = lax.all_to_all(msg, ('y', 'z'), 0, 0, tiled=True)  12.7 us
    ppermute x7, waiting for transfers between devices, from_ahead(): return lax.ppermute(tile, 'y', [((i + k) % M, i) for i in range(M)])  7.2 us
    all_to_all x1, starting transfers between devices, per_device(): msg = lax.all_to_all(msg, ('xh', 'xl', 'core'), 0, 0, tiled=True)  5.21 us
    all_to_all x1, waiting for transfers between devices, per_device(): recv = lax.all_to_all(pay, ('y', 'xl', 'core'), 0, 0, tiled=True)  3.7 us
    pallas_call x1, Pallas kernels, per_device(): call(pack_kernel, shape((GROUP, 32, 128), BF16), [hbm] * 2, 1 << 20, vmem...  2.1 us
    pallas_call x1, Pallas kernels, per_device(): call(mix_kernel, shape((1, C, ROWS, COLS), F32), [SMEM] + [VMEM] * (3 + M...  1.82 us
  transfers between devices with their start and end apart: 10, of which 5 were waited for; matrix products, arithmetic and copies ran while one was open for 0% of the time, Pallas kernels for 4%

profile of v2, /device:TPU:1, one launch (start us, length us, event | category | flops | bytes accessed | tf_op | source)
XLA Modules:
  0.0 78.3 jit_solution(15803150369599603027)
XLA Ops:
  0.0 2.1 %shard_map.37.pay_ref = bf16[32,32,128]{2,1,0:T(8,128)(2,1)} custom-call(bf16[1,16,24,256]{3,2,1,0:T(8,128)(2,1)} %own_ref.1, bf16[16,24,256]{2,1,0:T(8,128)(2,1)} %obs_ref.3), custom_call_target="tpu_custom_call" | custom-call | flops 1048576 | bytes 1048576 | tf_op jit(solution)/shard_map/pallas_call | solution.py:262
  2.1 0.0 copy-start
  2.1 0.0 copy-start.1
  2.1 0.0 copy-start.3
  2.1 17.8 %all-to-all-start = ((bf16[32,32,128]{2,1,0:T(8,128)(2,1)}), bf16[32,32,128]{2,1,0:T(8,128)(2,1)S(1)}, u32[]{:S(2)}, u32[]{:S(2)}) async-start(bf16[32,32,128]{2,1,0:T(8,128)(2,1)} %shard_map.37.pay_ref), calls=%async_computation | async-start | bytes 524288 | tf_op jit(solution)/shard_map/all_to_all | solution.py:279
  20.0 0.7 shard_map.38
  20.7 3.3 %collective-permute-start.1 = (bf16[16,24,256]{2,1,0:T(8,128)(2,1)S(1)}, bf16[16,24,256]{2,1,0:T(8,128)(2,1)S(1)}, u32[]{:S(2)}, u32[]{:S(2)}) collective-permute-start(bf16[16,24,256]{2,1,0:T(8,128)(2,1)S(1)} %get-tuple-element.20.refs_0_), channel_id=1, source_target_pairs={{896,0},{0,128},{128,256},{256,384},{384,512},{512,640},{640,768},... | collective-permute-start | bytes 589832 | tf_op jit(solution)/shard_map/ppermute | solution.py:254
  24.1 3.3 %collective-permute-start = (bf16[16,24,256]{2,1,0:T(8,128)(2,1)S(1)}, bf16[16,24,256]{2,1,0:T(8,128)(2,1)S(1)}, u32[]{:S(2)}, u32[]{:S(2)}) collective-permute-start(bf16[16,24,256]{2,1,0:T(8,128)(2,1)S(1)} %get-tuple-element.20.refs_0_), channel_id=1, source_target_pairs={{128,0},{256,128},{384,256},{512,384},{640,512},{768,640},{896,768... | collective-permute-start | bytes 589832 | tf_op jit(solution)/shard_map/ppermute | solution.py:254
  27.4 3.7 %all-to-all-done.recv_ref = bf16[32,32,128]{2,1,0:T(8,128)(2,1)S(1)} async-done(((bf16[32,32,128]{2,1,0:T(8,128)(2,1)}), bf16[32,32,128]{2,1,0:T(8,128)(2,1)S(1)}, u32[]{:S(2)}, u32[]{:S(2)}) %all-to-all-start) | async-done | bytes 262176 | tf_op jit(solution)/shard_map/all_to_all | solution.py:279
  31.1 1.7 %shard_map.39 = (f32[16,1,128]{2,1,0:T(1,128)}, f32[16,8,128]{2,1,0:T(8,128)S(1)}) custom-call(f32[16]{0:T(128)S(1)} %copy-done.3, bf16[32,32,128]{2,1,0:T(8,128)(2,1)S(1)} %all-to-all-done.recv_ref, f32[16,128]{1,0:T(8,128)S(1)} %get-tuple-element.15.aux_ref), custom_call_target="tpu_custom_call" | custom-call | flops 68719476736 | bytes 68719476736 | tf_op jit(solution)/shard_map/pallas_call | solution.py:281
  32.7 5.2 %all-to-all-start.1 = ((f32[16,1,128]{2,1,0:T(1,128)}), f32[16,1,128]{2,1,0:T(1,128)S(1)}, u32[]{:S(2)}, u32[]{:S(2)}) async-start(f32[16,1,128]{2,1,0:T(1,128)} %get-tuple-element.16.refs_2_), calls=%async_computation.1 | async-start | bytes 16384 | tf_op jit(solution)/shard_map/all_to_all | solution.py:290
  38.0 1.9 %collective-permute-start.2 = (bf16[16,24,256]{2,1,0:T(8,128)(2,1)S(1)}, bf16[16,24,256]{2,1,0:T(8,128)(2,1)S(1)}, u32[]{:S(2)}, u32[]{:S(2)}) collective-permute-start(bf16[16,24,256]{2,1,0:T(8,128)(2,1)S(1)} %get-tuple-element.21.refs_1_), channel_id=1, source_target_pairs={{128,0},{256,128},{384,256},{512,384},{640,512},{768,640},{896,768... | collective-permute-start | bytes 589832 | tf_op jit(solution)/shard_map/ppermute | solution.py:254
  39.9 3.4 %collective-permute-start.3 = (bf16[16,24,256]{2,1,0:T(8,128)(2,1)S(1)}, bf16[16,24,256]{2,1,0:T(8,128)(2,1)S(1)}, u32[]{:S(2)}, u32[]{:S(2)}) collective-permute-start(bf16[16,24,256]{2,1,0:T(8,128)(2,1)S(1)} %get-tuple-element.22.refs_7_), channel_id=1, source_target_pairs={{896,0},{0,128},{128,256},{256,384},{384,512},{512,640},{640,768},... | collective-permute-start | bytes 589832 | tf_op jit(solution)/shard_map/ppermute | solution.py:254
  43.3 1.7 %all-to-all-done.1.in_ref = f32[16,1,128]{2,1,0:T(1,128)S(1)} async-done(((f32[16,1,128]{2,1,0:T(1,128)}), f32[16,1,128]{2,1,0:T(1,128)S(1)}, u32[]{:S(2)}, u32[]{:S(2)}) %all-to-all-start.1) | async-done | bytes 8224 | tf_op jit(solution)/shard_map/all_to_all | solution.py:290
  44.9 0.6 shard_map.40.refs_2_
  45.6 12.7 %all-to-all-start.2 = ((f32[64,1,128]{2,1,0:T(1,128)}), f32[64,1,128]{2,1,0:T(1,128)S(1)}, u32[]{:S(2)}, u32[]{:S(2)}) async-start(f32[64,1,128]{2,1,0:T(1,128)} %shard_map.40.refs_2_), calls=%async_computation.2 | async-start | bytes 65536 | tf_op jit(solution)/shard_map/all_to_all | solution.py:294
  58.3 5.2 %collective-permute-start.5 = (bf16[16,24,256]{2,1,0:T(8,128)(2,1)S(1)}, bf16[16,24,256]{2,1,0:T(8,128)(2,1)S(1)}, u32[]{:S(2)}, u32[]{:S(2)}) collective-permute-start(bf16[16,24,256]{2,1,0:T(8,128)(2,1)S(1)} %get-tuple-element.23.refs_2_), channel_id=1, source_target_pairs={{256,0},{384,128},{512,256},{640,384},{768,512},{896,640},{0,768},... | collective-permute-start | bytes 589832 | tf_op jit(solution)/shard_map/ppermute | solution.py:254
  63.5 3.0 %collective-permute-start.4 = (bf16[16,24,256]{2,1,0:T(8,128)(2,1)S(1)}, bf16[16,24,256]{2,1,0:T(8,128)(2,1)S(1)}, u32[]{:S(2)}, u32[]{:S(2)}) collective-permute-start(bf16[16,24,256]{2,1,0:T(8,128)(2,1)S(1)} %get-tuple-element.23.refs_2_), channel_id=1, source_target_pairs={{128,0},{256,128},{384,256},{512,384},{640,512},{768,640},{896,768... | collective-permute-start | bytes 589832 | tf_op jit(solution)/shard_map/ppermute | solution.py:254
  66.6 2.2 %collective-permute-start.6 = (bf16[16,24,256]{2,1,0:T(8,128)(2,1)S(1)}, bf16[16,24,256]{2,1,0:T(8,128)(2,1)S(1)}, u32[]{:S(2)}, u32[]{:S(2)}) collective-permute-start(bf16[16,24,256]{2,1,0:T(8,128)(2,1)S(1)} %get-tuple-element.24.refs_6_), channel_id=1, source_target_pairs={{896,0},{0,128},{128,256},{256,384},{384,512},{512,640},{640,768},... | collective-permute-start | bytes 589832 | tf_op jit(solution)/shard_map/ppermute | solution.py:254
  68.8 0.2 all-to-all-done.2.msg_ref
  69.0 0.3 shard_map.41
  69.3 4.9 %collective-permute-done.6.refs_5_ = bf16[16,24,256]{2,1,0:T(8,128)(2,1)S(1)} collective-permute-done((bf16[16,24,256]{2,1,0:T(8,128)(2,1)S(1)}, bf16[16,24,256]{2,1,0:T(8,128)(2,1)S(1)}, u32[]{:S(2)}, u32[]{:S(2)}) %collective-permute-start.6) | collective-permute-done | bytes 196640 | tf_op jit(solution)/shard_map/ppermute | solution.py:254
  74.2 2.3 %collective-permute-done.4.refs_3_ = bf16[16,24,256]{2,1,0:T(8,128)(2,1)S(1)} collective-permute-done((bf16[16,24,256]{2,1,0:T(8,128)(2,1)S(1)}, bf16[16,24,256]{2,1,0:T(8,128)(2,1)S(1)}, u32[]{:S(2)}, u32[]{:S(2)}) %collective-permute-start.4) | collective-permute-done | bytes 196640 | tf_op jit(solution)/shard_map/ppermute | solution.py:254
  76.5 1.8 %shard_map.44 = f32[1,16,24,256]{3,2,1,0:T(8,128)} custom-call(f32[16]{0:T(128)S(1)} %copy-done.3, f32[16,128]{1,0:T(8,128)S(1)} %get-tuple-element.18.coef_ref, f32[384,128]{1,0:T(8,128)S(1)} %get-tuple-element.19.zcol_ref, bf16[16,24,256]{2,1,0:T(8,128)(2,1)S(1)} %copy-done.1, bf16[16,24,256]{2,1,0:T(8,128)(2,1)S(1)} %get-tuple-element.20.refs_0_, ...), custom_call_target="tpu_custom_call" | custom-call | flops 4194304 | bytes 4194304 | tf_op jit(solution)/shard_map/pallas_call | solution.py:303
  (12 shorter events, 0.0 us)
Async XLA Ops:
  0.0 20.0 %copy-start.2 = (bf16[1,16,24,256]{3,2,1,0:T(8,128)(2,1)S(1)}, bf16[1,16,24,256]{3,2,1,0:T(8,128)(2,1)}, u32[]{:S(2)}) copy-start(bf16[1,16,24,256]{3,2,1,0:T(8,128)(2,1)} %own_ref.1) | copy-start | bytes 589828
  2.1 17.9 %copy-start = (bf16[32,32,128]{2,1,0:T(8,128)(2,1)S(1)}, bf16[32,32,128]{2,1,0:T(8,128)(2,1)}, u32[]{:S(2)}) copy-start(bf16[32,32,128]{2,1,0:T(8,128)(2,1)} %shard_map.37.pay_ref) | copy-start | bytes 786436
  2.1 17.9 %copy-start.1 = (bf16[16,24,256]{2,1,0:T(8,128)(2,1)S(1)}, bf16[16,24,256]{2,1,0:T(8,128)(2,1)}, u32[]{:S(2)}) copy-start(bf16[16,24,256]{2,1,0:T(8,128)(2,1)} %obs_ref.3) | copy-start | bytes 589828
  2.1 17.9 %copy-start.3 = (f32[16]{0:T(128)S(1)}, f32[16]{0:T(128)}, u32[]{:S(2)}) copy-start(f32[16]{0:T(128)} %scales_ref.5) | copy-start | bytes 196
  2.1 28.9 %all-to-all-start = ((bf16[32,32,128]{2,1,0:T(8,128)(2,1)}), bf16[32,32,128]{2,1,0:T(8,128)(2,1)S(1)}, u32[]{:S(2)}, u32[]{:S(2)}) async-start(bf16[32,32,128]{2,1,0:T(8,128)(2,1)} %shard_map.37.pay_ref), calls=%async_computation | async-start | bytes 524288 | tf_op jit(solution)/shard_map/all_to_all | solution.py:279
  20.7 17.2 %collective-permute-start.1 = (bf16[16,24,256]{2,1,0:T(8,128)(2,1)S(1)}, bf16[16,24,256]{2,1,0:T(8,128)(2,1)S(1)}, u32[]{:S(2)}, u32[]{:S(2)}) collective-permute-start(bf16[16,24,256]{2,1,0:T(8,128)(2,1)S(1)} %get-tuple-element.20.refs_0_), channel_id=1, source_target_pairs={{896,0},{0,128},{128,256},{256,384},{384,512},{512,640},{640,768},... | collective-permute-start | bytes 589832 | tf_op jit(solution)/shard_map/ppermute | solution.py:254
  24.1 13.9 %collective-permute-start = (bf16[16,24,256]{2,1,0:T(8,128)(2,1)S(1)}, bf16[16,24,256]{2,1,0:T(8,128)(2,1)S(1)}, u32[]{:S(2)}, u32[]{:S(2)}) collective-permute-start(bf16[16,24,256]{2,1,0:T(8,128)(2,1)S(1)} %get-tuple-element.20.refs_0_), channel_id=1, source_target_pairs={{128,0},{256,128},{384,256},{512,384},{640,512},{768,640},{896,768... | collective-permute-start | bytes 589832 | tf_op jit(solution)/shard_map/ppermute | solution.py:254
  32.7 12.2 %all-to-all-start.1 = ((f32[16,1,128]{2,1,0:T(1,128)}), f32[16,1,128]{2,1,0:T(1,128)S(1)}, u32[]{:S(2)}, u32[]{:S(2)}) async-start(f32[16,1,128]{2,1,0:T(1,128)} %get-tuple-element.16.refs_2_), calls=%async_computation.1 | async-start | bytes 16384 | tf_op jit(solution)/shard_map/all_to_all | solution.py:290
  38.0 20.3 %collective-permute-start.2 = (bf16[16,24,256]{2,1,0:T(8,128)(2,1)S(1)}, bf16[16,24,256]{2,1,0:T(8,128)(2,1)S(1)}, u32[]{:S(2)}, u32[]{:S(2)}) collective-permute-start(bf16[16,24,256]{2,1,0:T(8,128)(2,1)S(1)} %get-tuple-element.21.refs_1_), channel_id=1, source_target_pairs={{128,0},{256,128},{384,256},{512,384},{640,512},{768,640},{896,768... | collective-permute-start | bytes 589832 | tf_op jit(solution)/shard_map/ppermute | solution.py:254
  39.9 18.4 %collective-permute-start.3 = (bf16[16,24,256]{2,1,0:T(8,128)(2,1)S(1)}, bf16[16,24,256]{2,1,0:T(8,128)(2,1)S(1)}, u32[]{:S(2)}, u32[]{:S(2)}) collective-permute-start(bf16[16,24,256]{2,1,0:T(8,128)(2,1)S(1)} %get-tuple-element.22.refs_7_), channel_id=1, source_target_pairs={{896,0},{0,128},{128,256},{256,384},{384,512},{512,640},{640,768},... | collective-permute-start | bytes 589832 | tf_op jit(solution)/shard_map/ppermute | solution.py:254
  45.6 23.4 %all-to-all-start.2 = ((f32[64,1,128]{2,1,0:T(1,128)}), f32[64,1,128]{2,1,0:T(1,128)S(1)}, u32[]{:S(2)}, u32[]{:S(2)}) async-start(f32[64,1,128]{2,1,0:T(1,128)} %shard_map.40.refs_2_), calls=%async_computation.2 | async-start | bytes 65536 | tf_op jit(solution)/shard_map/all_to_all | solution.py:294
  58.3 15.9 %collective-permute-start.5 = (bf16[16,24,256]{2,1,0:T(8,128)(2,1)S(1)}, bf16[16,24,256]{2,1,0:T(8,128)(2,1)S(1)}, u32[]{:S(2)}, u32[]{:S(2)}) collective-permute-start(bf16[16,24,256]{2,1,0:T(8,128)(2,1)S(1)} %get-tuple-element.23.refs_2_), channel_id=1, source_target_pairs={{256,0},{384,128},{512,256},{640,384},{768,512},{896,640},{0,768},... | collective-permute-start | bytes 589832 | tf_op jit(solution)/shard_map/ppermute | solution.py:254
  63.5 13.0 %collective-permute-start.4 = (bf16[16,24,256]{2,1,0:T(8,128)(2,1)S(1)}, bf16[16,24,256]{2,1,0:T(8,128)(2,1)S(1)}, u32[]{:S(2)}, u32[]{:S(2)}) collective-permute-start(bf16[16,24,256]{2,1,0:T(8,128)(2,1)S(1)} %get-tuple-element.23.refs_2_), channel_id=1, source_target_pairs={{128,0},{256,128},{384,256},{512,384},{640,512},{768,640},{896,768... | collective-permute-start | bytes 589832 | tf_op jit(solution)/shard_map/ppermute | solution.py:254
  66.6 7.6 %collective-permute-start.6 = (bf16[16,24,256]{2,1,0:T(8,128)(2,1)S(1)}, bf16[16,24,256]{2,1,0:T(8,128)(2,1)S(1)}, u32[]{:S(2)}, u32[]{:S(2)}) collective-permute-start(bf16[16,24,256]{2,1,0:T(8,128)(2,1)S(1)} %get-tuple-element.24.refs_6_), channel_id=1, source_target_pairs={{896,0},{0,128},{128,256},{256,384},{384,512},{512,640},{640,768},... | collective-permute-start | bytes 589832 | tf_op jit(solution)/shard_map/ppermute | solution.py:254

commit v3 on v2

--- a/solution.py
+++ b/solution.py
@@ -65,7 +65,25 @@
     return (flat >= part * (CELLS // M)) & (flat < (part + 1) * (CELLS // M))
 
 
-def pack_kernel(own_hbm, obs_hbm, pay_ref, own_ref, obs_ref, sems):
+def fill_local(scales_ref, x, y, aux_ref):
+    w = tile_weights((ROWS, 128))
+    total = jnp.zeros((ROWS, 128), F32)
+    for c in range(C):
+        d = x[c] - y[c]
+        d = d * d
+        total = total + (d[:, :128] + d[:, 128:]) * inverse_square(scales_ref, c)
+    total = total * w
+    aux_ref[0:8] = (total[0:8] + total[8:16] + total[16:24]) * np.float32(1.0 / (C * LON * SUMW))
+    flat = iota((8, 128), 0) * 128 + iota((8, 128), 1)
+    channel = lax.shift_right_logical(flat * 2731, 16)
+    weight = row_weight(lat_index() * ROWS + flat - channel * ROWS)
+    inv = jnp.zeros((8, 128), F32)
+    for c in range(C):
+        inv = jnp.where(channel == c, inverse_square(scales_ref, c), inv)
+    aux_ref[8:16] = weight * inv * np.float32(1.0 / (C * SUMW * GROUP))
+
+
+def pack_kernel(scales_ref, own_hbm, obs_hbm, pay_ref, aux_ref, own_ref, obs_ref, sems):
     me = lax.axis_index("y")
     get_own = pltpu.make_async_copy(own_hbm, own_ref, sems.at[0])
     get_obs = pltpu.make_async_copy(obs_hbm, obs_ref, sems.at[1])
@@ -75,7 +93,9 @@
     x = own_ref[0].astype(F32)
     zx = lanes_sum(x)
     get_obs.wait()
-    zy = lanes_sum(obs_ref[...].astype(F32))
+    y = obs_ref[...].astype(F32)
+    zy = lanes_sum(y)
+    fill_local(scales_ref, x, y, aux_ref)
     row, lane = iota((8, 128), 0), iota((8, 128), 1)
 
     def high(v):
@@ -95,26 +115,8 @@
         pay_ref[d] = jnp.concatenate([x[d // 2, :, h * 128 : (h + 1) * 128], extra], axis=0).astype(BF16)
 
 
-def local_kernel(scales_ref, own_ref, obs_ref, pay_ref, aux_ref, copy_ref):
-    copy_ref[...] = own_ref[0]
-    w = tile_weights((ROWS, 128))
-    total = jnp.zeros((ROWS, 128), F32)
-    for c in range(C):
-        d = own_ref[0, c].astype(F32) - obs_ref[c].astype(F32)
-        d = d * d
-        total = total + (d[:, :128] + d[:, 128:]) * inverse_square(scales_ref, c)
-    total = total * w
-    aux_ref[0:8] = (total[0:8] + total[8:16] + total[16:24]) * np.float32(1.0 / (C * LON * SUMW))
-    flat = iota((8, 128), 0) * 128 + iota((8, 128), 1)
-    channel = lax.shift_right_logical(flat * 2731, 16)
-    weight = row_weight(lat_index() * ROWS + flat - channel * ROWS)
-    inv = jnp.zeros((8, 128), F32)
-    for c in range(C):
-        inv = jnp.where(channel == c, inverse_square(scales_ref, c), inv)
-    aux_ref[8:16] = weight * inv * np.float32(1.0 / (C * SUMW * GROUP))
-
-
-def distance_kernel(scales_ref, recv_ref, aux_ref, msg_ref, zall_ref, rows_ref):
+def distance_kernel(scales_ref, recv_ref, aux_ref, msg_ref, zall_ref, token_ref, rows_ref):
+    token_ref[...] = jnp.zeros((8, 128), F32)
     me = lax.axis_index("y")
     inv = inverse_square(scales_ref, me * 2 + lax.axis_index("xl"))
     w = tile_weights((ROWS, 128)) * (inv * np.float32(1.0 / (C * LON * SUMW)))
@@ -243,7 +245,7 @@
     return call(
         after_kernel,
         [jax.ShapeDtypeStruct(a.shape, a.dtype) for a in arrays],
-        [spec] * (len(arrays) + 1),
+        [spec] * len(arrays) + [VMEM],
         1 << 22,
         out_specs=[spec] * len(arrays),
         input_output_aliases={i: i for i in range(len(arrays))},
@@ -256,48 +258,42 @@
 
 def per_device(members, observed, scales):
     shape = jax.ShapeDtypeStruct
-    tile = shape((C, ROWS, COLS), BF16)
-    anywhere = pl.BlockSpec(memory_space=pl.ANY)
     hbm = pl.BlockSpec(memory_space=pltpu.HBM)
-    pay = call(
+    pay, aux = call(
         pack_kernel,
-        shape((GROUP, 32, 128), BF16),
-        [hbm] * 2,
+        (shape((GROUP, 32, 128), BF16), shape((16, 128), F32)),
+        [SMEM, hbm, hbm],
         1 << 20,
         vmem=60,
-        out_specs=VMEM,
+        out_specs=(VMEM, VMEM),
         scratch_shapes=[
             pltpu.VMEM((1, C, ROWS, COLS), BF16),
             pltpu.VMEM((C, ROWS, COLS), BF16),
             pltpu.SemaphoreType.DMA((2,)),
         ],
-    )(members, observed)
-    aux, own = call(
-        local_kernel, (shape((16, 128), F32), tile), [SMEM, VMEM, VMEM, anywhere], 1 << 20, out_specs=(VMEM, VMEM)
-    )(scales, members, observed, pay)
-    tiles = [own] + [None] * 7
+    )(scales, members, observed)
+    tiles = [members[0]] + [None] * 7
+    tiles[1], tiles[7] = from_ahead(tiles[0], 1), from_ahead(tiles[0], -1)
     recv = lax.all_to_all(pay, ("y", "xl", "core"), 0, 0, tiled=True)
-    tiles[1], tiles[7] = from_ahead(own, 1), from_ahead(own, -1)
-    msg, zall = call(
+    tiles[2], tiles[6] = from_ahead(tiles[0], 2), from_ahead(tiles[0], -2)
+    msg, zall, token = call(
         distance_kernel,
-        (shape((16, 1, 128), F32), shape((16, 8, 128), F32)),
+        (shape((16, 1, 128), F32), shape((16, 8, 128), F32), shape((8, 128), F32)),
         [SMEM, VMEM, VMEM],
         LONG,
-        out_specs=(VMEM, VMEM),
+        out_specs=(VMEM, VMEM, VMEM),
         scratch_shapes=[pltpu.VMEM((128, 128), F32)],
     )(scales, recv, aux)
-    tiles[1], tiles[7] = after([tiles[1], tiles[7]], msg)
     msg = lax.all_to_all(msg, ("xh", "xl", "core"), 0, 0, tiled=True)
-    tiles[2], tiles[6] = from_ahead(tiles[1], 1), from_ahead(tiles[7], -1)
+    tiles[1], tiles[2], tiles[6], tiles[7] = after([tiles[1], tiles[2], tiles[6], tiles[7]], token)
+    tiles[3], tiles[5], tiles[4] = from_ahead(tiles[2], 1), from_ahead(tiles[6], -1), from_ahead(tiles[2], 2)
     msg = call(relay_kernel, shape((64, 1, 128), F32), [VMEM], LONG, out_specs=VMEM)(msg)
-    tiles[2], tiles[6] = after([tiles[2], tiles[6]], msg)
     msg = lax.all_to_all(msg, ("y", "z"), 0, 0, tiled=True)
-    tiles[3], tiles[5], tiles[4] = from_ahead(tiles[2], 1), from_ahead(tiles[6], -1), from_ahead(tiles[2], 2)
     coef, zcol = call(
         coefficient_kernel,
         (shape((16, 128), F32), shape((CELLS, 128), F32)),
         [VMEM] * 2,
-        LONG,
+        1 << 16,
         out_specs=(VMEM, VMEM),
     )(msg, zall)
     return call(

time: 78.8 us -> 83.6 us (1.061)
  the two profiles are of different devices: /device:TPU:1 before, /device:TPU:4 now
where the time goes in v3:
time: 83.6 us; the launch traced here: 83.1 us
  starting transfers between devices  45.9 us (55%)
  blocking collectives  30.3 us (36%)
  Pallas kernels  6.54 us (8%)
    all_to_all x1, blocking collectives, per_device(): msg = lax.all_to_all(msg, ('y', 'z'), 0, 0, tiled=True)  30.3 us
    ppermute x7, starting transfers between devices, from_ahead(): return lax.ppermute(tile, 'y', [((i + k) % M, i) for i in range(M)])  25.5 us
    all_to_all x1, starting transfers between devices, per_device(): msg = lax.all_to_all(msg, ('xh', 'xl', 'core'), 0, 0, tiled=True)  11.4 us
    all_to_all x1, starting transfers between devices, per_device(): recv = lax.all_to_all(pay, ('y', 'xl', 'core'), 0, 0, tiled=True)  9.02 us
    pallas_call x1, Pallas kernels, per_device(): call(pack_kernel, (shape((GROUP, 32, 128), BF16), shape((16, 128), F32)),...  2.71 us
    pallas_call x1, Pallas kernels, per_device(): call(mix_kernel, shape((1, C, ROWS, COLS), F32), [SMEM] + [VMEM] * (3 + M...  1.84 us
  transfers between devices with their start and end apart: 9, of which 0 were waited for; matrix products, arithmetic and copies ran while one was open for 0% of the time, Pallas kernels for 2%

profile of v3, /device:TPU:4, one launch (start us, length us, event | category | flops | bytes accessed | tf_op | source)
XLA Modules:
  0.0 83.1 jit_solution(15080243609992404980)
XLA Ops:
  0.0 2.7 %shard_map.37 = (bf16[32,32,128]{2,1,0:T(8,128)(2,1)}, f32[16,128]{1,0:T(8,128)}) custom-call(f32[16]{0:T(128)} %scales_ref.5, bf16[1,16,24,256]{3,2,1,0:T(8,128)(2,1)} %own_hbm.1, bf16[16,24,256]{2,1,0:T(8,128)(2,1)} %obs_ref.1), custom_call_target="tpu_custom_call" | custom-call | flops 1048576 | bytes 1048576 | tf_op jit(solution)/shard_map/pallas_call | solution.py:262
  2.7 0.0 copy-start
  2.7 9.0 %all-to-all-start = ((bf16[32,32,128]{2,1,0:T(8,128)(2,1)}), bf16[32,32,128]{2,1,0:T(8,128)(2,1)S(1)}, u32[]{:S(2)}, u32[]{:S(2)}) async-start(bf16[32,32,128]{2,1,0:T(8,128)(2,1)} %get-tuple-element.16), calls=%async_computation | async-start | bytes 524288 | tf_op jit(solution)/shard_map/all_to_all | solution.py:277
  11.8 0.0 copy-start.2
  11.8 3.7 %collective-permute-start.3 = (bf16[16,24,256]{2,1,0:T(8,128)(2,1)S(1)}, bf16[16,24,256]{2,1,0:T(8,128)(2,1)S(1)}, u32[]{:S(2)}, u32[]{:S(2)}) collective-permute-start(bf16[16,24,256]{2,1,0:T(8,128)(2,1)S(1)} %bitcast.1), channel_id=1, source_target_pairs={{896,0},{0,128},{128,256},{256,384},{384,512},{512,640},{640,768},... | collective-permute-start | bytes 589832 | tf_op jit(solution)/shard_map/ppermute | solution.py:256
  15.5 4.3 %collective-permute-start.2 = (bf16[16,24,256]{2,1,0:T(8,128)(2,1)S(1)}, bf16[16,24,256]{2,1,0:T(8,128)(2,1)S(1)}, u32[]{:S(2)}, u32[]{:S(2)}) collective-permute-start(bf16[16,24,256]{2,1,0:T(8,128)(2,1)S(1)} %bitcast.2), channel_id=1, source_target_pairs={{768,0},{896,128},{0,256},{128,384},{256,512},{384,640},{512,768},... | collective-permute-start | bytes 589832 | tf_op jit(solution)/shard_map/ppermute | solution.py:256
  19.8 3.7 %collective-permute-start.1 = (bf16[16,24,256]{2,1,0:T(8,128)(2,1)S(1)}, bf16[16,24,256]{2,1,0:T(8,128)(2,1)S(1)}, u32[]{:S(2)}, u32[]{:S(2)}) collective-permute-start(bf16[16,24,256]{2,1,0:T(8,128)(2,1)S(1)} %bitcast.3), channel_id=1, source_target_pairs={{256,0},{384,128},{512,256},{640,384},{768,512},{896,640},{0,768},... | collective-permute-start | bytes 589832 | tf_op jit(solution)/shard_map/ppermute | solution.py:256
  23.5 2.1 %collective-permute-start = (bf16[16,24,256]{2,1,0:T(8,128)(2,1)S(1)}, bf16[16,24,256]{2,1,0:T(8,128)(2,1)S(1)}, u32[]{:S(2)}, u32[]{:S(2)}) collective-permute-start(bf16[16,24,256]{2,1,0:T(8,128)(2,1)S(1)} %bitcast.4), channel_id=1, source_target_pairs={{128,0},{256,128},{384,256},{512,384},{640,512},{768,640},{896,768... | collective-permute-start | bytes 589832 | tf_op jit(solution)/shard_map/ppermute | solution.py:256
  25.6 0.0 all-to-all-done.recv_ref
  25.6 1.7 %shard_map.38 = (f32[16,1,128]{2,1,0:T(1,128)}, f32[16,8,128]{2,1,0:T(8,128)S(1)}, f32[8,128]{1,0:T(8,128)S(1)}) custom-call(f32[16]{0:T(128)S(1)} %copy-done.2, bf16[32,32,128]{2,1,0:T(8,128)(2,1)S(1)} %all-to-all-done.recv_ref, f32[16,128]{1,0:T(8,128)S(1)} %copy-done.3), custom_call_target="tpu_custom_call" | custom-call | flops 68719476736 | bytes 68719476736 | tf_op jit(solution)/shard_map/pallas_call | solution.py:279
  27.3 11.4 %all-to-all-start.1 = ((f32[16,1,128]{2,1,0:T(1,128)}), f32[16,1,128]{2,1,0:T(1,128)S(1)}, u32[]{:S(2)}, u32[]{:S(2)}) async-start(f32[16,1,128]{2,1,0:T(1,128)} %get-tuple-element.18), calls=%async_computation.1 | async-start | bytes 16384 | tf_op jit(solution)/shard_map/all_to_all | solution.py:287
  38.7 0.0 collective-permute-done.3.refs_3_
  38.8 0.0 collective-permute-done.2.refs_2_
  38.8 0.0 collective-permute-done.1.refs_1_
  38.8 0.0 collective-permute-done.refs_0_
  38.8 5.9 %collective-permute-start.5 = (bf16[16,24,256]{2,1,0:T(8,128)(2,1)S(1)}, bf16[16,24,256]{2,1,0:T(8,128)(2,1)S(1)}, u32[]{:S(2)}, u32[]{:S(2)}) collective-permute-start(bf16[16,24,256]{2,1,0:T(8,128)(2,1)S(1)} %get-tuple-element.24.refs_2_), channel_id=1, source_target_pairs={{256,0},{384,128},{512,256},{640,384},{768,512},{896,640},{0,768},... | collective-permute-start | bytes 589832 | tf_op jit(solution)/shard_map/ppermute | solution.py:256
  44.7 3.3 %collective-permute-start.4 = (bf16[16,24,256]{2,1,0:T(8,128)(2,1)S(1)}, bf16[16,24,256]{2,1,0:T(8,128)(2,1)S(1)}, u32[]{:S(2)}, u32[]{:S(2)}) collective-permute-start(bf16[16,24,256]{2,1,0:T(8,128)(2,1)S(1)} %get-tuple-element.24.refs_2_), channel_id=1, source_target_pairs={{128,0},{256,128},{384,256},{512,384},{640,512},{768,640},{896,768... | collective-permute-start | bytes 589832 | tf_op jit(solution)/shard_map/ppermute | solution.py:256
  48.0 2.5 %collective-permute-start.6 = (bf16[16,24,256]{2,1,0:T(8,128)(2,1)S(1)}, bf16[16,24,256]{2,1,0:T(8,128)(2,1)S(1)}, u32[]{:S(2)}, u32[]{:S(2)}) collective-permute-start(bf16[16,24,256]{2,1,0:T(8,128)(2,1)S(1)} %get-tuple-element.25.refs_6_), channel_id=1, source_target_pairs={{896,0},{0,128},{128,256},{256,384},{384,512},{512,640},{640,768},... | collective-permute-start | bytes 589832 | tf_op jit(solution)/shard_map/ppermute | solution.py:256
  50.5 0.0 all-to-all-done.1.in_ref
  50.5 0.0 copy-start.1
  50.6 30.3 %all_to_all.15.msg_ref = f32[64,1,128]{2,1,0:T(1,128)S(1)} all-to-all(f32[64,1,128]{2,1,0:T(1,128)S(1)} %shard_map.39), channel_id=1, replica_groups=mesh['y'=8,'z'=8,'xh'=4,'xl'=2,'core'=2] {'y','z'}, dimensions={0} | all-to-all | bytes 65536 | tf_op jit(solution)/shard_map/all_to_all | solution.py:291
  80.9 0.3 shard_map.40
  81.2 0.0 collective-permute-done.4.refs_3_
  81.2 1.8 %shard_map.42 = f32[1,16,24,256]{3,2,1,0:T(8,128)} custom-call(f32[16]{0:T(128)S(1)} %copy-done.2, f32[16,128]{1,0:T(8,128)S(1)} %get-tuple-element.20.coef_ref, f32[384,128]{1,0:T(8,128)S(1)} %get-tuple-element.21.zcol_ref, bf16[16,24,256]{2,1,0:T(8,128)(2,1)S(1)} %copy-done.1, bf16[16,24,256]{2,1,0:T(8,128)(2,1)S(1)} %bitcast.5, ...), custom_call_target="tpu_custom_call" | custom-call | flops 4194304 | bytes 4194304 | tf_op jit(solution)/shard_map/pallas_call | solution.py:299
  (9 shorter events, 0.1 us)
Async XLA Ops:
  2.7 9.1 %copy-start = (bf16[1,16,24,256]{3,2,1,0:T(8,128)(2,1)S(1)}, bf16[1,16,24,256]{3,2,1,0:T(8,128)(2,1)}, u32[]{:S(2)}) copy-start(bf16[1,16,24,256]{3,2,1,0:T(8,128)(2,1)} %own_hbm.1) | copy-start | bytes 589828
  2.7 22.9 %copy-start.3 = (f32[16,128]{1,0:T(8,128)S(1)}, f32[16,128]{1,0:T(8,128)}, u32[]{:S(2)}) copy-start(f32[16,128]{1,0:T(8,128)} %get-tuple-element.17.aux_ref) | copy-start | bytes 24580
  2.7 22.9 %all-to-all-start = ((bf16[32,32,128]{2,1,0:T(8,128)(2,1)}), bf16[32,32,128]{2,1,0:T(8,128)(2,1)S(1)}, u32[]{:S(2)}, u32[]{:S(2)}) async-start(bf16[32,32,128]{2,1,0:T(8,128)(2,1)} %get-tuple-element.16), calls=%async_computation | async-start | bytes 524288 | tf_op jit(solution)/shard_map/all_to_all | solution.py:277
  11.8 13.9 %copy-start.2 = (f32[16]{0:T(128)S(1)}, f32[16]{0:T(128)}, u32[]{:S(2)}) copy-start(f32[16]{0:T(128)} %scales_ref.5) | copy-start | bytes 196
  11.8 27.0 %collective-permute-start.3 = (bf16[16,24,256]{2,1,0:T(8,128)(2,1)S(1)}, bf16[16,24,256]{2,1,0:T(8,128)(2,1)S(1)}, u32[]{:S(2)}, u32[]{:S(2)}) collective-permute-start(bf16[16,24,256]{2,1,0:T(8,128)(2,1)S(1)} %bitcast.1), channel_id=1, source_target_pairs={{896,0},{0,128},{128,256},{256,384},{384,512},{512,640},{640,768},... | collective-permute-start | bytes 589832 | tf_op jit(solution)/shard_map/ppermute | solution.py:256
  15.5 23.3 %collective-permute-start.2 = (bf16[16,24,256]{2,1,0:T(8,128)(2,1)S(1)}, bf16[16,24,256]{2,1,0:T(8,128)(2,1)S(1)}, u32[]{:S(2)}, u32[]{:S(2)}) collective-permute-start(bf16[16,24,256]{2,1,0:T(8,128)(2,1)S(1)} %bitcast.2), channel_id=1, source_target_pairs={{768,0},{896,128},{0,256},{128,384},{256,512},{384,640},{512,768},... | collective-permute-start | bytes 589832 | tf_op jit(solution)/shard_map/ppermute | solution.py:256
  19.8 19.0 %collective-permute-start.1 = (bf16[16,24,256]{2,1,0:T(8,128)(2,1)S(1)}, bf16[16,24,256]{2,1,0:T(8,128)(2,1)S(1)}, u32[]{:S(2)}, u32[]{:S(2)}) collective-permute-start(bf16[16,24,256]{2,1,0:T(8,128)(2,1)S(1)} %bitcast.3), channel_id=1, source_target_pairs={{256,0},{384,128},{512,256},{640,384},{768,512},{896,640},{0,768},... | collective-permute-start | bytes 589832 | tf_op jit(solution)/shard_map/ppermute | solution.py:256
  23.5 15.3 %collective-permute-start = (bf16[16,24,256]{2,1,0:T(8,128)(2,1)S(1)}, bf16[16,24,256]{2,1,0:T(8,128)(2,1)S(1)}, u32[]{:S(2)}, u32[]{:S(2)}) collective-permute-start(bf16[16,24,256]{2,1,0:T(8,128)(2,1)S(1)} %bitcast.4), channel_id=1, source_target_pairs={{128,0},{256,128},{384,256},{512,384},{640,512},{768,640},{896,768... | collective-permute-start | bytes 589832 | tf_op jit(solution)/shard_map/ppermute | solution.py:256
  27.3 23.2 %all-to-all-start.1 = ((f32[16,1,128]{2,1,0:T(1,128)}), f32[16,1,128]{2,1,0:T(1,128)S(1)}, u32[]{:S(2)}, u32[]{:S(2)}) async-start(f32[16,1,128]{2,1,0:T(1,128)} %get-tuple-element.18), calls=%async_computation.1 | async-start | bytes 16384 | tf_op jit(solution)/shard_map/all_to_all | solution.py:287
  38.8 42.4 %collective-permute-start.5 = (bf16[16,24,256]{2,1,0:T(8,128)(2,1)S(1)}, bf16[16,24,256]{2,1,0:T(8,128)(2,1)S(1)}, u32[]{:S(2)}, u32[]{:S(2)}) collective-permute-start(bf16[16,24,256]{2,1,0:T(8,128)(2,1)S(1)} %get-tuple-element.24.refs_2_), channel_id=1, source_target_pairs={{256,0},{384,128},{512,256},{640,384},{768,512},{896,640},{0,768},... | collective-permute-start | bytes 589832 | tf_op jit(solution)/shard_map/ppermute | solution.py:256
  44.7 36.5 %collective-permute-start.4 = (bf16[16,24,256]{2,1,0:T(8,128)(2,1)S(1)}, bf16[16,24,256]{2,1,0:T(8,128)(2,1)S(1)}, u32[]{:S(2)}, u32[]{:S(2)}) collective-permute-start(bf16[16,24,256]{2,1,0:T(8,128)(2,1)S(1)} %get-tuple-element.24.refs_2_), channel_id=1, source_target_pairs={{128,0},{256,128},{384,256},{512,384},{640,512},{768,640},{896,768... | collective-permute-start | bytes 589832 | tf_op jit(solution)/shard_map/ppermute | solution.py:256
  48.0 33.2 %collective-permute-start.6 = (bf16[16,24,256]{2,1,0:T(8,128)(2,1)S(1)}, bf16[16,24,256]{2,1,0:T(8,128)(2,1)S(1)}, u32[]{:S(2)}, u32[]{:S(2)}) collective-permute-start(bf16[16,24,256]{2,1,0:T(8,128)(2,1)S(1)} %get-tuple-element.25.refs_6_), channel_id=1, source_target_pairs={{896,0},{0,128},{128,256},{256,384},{384,512},{512,640},{640,768},... | collective-permute-start | bytes 589832 | tf_op jit(solution)/shard_map/ppermute | solution.py:256
  50.5 30.7 %copy-start.1 = (bf16[16,24,256]{2,1,0:T(8,128)(2,1)S(1)}, bf16[16,24,256]{2,1,0:T(8,128)(2,1)}, u32[]{:S(2)}) copy-start(bf16[16,24,256]{2,1,0:T(8,128)(2,1)} %obs_ref.1) | copy-start | bytes 589828

commit v4 on v3

--- a/solution.py
+++ b/solution.py
@@ -173,8 +173,12 @@
     out_ref[...] = jnp.broadcast_to(total[None], out_ref.shape)
 
 
-def after_kernel(*refs):
-    pass
+def stack_kernel(own_ref, up_ref, down_ref, token_ref, ups_ref, downs_ref, again_ref):
+    ups_ref[0] = own_ref[0]
+    ups_ref[1] = up_ref[...]
+    downs_ref[0] = own_ref[0]
+    downs_ref[1] = down_ref[...]
+    again_ref[...] = up_ref[...]
 
 
 def coefficient_kernel(msg_ref, zall_ref, coef_ref, zcol_ref):
@@ -202,8 +206,12 @@
         zcol_ref[b * 128 : (b + 1) * 128] = jnp.broadcast_to(z[b : b + 1], (128, 128)).T
 
 
-def mix_kernel(scales_ref, coef_ref, zcol_ref, obs_ref, *refs):
-    tiles, (out_hbm, out_ref, sems) = refs[:M], refs[M:]
+def mix_kernel(
+    scales_ref, coef_ref, zcol_ref, obs_ref, own_ref, t2_ref, t4_ref, t6_ref, ups_ref, downs_ref, out_hbm, out_ref, sems
+):
+    tiles = [
+        own_ref.at[0], ups_ref.at[0], t2_ref, ups_ref.at[1], t4_ref, downs_ref.at[1], t6_ref, downs_ref.at[0]
+    ]
     fac = tile_weights((ROWS, COLS)) * np.float32(LAT / SUMW)
     coef = coef_ref[...]
     coef = jnp.concatenate([coef, coef], axis=1)
@@ -240,18 +248,6 @@
     )
 
 
-def after(arrays, made):
-    spec = pl.BlockSpec(memory_space=pl.ANY)
-    return call(
-        after_kernel,
-        [jax.ShapeDtypeStruct(a.shape, a.dtype) for a in arrays],
-        [spec] * len(arrays) + [VMEM],
-        1 << 22,
-        out_specs=[spec] * len(arrays),
-        input_output_aliases={i: i for i in range(len(arrays))},
-    )(*arrays, made)
-
-
 def from_ahead(tile, k):
     return lax.ppermute(tile, "y", [((i + k) % M, i) for i in range(M)])
 
@@ -273,7 +269,6 @@
         ],
     )(scales, members, observed)
     tiles = [members[0]] + [None] * 7
-    tiles[1], tiles[7] = from_ahead(tiles[0], 1), from_ahead(tiles[0], -1)
     recv = lax.all_to_all(pay, ("y", "xl", "core"), 0, 0, tiled=True)
     tiles[2], tiles[6] = from_ahead(tiles[0], 2), from_ahead(tiles[0], -2)
     msg, zall, token = call(
@@ -285,8 +280,13 @@
         scratch_shapes=[pltpu.VMEM((128, 128), F32)],
     )(scales, recv, aux)
     msg = lax.all_to_all(msg, ("xh", "xl", "core"), 0, 0, tiled=True)
-    tiles[1], tiles[2], tiles[6], tiles[7] = after([tiles[1], tiles[2], tiles[6], tiles[7]], token)
-    tiles[3], tiles[5], tiles[4] = from_ahead(tiles[2], 1), from_ahead(tiles[6], -1), from_ahead(tiles[2], 2)
+    tile = shape((C, ROWS, COLS), BF16)
+    pair = shape((2, C, ROWS, COLS), BF16)
+    ups, downs, again = call(stack_kernel, (pair, pair, tile), [VMEM] * 4, 1 << 22, out_specs=(VMEM,) * 3)(
+        members, tiles[2], tiles[6], token
+    )
+    ups, downs = from_ahead(ups, 1), from_ahead(downs, -1)
+    tiles[4] = from_ahead(again, 2)
     msg = call(relay_kernel, shape((64, 1, 128), F32), [VMEM], LONG, out_specs=VMEM)(msg)
     msg = lax.all_to_all(msg, ("y", "z"), 0, 0, tiled=True)
     coef, zcol = call(
@@ -299,11 +299,11 @@
     return call(
         mix_kernel,
         shape((1, C, ROWS, COLS), F32),
-        [SMEM] + [VMEM] * (3 + M),
+        [SMEM] + [VMEM] * 9,
         1 << 22,
         out_specs=hbm,
         scratch_shapes=[pltpu.VMEM((C, ROWS, COLS), F32), pltpu.SemaphoreType.DMA((PARTS,))],
-    )(scales, coef, zcol, observed, *tiles)
+    )(scales, coef, zcol, observed, members, tiles[2], tiles[4], tiles[6], ups, downs)
 
 
 def solution(mesh):

time: 83.6 us -> 76.7 us (0.917)
  starting transfers between devices: 45.9 us -> 36.5 us
  waiting for transfers between devices: 0.02 us -> 4.42 us
  blocking collectives: 30.3 us -> 28.5 us
    ppermute x7 -> x5, starting transfers between devices: 25.5 us -> 15.9 us  [from_ahead(): return lax.ppermute(tile, 'y', [((i + k) % M, i) for i in range(M)])]
    all_to_all x1, waiting for transfers between devices: 0.01 us -> 4.4 us  [per_device(): recv = lax.all_to_all(pay, ('y', 'xl', 'core'), 0, 0, tiled=True)]
    all_to_all x1, blocking collectives: 30.3 us -> 28.5 us  [per_device(): msg = lax.all_to_all(msg, ('y', 'z'), 0, 0, tiled=True)]
  transfers between devices with their start and end apart: 9 -> 7, of which waited for: 0 -> 1; matrix products, arithmetic and copies ran while one was open for 0% -> 0% of each run, Pallas kernels for 2% -> 3%
where the time goes in v4:
time: 76.7 us; the launch traced here: 76.2 us
  starting transfers between devices  36.5 us (48%)
  blocking collectives  28.5 us (37%)
  Pallas kernels  6.63 us (9%)
  waiting for transfers between devices  4.42 us (6%)
    all_to_all x1, blocking collectives, per_device(): msg = lax.all_to_all(msg, ('y', 'z'), 0, 0, tiled=True)  28.5 us
    ppermute x5, starting transfers between devices, from_ahead(): return lax.ppermute(tile, 'y', [((i + k) % M, i) for i in range(M)])  15.9 us
    all_to_all x1, starting transfers between devices, per_device(): msg = lax.all_to_all(msg, ('xh', 'xl', 'core'), 0, 0, tiled=True)  11.6 us
    all_to_all x1, starting transfers between devices, per_device(): recv = lax.all_to_all(pay, ('y', 'xl', 'core'), 0, 0, tiled=True)  9.02 us
    all_to_all x1, waiting for transfers between devices, per_device(): recv = lax.all_to_all(pay, ('y', 'xl', 'core'), 0, 0, tiled=True)  4.4 us
    pallas_call x1, Pallas kernels, per_device(): call(pack_kernel, (shape((GROUP, 32, 128), BF16), shape((16, 128), F32)),...  2.71 us
    pallas_call x1, Pallas kernels, per_device(): call(mix_kernel, shape((1, C, ROWS, COLS), F32), [SMEM] + [VMEM] * 9, 1 <...  1.87 us
    pallas_call x1, Pallas kernels, per_device(): call(distance_kernel, (shape((16, 1, 128), F32), shape((16, 8, 128), F32)...  1.67 us
  transfers between devices with their start and end apart: 7, of which 1 were waited for; matrix products, arithmetic and copies ran while one was open for 0% of the time, Pallas kernels for 3%

profile of v4, /device:TPU:4, one launch (start us, length us, event | category | flops | bytes accessed | tf_op | source)
XLA Modules:
  0.0 76.2 jit_solution(13279665975645789829)
XLA Ops:
  0.0 2.7 %shard_map.37 = (bf16[32,32,128]{2,1,0:T(8,128)(2,1)}, f32[16,128]{1,0:T(8,128)}) custom-call(f32[16]{0:T(128)} %scales_ref.5, bf16[1,16,24,256]{3,2,1,0:T(8,128)(2,1)} %own_ref.3, bf16[16,24,256]{2,1,0:T(8,128)(2,1)} %obs_ref.1), custom_call_target="tpu_custom_call" | custom-call | flops 1048576 | bytes 1048576 | tf_op jit(solution)/shard_map/pallas_call | solution.py:258
  2.7 0.0 copy-start
  2.7 9.0 %all-to-all-start = ((bf16[32,32,128]{2,1,0:T(8,128)(2,1)}), bf16[32,32,128]{2,1,0:T(8,128)(2,1)S(1)}, u32[]{:S(2)}, u32[]{:S(2)}) async-start(bf16[32,32,128]{2,1,0:T(8,128)(2,1)} %get-tuple-element.15), calls=%async_computation | async-start | bytes 524288 | tf_op jit(solution)/shard_map/all_to_all | solution.py:272
  11.8 0.0 copy-start.2
  11.8 5.9 %collective-permute-start = (bf16[16,24,256]{2,1,0:T(8,128)(2,1)S(1)}, bf16[16,24,256]{2,1,0:T(8,128)(2,1)S(1)}, u32[]{:S(2)}, u32[]{:S(2)}) collective-permute-start(bf16[16,24,256]{2,1,0:T(8,128)(2,1)S(1)} %bitcast.1), channel_id=1, source_target_pairs={{256,0},{384,128},{512,256},{640,384},{768,512},{896,640},{0,768},... | collective-permute-start | bytes 589832 | tf_op jit(solution)/shard_map/ppermute | solution.py:252
  17.6 1.9 %collective-permute-start.1 = (bf16[16,24,256]{2,1,0:T(8,128)(2,1)S(1)}, bf16[16,24,256]{2,1,0:T(8,128)(2,1)S(1)}, u32[]{:S(2)}, u32[]{:S(2)}) collective-permute-start(bf16[16,24,256]{2,1,0:T(8,128)(2,1)S(1)} %bitcast.2), channel_id=1, source_target_pairs={{768,0},{896,128},{0,256},{128,384},{256,512},{384,640},{512,768},... | collective-permute-start | bytes 589832 | tf_op jit(solution)/shard_map/ppermute | solution.py:252
  19.6 4.4 %all-to-all-done.recv_ref = bf16[32,32,128]{2,1,0:T(8,128)(2,1)S(1)} async-done(((bf16[32,32,128]{2,1,0:T(8,128)(2,1)}), bf16[32,32,128]{2,1,0:T(8,128)(2,1)S(1)}, u32[]{:S(2)}, u32[]{:S(2)}) %all-to-all-start) | async-done | bytes 262176 | tf_op jit(solution)/shard_map/all_to_all | solution.py:272
  24.0 0.0 copy-done.3
  24.0 1.7 %shard_map.38 = (f32[16,1,128]{2,1,0:T(1,128)}, f32[16,8,128]{2,1,0:T(8,128)S(1)}, f32[8,128]{1,0:T(8,128)S(1)}) custom-call(f32[16]{0:T(128)S(1)} %copy-done.2, bf16[32,32,128]{2,1,0:T(8,128)(2,1)S(1)} %all-to-all-done.recv_ref, f32[16,128]{1,0:T(8,128)S(1)} %copy-done.3), custom_call_target="tpu_custom_call" | custom-call | flops 68719476736 | bytes 68719476736 | tf_op jit(solution)/shard_map/pallas_call | solution.py:274
  25.7 11.6 %all-to-all-start.1 = ((f32[16,1,128]{2,1,0:T(1,128)}), f32[16,1,128]{2,1,0:T(1,128)S(1)}, u32[]{:S(2)}, u32[]{:S(2)}) async-start(f32[16,1,128]{2,1,0:T(1,128)} %get-tuple-element.17), calls=%async_computation.1 | async-start | bytes 16384 | tf_op jit(solution)/shard_map/all_to_all | solution.py:282
  37.2 0.0 collective-permute-done.up_ref.t2_ref
  37.2 0.0 collective-permute-done.1.down_ref.t6_ref
  37.3 0.1 shard_map.41
  37.3 1.9 %collective-permute-start.3 = (bf16[2,16,24,256]{3,2,1,0:T(8,128)(2,1)S(1)}, bf16[2,16,24,256]{3,2,1,0:T(8,128)(2,1)S(1)}, u32[]{:S(2)}, u32[]{:S(2)}) collective-permute-start(bf16[2,16,24,256]{3,2,1,0:T(8,128)(2,1)S(1)} %get-tuple-element.23), channel_id=1, source_target_pairs={{128,0},{256,128},{384,256},{512,384},{640,512},{768,640},{896,768... | collective-permute-start | bytes 1179656 | tf_op jit(solution)/shard_map/ppermute | solution.py:252
  39.3 3.9 %collective-permute-start.4 = (bf16[2,16,24,256]{3,2,1,0:T(8,128)(2,1)S(1)}, bf16[2,16,24,256]{3,2,1,0:T(8,128)(2,1)S(1)}, u32[]{:S(2)}, u32[]{:S(2)}) collective-permute-start(bf16[2,16,24,256]{3,2,1,0:T(8,128)(2,1)S(1)} %get-tuple-element.24), channel_id=1, source_target_pairs={{896,0},{0,128},{128,256},{256,384},{384,512},{512,640},{640,768},... | collective-permute-start | bytes 1179656 | tf_op jit(solution)/shard_map/ppermute | solution.py:252
  43.2 2.3 %collective-permute-start.2 = (bf16[16,24,256]{2,1,0:T(8,128)(2,1)S(1)}, bf16[16,24,256]{2,1,0:T(8,128)(2,1)S(1)}, u32[]{:S(2)}, u32[]{:S(2)}) collective-permute-start(bf16[16,24,256]{2,1,0:T(8,128)(2,1)S(1)} %get-tuple-element.22), channel_id=1, source_target_pairs={{256,0},{384,128},{512,256},{640,384},{768,512},{896,640},{0,768},... | collective-permute-start | bytes 589832 | tf_op jit(solution)/shard_map/ppermute | solution.py:252
  45.5 0.0 all-to-all-done.1.in_ref
  45.5 0.0 copy-start.1
  45.5 28.5 %all_to_all.15.msg_ref = f32[64,1,128]{2,1,0:T(1,128)S(1)} all-to-all(f32[64,1,128]{2,1,0:T(1,128)S(1)} %shard_map.39), channel_id=1, replica_groups=mesh['y'=8,'z'=8,'xh'=4,'xl'=2,'core'=2] {'y','z'}, dimensions={0} | all-to-all | bytes 65536 | tf_op jit(solution)/shard_map/all_to_all | solution.py:291
  74.0 0.3 shard_map.40
  74.3 0.0 collective-permute-done.2.t4_ref
  74.3 0.0 collective-permute-done.3.ups_ref
  74.3 0.0 collective-permute-done.4.downs_ref
  74.4 1.9 %shard_map.42 = f32[1,16,24,256]{3,2,1,0:T(8,128)} custom-call(f32[16]{0:T(128)S(1)} %copy-done.2, f32[16,128]{1,0:T(8,128)S(1)} %get-tuple-element.19.coef_ref, f32[384,128]{1,0:T(8,128)S(1)} %get-tuple-element.20.zcol_ref, bf16[16,24,256]{2,1,0:T(8,128)(2,1)S(1)} %copy-done.1, bf16[1,16,24,256]{3,2,1,0:T(8,128)(2,1)S(1)} %copy-done, ...), custom_call_target="tpu_custom_call" | custom-call | flops 4194304 | bytes 4194304 | tf_op jit(solution)/shard_map/pallas_call | solution.py:299
  (5 shorter events, 0.0 us)
Async XLA Ops:
  2.7 9.1 %copy-start = (bf16[1,16,24,256]{3,2,1,0:T(8,128)(2,1)S(1)}, bf16[1,16,24,256]{3,2,1,0:T(8,128)(2,1)}, u32[]{:S(2)}) copy-start(bf16[1,16,24,256]{3,2,1,0:T(8,128)(2,1)} %own_ref.3) | copy-start | bytes 589828
  2.7 21.2 %copy-start.3 = (f32[16,128]{1,0:T(8,128)S(1)}, f32[16,128]{1,0:T(8,128)}, u32[]{:S(2)}) copy-start(f32[16,128]{1,0:T(8,128)} %get-tuple-element.16.aux_ref) | copy-start | bytes 24580
  2.7 21.2 %all-to-all-start = ((bf16[32,32,128]{2,1,0:T(8,128)(2,1)}), bf16[32,32,128]{2,1,0:T(8,128)(2,1)S(1)}, u32[]{:S(2)}, u32[]{:S(2)}) async-start(bf16[32,32,128]{2,1,0:T(8,128)(2,1)} %get-tuple-element.15), calls=%async_computation | async-start | bytes 524288 | tf_op jit(solution)/shard_map/all_to_all | solution.py:272
  11.8 12.2 %copy-start.2 = (f32[16]{0:T(128)S(1)}, f32[16]{0:T(128)}, u32[]{:S(2)}) copy-start(f32[16]{0:T(128)} %scales_ref.5) | copy-start | bytes 196
  11.8 25.5 %collective-permute-start = (bf16[16,24,256]{2,1,0:T(8,128)(2,1)S(1)}, bf16[16,24,256]{2,1,0:T(8,128)(2,1)S(1)}, u32[]{:S(2)}, u32[]{:S(2)}) collective-permute-start(bf16[16,24,256]{2,1,0:T(8,128)(2,1)S(1)} %bitcast.1), channel_id=1, source_target_pairs={{256,0},{384,128},{512,256},{640,384},{768,512},{896,640},{0,768},... | collective-permute-start | bytes 589832 | tf_op jit(solution)/shard_map/ppermute | solution.py:252
  17.6 19.6 %collective-permute-start.1 = (bf16[16,24,256]{2,1,0:T(8,128)(2,1)S(1)}, bf16[16,24,256]{2,1,0:T(8,128)(2,1)S(1)}, u32[]{:S(2)}, u32[]{:S(2)}) collective-permute-start(bf16[16,24,256]{2,1,0:T(8,128)(2,1)S(1)} %bitcast.2), channel_id=1, source_target_pairs={{768,0},{896,128},{0,256},{128,384},{256,512},{384,640},{512,768},... | collective-permute-start | bytes 589832 | tf_op jit(solution)/shard_map/ppermute | solution.py:252
  25.7 19.8 %all-to-all-start.1 = ((f32[16,1,128]{2,1,0:T(1,128)}), f32[16,1,128]{2,1,0:T(1,128)S(1)}, u32[]{:S(2)}, u32[]{:S(2)}) async-start(f32[16,1,128]{2,1,0:T(1,128)} %get-tuple-element.17), calls=%async_computation.1 | async-start | bytes 16384 | tf_op jit(solution)/shard_map/all_to_all | solution.py:282
  37.3 37.0 %collective-permute-start.3 = (bf16[2,16,24,256]{3,2,1,0:T(8,128)(2,1)S(1)}, bf16[2,16,24,256]{3,2,1,0:T(8,128)(2,1)S(1)}, u32[]{:S(2)}, u32[]{:S(2)}) collective-permute-start(bf16[2,16,24,256]{3,2,1,0:T(8,128)(2,1)S(1)} %get-tuple-element.23), channel_id=1, source_target_pairs={{128,0},{256,128},{384,256},{512,384},{640,512},{768,640},{896,768... | collective-permute-start | bytes 1179656 | tf_op jit(solution)/shard_map/ppermute | solution.py:252
  39.3 35.1 %collective-permute-start.4 = (bf16[2,16,24,256]{3,2,1,0:T(8,128)(2,1)S(1)}, bf16[2,16,24,256]{3,2,1,0:T(8,128)(2,1)S(1)}, u32[]{:S(2)}, u32[]{:S(2)}) collective-permute-start(bf16[2,16,24,256]{3,2,1,0:T(8,128)(2,1)S(1)} %get-tuple-element.24), channel_id=1, source_target_pairs={{896,0},{0,128},{128,256},{256,384},{384,512},{512,640},{640,768},... | collective-permute-start | bytes 1179656 | tf_op jit(solution)/shard_map/ppermute | solution.py:252
  43.2 31.1 %collective-permute-start.2 = (bf16[16,24,256]{2,1,0:T(8,128)(2,1)S(1)}, bf16[16,24,256]{2,1,0:T(8,128)(2,1)S(1)}, u32[]{:S(2)}, u32[]{:S(2)}) collective-permute-start(bf16[16,24,256]{2,1,0:T(8,128)(2,1)S(1)} %get-tuple-element.22), channel_id=1, source_target_pairs={{256,0},{384,128},{512,256},{640,384},{768,512},{896,640},{0,768},... | collective-permute-start | bytes 589832 | tf_op jit(solution)/shard_map/ppermute | solution.py:252
  45.5 28.9 %copy-start.1 = (bf16[16,24,256]{2,1,0:T(8,128)(2,1)S(1)}, bf16[16,24,256]{2,1,0:T(8,128)(2,1)}, u32[]{:S(2)}) copy-start(bf16[16,24,256]{2,1,0:T(8,128)(2,1)} %obs_ref.1) | copy-start | bytes 589828

commit v5 on v4

--- a/solution.py
+++ b/solution.py
@@ -15,6 +15,7 @@
 C, M, LAT, LON = 16, 8, 768, 1024
 ROWS, COLS = 24, 256
 CELLS = C * ROWS
+PIECES = 4
 PARTS = 8
 GROUP = 32
 LONG = 1 << 36
@@ -65,15 +66,22 @@
     return (flat >= part * (CELLS // M)) & (flat < (part + 1) * (CELLS // M))
 
 
-def fill_local(scales_ref, x, y, aux_ref):
+def pack_kernel(scales_ref, own_hbm, obs_hbm, pay_ref, aux_ref, own_ref, obs_ref, sems):
+    me = lax.axis_index("y")
+    per = C // PIECES
+    copies = []
+    for i in range(PIECES):
+        part = pl.ds(i * per, per)
+        copies.append(
+            (
+                pltpu.make_async_copy(own_hbm.at[0, part], own_ref.at[part], sems.at[2 * i]),
+                pltpu.make_async_copy(obs_hbm.at[part], obs_ref.at[part], sems.at[2 * i + 1]),
+            )
+        )
+        for copy in copies[-1]:
+            copy.start()
+
     w = tile_weights((ROWS, 128))
-    total = jnp.zeros((ROWS, 128), F32)
-    for c in range(C):
-        d = x[c] - y[c]
-        d = d * d
-        total = total + (d[:, :128] + d[:, 128:]) * inverse_square(scales_ref, c)
-    total = total * w
-    aux_ref[0:8] = (total[0:8] + total[8:16] + total[16:24]) * np.float32(1.0 / (C * LON * SUMW))
     flat = iota((8, 128), 0) * 128 + iota((8, 128), 1)
     channel = lax.shift_right_logical(flat * 2731, 16)
     weight = row_weight(lat_index() * ROWS + flat - channel * ROWS)
@@ -82,20 +90,23 @@
         inv = jnp.where(channel == c, inverse_square(scales_ref, c), inv)
     aux_ref[8:16] = weight * inv * np.float32(1.0 / (C * SUMW * GROUP))
 
-
-def pack_kernel(scales_ref, own_hbm, obs_hbm, pay_ref, aux_ref, own_ref, obs_ref, sems):
-    me = lax.axis_index("y")
-    get_own = pltpu.make_async_copy(own_hbm, own_ref, sems.at[0])
-    get_obs = pltpu.make_async_copy(obs_hbm, obs_ref, sems.at[1])
-    get_own.start()
-    get_obs.start()
-    get_own.wait()
-    x = own_ref[0].astype(F32)
+    total = jnp.zeros((ROWS, 128), F32)
+    for i in range(PIECES):
+        for copy in copies[i]:
+            copy.wait()
+        for c in range(i * per, (i + 1) * per):
+            x = own_ref[c].astype(F32)
+            d = x - obs_ref[c].astype(F32)
+            d = d * d
+            total = total + (d[:, :128] + d[:, 128:]) * inverse_square(scales_ref, c)
+            for h in range(2):
+                pay_ref[2 * c + h, 0:16] = x[0:16, h * 128 : (h + 1) * 128].astype(BF16)
+    total = total * w
+    aux_ref[0:8] = (total[0:8] + total[8:16] + total[16:24]) * np.float32(1.0 / (C * LON * SUMW))
+
+    x = own_ref[...].astype(F32)
     zx = lanes_sum(x)
-    get_obs.wait()
-    y = obs_ref[...].astype(F32)
-    zy = lanes_sum(y)
-    fill_local(scales_ref, x, y, aux_ref)
+    zy = lanes_sum(obs_ref[...].astype(F32))
     row, lane = iota((8, 128), 0), iota((8, 128), 1)
 
     def high(v):
@@ -112,7 +123,8 @@
     extra = jnp.where(row == 7, part - high(part), extra)
     for d in range(GROUP):
         h = d % 2
-        pay_ref[d] = jnp.concatenate([x[d // 2, :, h * 128 : (h + 1) * 128], extra], axis=0).astype(BF16)
+        last = jnp.concatenate([x[d // 2, 16:24, h * 128 : (h + 1) * 128], extra], axis=0)
+        pay_ref[d, 16:32] = last.astype(BF16)
 
 
 def distance_kernel(scales_ref, recv_ref, aux_ref, msg_ref, zall_ref, token_ref, rows_ref):
@@ -173,12 +185,14 @@
     out_ref[...] = jnp.broadcast_to(total[None], out_ref.shape)
 
 
-def stack_kernel(own_ref, up_ref, down_ref, token_ref, ups_ref, downs_ref, again_ref):
-    ups_ref[0] = own_ref[0]
-    ups_ref[1] = up_ref[...]
-    downs_ref[0] = own_ref[0]
-    downs_ref[1] = down_ref[...]
-    again_ref[...] = up_ref[...]
+def stack_kernel(own_ref, up_ref, down_ref, token_ref, ups_ref, downs_ref):
+    half = C // 2
+    ups_ref[0:C] = own_ref[0]
+    ups_ref[C : 2 * C] = down_ref[...]
+    ups_ref[2 * C :] = up_ref[0:half]
+    downs_ref[0:C] = own_ref[0]
+    downs_ref[C : 2 * C] = up_ref[...]
+    downs_ref[2 * C :] = down_ref[half:]
 
 
 def coefficient_kernel(msg_ref, zall_ref, coef_ref, zcol_ref):
@@ -207,21 +221,25 @@
 
 
 def mix_kernel(
-    scales_ref, coef_ref, zcol_ref, obs_ref, own_ref, t2_ref, t4_ref, t6_ref, ups_ref, downs_ref, out_hbm, out_ref, sems
+    scales_ref, coef_ref, zcol_ref, obs_ref, own_ref, up_ref, down_ref, ups_ref, downs_ref, out_hbm, out_ref, sems
 ):
-    tiles = [
-        own_ref.at[0], ups_ref.at[0], t2_ref, ups_ref.at[1], t4_ref, downs_ref.at[1], t6_ref, downs_ref.at[0]
-    ]
+    def tile(k, c):
+        if k == 4:
+            return ups_ref[2 * C + c] if c < C // 2 else downs_ref[2 * C + c - C // 2]
+        return {
+            1: ups_ref, 6: ups_ref, 7: downs_ref, 2: downs_ref, 3: up_ref, 5: down_ref
+        }[k][c + (C if k in (6, 2) else 0)]
+
     fac = tile_weights((ROWS, COLS)) * np.float32(LAT / SUMW)
     coef = coef_ref[...]
     coef = jnp.concatenate([coef, coef], axis=1)
     per = C // PARTS
     copies = []
     for c in range(C):
-        xm = tiles[0][c].astype(F32)
+        xm = own_ref[0, c].astype(F32)
         acc = coef[7:8] * (xm - obs_ref[c].astype(F32))
         for k in range(1, M):
-            acc = acc + coef[k - 1 : k] * (tiles[k][c].astype(F32) - xm)
+            acc = acc + coef[k - 1 : k] * (tile(k, c).astype(F32) - xm)
         z = zcol_ref[c * ROWS : (c + 1) * ROWS]
         acc = acc + jnp.concatenate([z, z], axis=1)
         out_ref[c] = acc * (fac * inverse_square(scales_ref, c))
@@ -263,14 +281,13 @@
         vmem=60,
         out_specs=(VMEM, VMEM),
         scratch_shapes=[
-            pltpu.VMEM((1, C, ROWS, COLS), BF16),
             pltpu.VMEM((C, ROWS, COLS), BF16),
-            pltpu.SemaphoreType.DMA((2,)),
+            pltpu.VMEM((C, ROWS, COLS), BF16),
+            pltpu.SemaphoreType.DMA((2 * PIECES,)),
         ],
     )(scales, members, observed)
-    tiles = [members[0]] + [None] * 7
     recv = lax.all_to_all(pay, ("y", "xl", "core"), 0, 0, tiled=True)
-    tiles[2], tiles[6] = from_ahead(tiles[0], 2), from_ahead(tiles[0], -2)
+    up, down = from_ahead(members[0], 3), from_ahead(members[0], -3)
     msg, zall, token = call(
         distance_kernel,
         (shape((16, 1, 128), F32), shape((16, 8, 128), F32), shape((8, 128), F32)),
@@ -280,13 +297,11 @@
         scratch_shapes=[pltpu.VMEM((128, 128), F32)],
     )(scales, recv, aux)
     msg = lax.all_to_all(msg, ("xh", "xl", "core"), 0, 0, tiled=True)
-    tile = shape((C, ROWS, COLS), BF16)
-    pair = shape((2, C, ROWS, COLS), BF16)
-    ups, downs, again = call(stack_kernel, (pair, pair, tile), [VMEM] * 4, 1 << 22, out_specs=(VMEM,) * 3)(
-        members, tiles[2], tiles[6], token
+    stack = shape((5 * C // 2, ROWS, COLS), BF16)
+    ups, downs = call(stack_kernel, (stack, stack), [VMEM] * 4, 1 << 22, out_specs=(VMEM,) * 2)(
+        members, up, down, token
     )
     ups, downs = from_ahead(ups, 1), from_ahead(downs, -1)
-    tiles[4] = from_ahead(again, 2)
     msg = call(relay_kernel, shape((64, 1, 128), F32), [VMEM], LONG, out_specs=VMEM)(msg)
     msg = lax.all_to_all(msg, ("y", "z"), 0, 0, tiled=True)
     coef, zcol = call(
@@ -299,11 +314,11 @@
     return call(
         mix_kernel,
         shape((1, C, ROWS, COLS), F32),
-        [SMEM] + [VMEM] * 9,
+        [SMEM] + [VMEM] * 8,
         1 << 22,
         out_specs=hbm,
         scratch_shapes=[pltpu.VMEM((C, ROWS, COLS), F32), pltpu.SemaphoreType.DMA((PARTS,))],
-    )(scales, coef, zcol, observed, members, tiles[2], tiles[4], tiles[6], ups, downs)
+    )(scales, coef, zcol, observed, members, up, down, ups, downs)
 
 
 def solution(mesh):

time: 76.7 us -> 77.6 us (1.012)
  the two profiles are of different devices: /device:TPU:4 before, /device:TPU:1 now
where the time goes in v5:
time: 77.6 us; the launch traced here: 76.1 us
  starting transfers between devices  36.4 us (47%)
  blocking collectives  21.7 us (28%)
  waiting for transfers between devices  11.3 us (15%)
  Pallas kernels  6.55 us (8%)
    all_to_all x1, blocking collectives, per_device(): msg = lax.all_to_all(msg, ('y', 'z'), 0, 0, tiled=True)  21.7 us
    all_to_all x1, starting transfers between devices, per_device(): recv = lax.all_to_all(pay, ('y', 'xl', 'core'), 0, 0, tiled=True)  17.8 us
    ppermute x4, starting transfers between devices, from_ahead(): return lax.ppermute(tile, 'y', [((i + k) % M, i) for i in range(M)])  13.6 us
    ppermute x4, waiting for transfers between devices, from_ahead(): return lax.ppermute(tile, 'y', [((i + k) % M, i) for i in range(M)])  8.63 us
    all_to_all x1, starting transfers between devices, per_device(): msg = lax.all_to_all(msg, ('xh', 'xl', 'core'), 0, 0, tiled=True)  4.9 us
    all_to_all x1, waiting for transfers between devices, per_device(): recv = lax.all_to_all(pay, ('y', 'xl', 'core'), 0, 0, tiled=True)  2.68 us
    pallas_call x1, Pallas kernels, per_device(): call(pack_kernel, (shape((GROUP, 32, 128), BF16), shape((16, 128), F32)),...  2.66 us
    pallas_call x1, Pallas kernels, per_device(): call(mix_kernel, shape((1, C, ROWS, COLS), F32), [SMEM] + [VMEM] * 8, 1 <...  1.84 us
  transfers between devices with their start and end apart: 6, of which 3 were waited for; matrix products, arithmetic and copies ran while one was open for 0% of the time, Pallas kernels for 3%

profile of v5, /device:TPU:1, one launch (start us, length us, event | category | flops | bytes accessed | tf_op | source)
XLA Modules:
  0.0 76.1 jit_solution(7827126657657215064)
XLA Ops:
  0.0 2.7 %shard_map.37 = (bf16[32,32,128]{2,1,0:T(8,128)(2,1)}, f32[16,128]{1,0:T(8,128)}) custom-call(f32[16]{0:T(128)} %scales_ref.5, bf16[1,16,24,256]{3,2,1,0:T(8,128)(2,1)} %own_ref.3, bf16[16,24,256]{2,1,0:T(8,128)(2,1)} %obs_ref.1), custom_call_target="tpu_custom_call" | custom-call | flops 1048576 | bytes 1048576 | tf_op jit(solution)/shard_map/pallas_call | solution.py:276
  2.7 0.0 copy-start
  2.7 0.0 copy-start.3
  2.7 17.8 %all-to-all-start = ((bf16[32,32,128]{2,1,0:T(8,128)(2,1)}), bf16[32,32,128]{2,1,0:T(8,128)(2,1)S(1)}, u32[]{:S(2)}, u32[]{:S(2)}) async-start(bf16[32,32,128]{2,1,0:T(8,128)(2,1)} %get-tuple-element.14), calls=%async_computation | async-start | bytes 524288 | tf_op jit(solution)/shard_map/all_to_all | solution.py:289
  20.5 0.0 copy-start.2
  20.5 6.4 %collective-permute-start = (bf16[16,24,256]{2,1,0:T(8,128)(2,1)S(1)}, bf16[16,24,256]{2,1,0:T(8,128)(2,1)S(1)}, u32[]{:S(2)}, u32[]{:S(2)}) collective-permute-start(bf16[16,24,256]{2,1,0:T(8,128)(2,1)S(1)} %bitcast.1), channel_id=1, source_target_pairs={{384,0},{512,128},{640,256},{768,384},{896,512},{0,640},{128,768},... | collective-permute-start | bytes 589832 | tf_op jit(solution)/shard_map/ppermute | solution.py:270
  27.0 1.9 %collective-permute-start.1 = (bf16[16,24,256]{2,1,0:T(8,128)(2,1)S(1)}, bf16[16,24,256]{2,1,0:T(8,128)(2,1)S(1)}, u32[]{:S(2)}, u32[]{:S(2)}) collective-permute-start(bf16[16,24,256]{2,1,0:T(8,128)(2,1)S(1)} %bitcast.2), channel_id=1, source_target_pairs={{640,0},{768,128},{896,256},{0,384},{128,512},{256,640},{384,768},... | collective-permute-start | bytes 589832 | tf_op jit(solution)/shard_map/ppermute | solution.py:270
  28.9 2.7 %all-to-all-done.recv_ref = bf16[32,32,128]{2,1,0:T(8,128)(2,1)S(1)} async-done(((bf16[32,32,128]{2,1,0:T(8,128)(2,1)}), bf16[32,32,128]{2,1,0:T(8,128)(2,1)S(1)}, u32[]{:S(2)}, u32[]{:S(2)}) %all-to-all-start) | async-done | bytes 262176 | tf_op jit(solution)/shard_map/all_to_all | solution.py:289
  31.6 0.0 copy-done.2
  31.6 1.7 %shard_map.38 = (f32[16,1,128]{2,1,0:T(1,128)}, f32[16,8,128]{2,1,0:T(8,128)S(1)}, f32[8,128]{1,0:T(8,128)S(1)}) custom-call(f32[16]{0:T(128)S(1)} %copy-done.2, bf16[32,32,128]{2,1,0:T(8,128)(2,1)S(1)} %all-to-all-done.recv_ref, f32[16,128]{1,0:T(8,128)S(1)} %copy-done.3), custom_call_target="tpu_custom_call" | custom-call | flops 68719476736 | bytes 68719476736 | tf_op jit(solution)/shard_map/pallas_call | solution.py:291
  33.3 4.9 %all-to-all-start.1 = ((f32[16,1,128]{2,1,0:T(1,128)}), f32[16,1,128]{2,1,0:T(1,128)S(1)}, u32[]{:S(2)}, u32[]{:S(2)}) async-start(f32[16,1,128]{2,1,0:T(1,128)} %get-tuple-element.16), calls=%async_computation.1 | async-start | bytes 16384 | tf_op jit(solution)/shard_map/all_to_all | solution.py:299
  38.2 0.8 %collective-permute-done.up_ref = bf16[16,24,256]{2,1,0:T(8,128)(2,1)S(1)} collective-permute-done((bf16[16,24,256]{2,1,0:T(8,128)(2,1)S(1)}, bf16[16,24,256]{2,1,0:T(8,128)(2,1)S(1)}, u32[]{:S(2)}, u32[]{:S(2)}) %collective-permute-start) | collective-permute-done | bytes 196640 | tf_op jit(solution)/shard_map/ppermute | solution.py:270
  39.0 7.8 %collective-permute-done.1.down_ref = bf16[16,24,256]{2,1,0:T(8,128)(2,1)S(1)} collective-permute-done((bf16[16,24,256]{2,1,0:T(8,128)(2,1)S(1)}, bf16[16,24,256]{2,1,0:T(8,128)(2,1)S(1)}, u32[]{:S(2)}, u32[]{:S(2)}) %collective-permute-start.1) | collective-permute-done | bytes 196640 | tf_op jit(solution)/shard_map/ppermute | solution.py:270
  46.8 0.1 shard_map.41
  46.9 1.9 %collective-permute-start.2 = (bf16[40,24,256]{2,1,0:T(8,128)(2,1)S(1)}, bf16[40,24,256]{2,1,0:T(8,128)(2,1)S(1)}, u32[]{:S(2)}, u32[]{:S(2)}) collective-permute-start(bf16[40,24,256]{2,1,0:T(8,128)(2,1)S(1)} %get-tuple-element.21), channel_id=1, source_target_pairs={{128,0},{256,128},{384,256},{512,384},{640,512},{768,640},{896,768... | collective-permute-start | bytes 1474568 | tf_op jit(solution)/shard_map/ppermute | solution.py:270
  48.8 3.4 %collective-permute-start.3 = (bf16[40,24,256]{2,1,0:T(8,128)(2,1)S(1)}, bf16[40,24,256]{2,1,0:T(8,128)(2,1)S(1)}, u32[]{:S(2)}, u32[]{:S(2)}) collective-permute-start(bf16[40,24,256]{2,1,0:T(8,128)(2,1)S(1)} %get-tuple-element.22), channel_id=1, source_target_pairs={{896,0},{0,128},{128,256},{256,384},{384,512},{512,640},{640,768},... | collective-permute-start | bytes 1474568 | tf_op jit(solution)/shard_map/ppermute | solution.py:270
  52.2 0.0 all-to-all-done.1.in_ref
  52.2 0.0 copy-start.1
  52.2 21.7 %all_to_all.15.msg_ref = f32[64,1,128]{2,1,0:T(1,128)S(1)} all-to-all(f32[64,1,128]{2,1,0:T(1,128)S(1)} %shard_map.39), channel_id=1, replica_groups=mesh['y'=8,'z'=8,'xh'=4,'xl'=2,'core'=2] {'y','z'}, dimensions={0} | all-to-all | bytes 65536 | tf_op jit(solution)/shard_map/all_to_all | solution.py:306
  73.9 0.3 shard_map.40
  74.2 0.0 collective-permute-done.2.ups_ref
  74.2 0.0 collective-permute-done.3.downs_ref
  74.2 0.0 copy-done.1
  74.3 1.8 %shard_map.42 = f32[1,16,24,256]{3,2,1,0:T(8,128)} custom-call(f32[16]{0:T(128)S(1)} %copy-done.2, f32[16,128]{1,0:T(8,128)S(1)} %get-tuple-element.18.coef_ref, f32[384,128]{1,0:T(8,128)S(1)} %get-tuple-element.19.zcol_ref, bf16[16,24,256]{2,1,0:T(8,128)(2,1)S(1)} %copy-done.1, bf16[1,16,24,256]{3,2,1,0:T(8,128)(2,1)S(1)} %copy-done, ...), custom_call_target="tpu_custom_call" | custom-call | flops 4194304 | bytes 4194304 | tf_op jit(solution)/shard_map/pallas_call | solution.py:314
  (3 shorter events, 0.0 us)
Async XLA Ops:
  2.7 17.9 %copy-start = (bf16[1,16,24,256]{3,2,1,0:T(8,128)(2,1)S(1)}, bf16[1,16,24,256]{3,2,1,0:T(8,128)(2,1)}, u32[]{:S(2)}) copy-start(bf16[1,16,24,256]{3,2,1,0:T(8,128)(2,1)} %own_ref.3) | copy-start | bytes 589828
  2.7 28.9 %copy-start.3 = (f32[16,128]{1,0:T(8,128)S(1)}, f32[16,128]{1,0:T(8,128)}, u32[]{:S(2)}) copy-start(f32[16,128]{1,0:T(8,128)} %get-tuple-element.15.aux_ref) | copy-start | bytes 24580
  2.7 28.9 %all-to-all-start = ((bf16[32,32,128]{2,1,0:T(8,128)(2,1)}), bf16[32,32,128]{2,1,0:T(8,128)(2,1)S(1)}, u32[]{:S(2)}, u32[]{:S(2)}) async-start(bf16[32,32,128]{2,1,0:T(8,128)(2,1)} %get-tuple-element.14), calls=%async_computation | async-start | bytes 524288 | tf_op jit(solution)/shard_map/all_to_all | solution.py:289
  20.5 11.1 %copy-start.2 = (f32[16]{0:T(128)S(1)}, f32[16]{0:T(128)}, u32[]{:S(2)}) copy-start(f32[16]{0:T(128)} %scales_ref.5) | copy-start | bytes 196
  20.5 18.5 %collective-permute-start = (bf16[16,24,256]{2,1,0:T(8,128)(2,1)S(1)}, bf16[16,24,256]{2,1,0:T(8,128)(2,1)S(1)}, u32[]{:S(2)}, u32[]{:S(2)}) collective-permute-start(bf16[16,24,256]{2,1,0:T(8,128)(2,1)S(1)} %bitcast.1), channel_id=1, source_target_pairs={{384,0},{512,128},{640,256},{768,384},{896,512},{0,640},{128,768},... | collective-permute-start | bytes 589832 | tf_op jit(solution)/shard_map/ppermute | solution.py:270
  27.0 19.8 %collective-permute-start.1 = (bf16[16,24,256]{2,1,0:T(8,128)(2,1)S(1)}, bf16[16,24,256]{2,1,0:T(8,128)(2,1)S(1)}, u32[]{:S(2)}, u32[]{:S(2)}) collective-permute-start(bf16[16,24,256]{2,1,0:T(8,128)(2,1)S(1)} %bitcast.2), channel_id=1, source_target_pairs={{640,0},{768,128},{896,256},{0,384},{128,512},{256,640},{384,768},... | collective-permute-start | bytes 589832 | tf_op jit(solution)/shard_map/ppermute | solution.py:270
  33.3 18.9 %all-to-all-start.1 = ((f32[16,1,128]{2,1,0:T(1,128)}), f32[16,1,128]{2,1,0:T(1,128)S(1)}, u32[]{:S(2)}, u32[]{:S(2)}) async-start(f32[16,1,128]{2,1,0:T(1,128)} %get-tuple-element.16), calls=%async_computation.1 | async-start | bytes 16384 | tf_op jit(solution)/shard_map/all_to_all | solution.py:299
  46.9 27.4 %collective-permute-start.2 = (bf16[40,24,256]{2,1,0:T(8,128)(2,1)S(1)}, bf16[40,24,256]{2,1,0:T(8,128)(2,1)S(1)}, u32[]{:S(2)}, u32[]{:S(2)}) collective-permute-start(bf16[40,24,256]{2,1,0:T(8,128)(2,1)S(1)} %get-tuple-element.21), channel_id=1, source_target_pairs={{128,0},{256,128},{384,256},{512,384},{640,512},{768,640},{896,768... | collective-permute-start | bytes 1474568 | tf_op jit(solution)/shard_map/ppermute | solution.py:270
  48.8 25.5 %collective-permute-start.3 = (bf16[40,24,256]{2,1,0:T(8,128)(2,1)S(1)}, bf16[40,24,256]{2,1,0:T(8,128)(2,1)S(1)}, u32[]{:S(2)}, u32[]{:S(2)}) collective-permute-start(bf16[40,24,256]{2,1,0:T(8,128)(2,1)S(1)} %get-tuple-element.22), channel_id=1, source_target_pairs={{896,0},{0,128},{128,256},{256,384},{384,512},{512,640},{640,768},... | collective-permute-start | bytes 1474568 | tf_op jit(solution)/shard_map/ppermute | solution.py:270
  52.2 22.1 %copy-start.1 = (bf16[16,24,256]{2,1,0:T(8,128)(2,1)S(1)}, bf16[16,24,256]{2,1,0:T(8,128)(2,1)}, u32[]{:S(2)}) copy-start(bf16[16,24,256]{2,1,0:T(8,128)(2,1)} %obs_ref.1) | copy-start | bytes 589828

commit v6 on v5

--- a/solution.py
+++ b/solution.py
@@ -50,9 +50,9 @@
     return row_weight(lat_index() * ROWS + iota(shape, 0))
 
 
-def inverse_square(scales_ref, c):
-    s = scales_ref[c]
-    return 1.0 / (s * s)
+def inverse_square(scales_ref, c, rows=8):
+    s = jnp.full((8, 128), scales_ref[c], F32)
+    return jnp.concatenate([1.0 / (s * s)] * (rows // 8), axis=0)
 
 
 def lanes_sum(x):
@@ -98,7 +98,7 @@
             x = own_ref[c].astype(F32)
             d = x - obs_ref[c].astype(F32)
             d = d * d
-            total = total + (d[:, :128] + d[:, 128:]) * inverse_square(scales_ref, c)
+            total = total + (d[:, :128] + d[:, 128:]) * inverse_square(scales_ref, c, ROWS)
             for h in range(2):
                 pay_ref[2 * c + h, 0:16] = x[0:16, h * 128 : (h + 1) * 128].astype(BF16)
     total = total * w
@@ -130,7 +130,7 @@
 def distance_kernel(scales_ref, recv_ref, aux_ref, msg_ref, zall_ref, token_ref, rows_ref):
     token_ref[...] = jnp.zeros((8, 128), F32)
     me = lax.axis_index("y")
-    inv = inverse_square(scales_ref, me * 2 + lax.axis_index("xl"))
+    inv = inverse_square(scales_ref, me * 2 + lax.axis_index("xl"), ROWS)
     w = tile_weights((ROWS, 128)) * (inv * np.float32(1.0 / (C * LON * SUMW)))
     row, lane = iota((8, 128), 0), iota((8, 128), 1)
     got = [recv_ref[s].astype(F32) for s in range(GROUP)]
@@ -230,7 +230,7 @@
             1: ups_ref, 6: ups_ref, 7: downs_ref, 2: downs_ref, 3: up_ref, 5: down_ref
         }[k][c + (C if k in (6, 2) else 0)]
 
-    fac = tile_weights((ROWS, COLS)) * np.float32(LAT / SUMW)
+    fac = tile_weights((ROWS, 128)) * np.float32(LAT / SUMW)
     coef = coef_ref[...]
     coef = jnp.concatenate([coef, coef], axis=1)
     per = C // PARTS
@@ -242,7 +242,8 @@
             acc = acc + coef[k - 1 : k] * (tile(k, c).astype(F32) - xm)
         z = zcol_ref[c * ROWS : (c + 1) * ROWS]
         acc = acc + jnp.concatenate([z, z], axis=1)
-        out_ref[c] = acc * (fac * inverse_square(scales_ref, c))
+        f = fac * inverse_square(scales_ref, c, ROWS)
+        out_ref[c] = acc * jnp.concatenate([f, f], axis=1)
         if c % per == per - 1:
             part = pl.ds(c + 1 - per, per)
             copies.append(pltpu.make_async_copy(out_ref.at[part], out_hbm.at[0, part], sems.at[c // per]))
@@ -290,20 +291,20 @@
     up, down = from_ahead(members[0], 3), from_ahead(members[0], -3)
     msg, zall, token = call(
         distance_kernel,
-        (shape((16, 1, 128), F32), shape((16, 8, 128), F32), shape((8, 128), F32)),
+        (shape((64, 1, 128), F32), shape((16, 8, 128), F32), shape((8, 128), F32)),
         [SMEM, VMEM, VMEM],
         LONG,
         out_specs=(VMEM, VMEM, VMEM),
         scratch_shapes=[pltpu.VMEM((128, 128), F32)],
     )(scales, recv, aux)
-    msg = lax.all_to_all(msg, ("xh", "xl", "core"), 0, 0, tiled=True)
+    msg = lax.all_to_all(msg, ("y", "z"), 0, 0, tiled=True)
     stack = shape((5 * C // 2, ROWS, COLS), BF16)
     ups, downs = call(stack_kernel, (stack, stack), [VMEM] * 4, 1 << 22, out_specs=(VMEM,) * 2)(
         members, up, down, token
     )
     ups, downs = from_ahead(ups, 1), from_ahead(downs, -1)
-    msg = call(relay_kernel, shape((64, 1, 128), F32), [VMEM], LONG, out_specs=VMEM)(msg)
-    msg = lax.all_to_all(msg, ("y", "z"), 0, 0, tiled=True)
+    msg = call(relay_kernel, shape((16, 1, 128), F32), [VMEM], LONG, out_specs=VMEM)(msg)
+    msg = lax.all_to_all(msg, ("xh", "xl", "core"), 0, 0, tiled=True)
     coef, zcol = call(
         coefficient_kernel,
         (shape((16, 128), F32), shape((CELLS, 128), F32)),

time: 77.6 us -> 73.9 us (0.952); the launches traced: 76.1 us -> 73.4 us
  starting transfers between devices: 36.4 us -> 44.7 us
  blocking collectives: 21.7 us -> 14.4 us
  waiting for transfers between devices: 11.3 us -> 7.68 us
    ppermute x4, waiting for transfers between devices: 8.63 us -> 0.64 us  [from_ahead(): return lax.ppermute(tile, 'y', [((i + k) % M, i) for i in range(M)])]
    all_to_all x1, starting transfers between devices: 4.9 us -> 12.8 us  [per_device(): msg = lax.all_to_all(msg, ('y', 'z'), 0, 0, tiled=True)]
    all_to_all x1, blocking collectives: 21.7 us -> 14.4 us  [per_device(): msg = lax.all_to_all(msg, ('xh', 'xl', 'core'), 0, 0, tiled=True)]
    all_to_all x1, waiting for transfers between devices: 0.01 us -> 4.35 us  [per_device(): msg = lax.all_to_all(msg, ('y', 'z'), 0, 0, tiled=True)]
where the time goes in v6:
time: 73.9 us; the launch traced here: 73.4 us
  starting transfers between devices  44.7 us (60%)
  blocking collectives  14.4 us (19%)
  waiting for transfers between devices  7.68 us (10%)
  Pallas kernels  6.43 us (9%)
    all_to_all x1, starting transfers between devices, per_device(): recv = lax.all_to_all(pay, ('y', 'xl', 'core'), 0, 0, tiled=True)  17.8 us
    all_to_all x1, blocking collectives, per_device(): msg = lax.all_to_all(msg, ('xh', 'xl', 'core'), 0, 0, tiled=True)  14.4 us
    ppermute x4, starting transfers between devices, from_ahead(): return lax.ppermute(tile, 'y', [((i + k) % M, i) for i in range(M)])  14 us
    all_to_all x1, starting transfers between devices, per_device(): msg = lax.all_to_all(msg, ('y', 'z'), 0, 0, tiled=True)  12.8 us
    all_to_all x1, waiting for transfers between devices, per_device(): msg = lax.all_to_all(msg, ('y', 'z'), 0, 0, tiled=True)  4.35 us
    all_to_all x1, waiting for transfers between devices, per_device(): recv = lax.all_to_all(pay, ('y', 'xl', 'core'), 0, 0, tiled=True)  2.68 us
    pallas_call x1, Pallas kernels, per_device(): call(pack_kernel, (shape((GROUP, 32, 128), BF16), shape((16, 128), F32)),...  2.63 us
    pallas_call x1, Pallas kernels, per_device(): call(mix_kernel, shape((1, C, ROWS, COLS), F32), [SMEM] + [VMEM] * 8, 1 <...  1.73 us
  transfers between devices with their start and end apart: 6, of which 3 were waited for; matrix products, arithmetic and copies ran while one was open for 0% of the time, Pallas kernels for 3%

profile of v6, /device:TPU:1, one launch (start us, length us, event | category | flops | bytes accessed | tf_op | source)
XLA Modules:
  0.0 73.4 jit_solution(14429140658583667997)
XLA Ops:
  0.0 2.6 %shard_map.37 = (bf16[32,32,128]{2,1,0:T(8,128)(2,1)}, f32[16,128]{1,0:T(8,128)}) custom-call(f32[16]{0:T(128)} %scales_ref.5, bf16[1,16,24,256]{3,2,1,0:T(8,128)(2,1)} %own_ref.3, bf16[16,24,256]{2,1,0:T(8,128)(2,1)} %obs_ref.1), custom_call_target="tpu_custom_call" | custom-call | flops 1048576 | bytes 1048576 | tf_op jit(solution)/shard_map/pallas_call | solution.py:277
  2.6 0.0 copy-start
  2.7 0.0 copy-start.3
  2.7 17.8 %all-to-all-start = ((bf16[32,32,128]{2,1,0:T(8,128)(2,1)}), bf16[32,32,128]{2,1,0:T(8,128)(2,1)S(1)}, u32[]{:S(2)}, u32[]{:S(2)}) async-start(bf16[32,32,128]{2,1,0:T(8,128)(2,1)} %get-tuple-element.14), calls=%async_computation | async-start | bytes 524288 | tf_op jit(solution)/shard_map/all_to_all | solution.py:290
  20.5 0.0 copy-done
  20.5 0.0 copy-start.2
  20.5 6.4 %collective-permute-start = (bf16[16,24,256]{2,1,0:T(8,128)(2,1)S(1)}, bf16[16,24,256]{2,1,0:T(8,128)(2,1)S(1)}, u32[]{:S(2)}, u32[]{:S(2)}) collective-permute-start(bf16[16,24,256]{2,1,0:T(8,128)(2,1)S(1)} %bitcast.1), channel_id=1, source_target_pairs={{384,0},{512,128},{640,256},{768,384},{896,512},{0,640},{128,768},... | collective-permute-start | bytes 589832 | tf_op jit(solution)/shard_map/ppermute | solution.py:271
  27.0 1.9 %collective-permute-start.1 = (bf16[16,24,256]{2,1,0:T(8,128)(2,1)S(1)}, bf16[16,24,256]{2,1,0:T(8,128)(2,1)S(1)}, u32[]{:S(2)}, u32[]{:S(2)}) collective-permute-start(bf16[16,24,256]{2,1,0:T(8,128)(2,1)S(1)} %bitcast.2), channel_id=1, source_target_pairs={{640,0},{768,128},{896,256},{0,384},{128,512},{256,640},{384,768},... | collective-permute-start | bytes 589832 | tf_op jit(solution)/shard_map/ppermute | solution.py:271
  28.9 2.7 %all-to-all-done.recv_ref = bf16[32,32,128]{2,1,0:T(8,128)(2,1)S(1)} async-done(((bf16[32,32,128]{2,1,0:T(8,128)(2,1)}), bf16[32,32,128]{2,1,0:T(8,128)(2,1)S(1)}, u32[]{:S(2)}, u32[]{:S(2)}) %all-to-all-start) | async-done | bytes 262176 | tf_op jit(solution)/shard_map/all_to_all | solution.py:290
  31.6 0.0 copy-done.3
  31.6 1.7 %shard_map.38 = (f32[64,1,128]{2,1,0:T(1,128)}, f32[16,8,128]{2,1,0:T(8,128)S(1)}, f32[8,128]{1,0:T(8,128)S(1)}) custom-call(f32[16]{0:T(128)S(1)} %copy-done.2, bf16[32,32,128]{2,1,0:T(8,128)(2,1)S(1)} %all-to-all-done.recv_ref, f32[16,128]{1,0:T(8,128)S(1)} %copy-done.3), custom_call_target="tpu_custom_call" | custom-call | flops 68719476736 | bytes 68719476736 | tf_op jit(solution)/shard_map/pallas_call | solution.py:292
  33.3 12.8 %all-to-all-start.1 = ((f32[64,1,128]{2,1,0:T(1,128)}), f32[64,1,128]{2,1,0:T(1,128)S(1)}, u32[]{:S(2)}, u32[]{:S(2)}) async-start(f32[64,1,128]{2,1,0:T(1,128)} %get-tuple-element.16), calls=%async_computation.1 | async-start | bytes 65536 | tf_op jit(solution)/shard_map/all_to_all | solution.py:300
  46.1 0.0 collective-permute-done.up_ref
  46.1 0.6 collective-permute-done.1.down_ref
  46.8 0.1 shard_map.41
  46.8 3.8 %collective-permute-start.2 = (bf16[40,24,256]{2,1,0:T(8,128)(2,1)S(1)}, bf16[40,24,256]{2,1,0:T(8,128)(2,1)S(1)}, u32[]{:S(2)}, u32[]{:S(2)}) collective-permute-start(bf16[40,24,256]{2,1,0:T(8,128)(2,1)S(1)} %get-tuple-element.21), channel_id=1, source_target_pairs={{128,0},{256,128},{384,256},{512,384},{640,512},{768,640},{896,768... | collective-permute-start | bytes 1474568 | tf_op jit(solution)/shard_map/ppermute | solution.py:271
  50.6 1.9 %collective-permute-start.3 = (bf16[40,24,256]{2,1,0:T(8,128)(2,1)S(1)}, bf16[40,24,256]{2,1,0:T(8,128)(2,1)S(1)}, u32[]{:S(2)}, u32[]{:S(2)}) collective-permute-start(bf16[40,24,256]{2,1,0:T(8,128)(2,1)S(1)} %get-tuple-element.22), channel_id=1, source_target_pairs={{896,0},{0,128},{128,256},{256,384},{384,512},{512,640},{640,768},... | collective-permute-start | bytes 1474568 | tf_op jit(solution)/shard_map/ppermute | solution.py:271
  52.5 4.4 %all-to-all-done.1.in_ref = f32[64,1,128]{2,1,0:T(1,128)S(1)} async-done(((f32[64,1,128]{2,1,0:T(1,128)}), f32[64,1,128]{2,1,0:T(1,128)S(1)}, u32[]{:S(2)}, u32[]{:S(2)}) %all-to-all-start.1) | async-done | bytes 32800 | tf_op jit(solution)/shard_map/all_to_all | solution.py:300
  56.9 0.1 shard_map.39
  57.0 14.4 %all_to_all.15.msg_ref = f32[16,1,128]{2,1,0:T(1,128)S(1)} all-to-all(f32[16,1,128]{2,1,0:T(1,128)S(1)} %shard_map.39), channel_id=1, replica_groups=mesh['y'=8,'z'=8,'xh'=4,'xl'=2,'core'=2] {'xh','xl','core'}, dimensions={0} | all-to-all | bytes 16384 | tf_op jit(solution)/shard_map/all_to_all | solution.py:307
  71.4 0.2 shard_map.40
  71.6 0.0 collective-permute-done.2.ups_ref
  71.6 0.0 collective-permute-done.3.downs_ref
  71.7 1.7 %shard_map.42 = f32[1,16,24,256]{3,2,1,0:T(8,128)} custom-call(f32[16]{0:T(128)S(1)} %copy-done.2, f32[16,128]{1,0:T(8,128)S(1)} %get-tuple-element.18.coef_ref, f32[384,128]{1,0:T(8,128)S(1)} %get-tuple-element.19.zcol_ref, bf16[16,24,256]{2,1,0:T(8,128)(2,1)S(1)} %copy-done.1, bf16[1,16,24,256]{3,2,1,0:T(8,128)(2,1)S(1)} %copy-done, ...), custom_call_target="tpu_custom_call" | custom-call | flops 4194304 | bytes 4194304 | tf_op jit(solution)/shard_map/pallas_call | solution.py:315
  (3 shorter events, 0.0 us)
Async XLA Ops:
  2.6 17.9 %copy-start = (bf16[1,16,24,256]{3,2,1,0:T(8,128)(2,1)S(1)}, bf16[1,16,24,256]{3,2,1,0:T(8,128)(2,1)}, u32[]{:S(2)}) copy-start(bf16[1,16,24,256]{3,2,1,0:T(8,128)(2,1)} %own_ref.3) | copy-start | bytes 589828
  2.7 28.9 %copy-start.3 = (f32[16,128]{1,0:T(8,128)S(1)}, f32[16,128]{1,0:T(8,128)}, u32[]{:S(2)}) copy-start(f32[16,128]{1,0:T(8,128)} %get-tuple-element.15.aux_ref) | copy-start | bytes 24580
  2.7 28.9 %all-to-all-start = ((bf16[32,32,128]{2,1,0:T(8,128)(2,1)}), bf16[32,32,128]{2,1,0:T(8,128)(2,1)S(1)}, u32[]{:S(2)}, u32[]{:S(2)}) async-start(bf16[32,32,128]{2,1,0:T(8,128)(2,1)} %get-tuple-element.14), calls=%async_computation | async-start | bytes 524288 | tf_op jit(solution)/shard_map/all_to_all | solution.py:290
  20.5 11.1 %copy-start.2 = (f32[16]{0:T(128)S(1)}, f32[16]{0:T(128)}, u32[]{:S(2)}) copy-start(f32[16]{0:T(128)} %scales_ref.5) | copy-start | bytes 196
  20.5 25.6 %collective-permute-start = (bf16[16,24,256]{2,1,0:T(8,128)(2,1)S(1)}, bf16[16,24,256]{2,1,0:T(8,128)(2,1)S(1)}, u32[]{:S(2)}, u32[]{:S(2)}) collective-permute-start(bf16[16,24,256]{2,1,0:T(8,128)(2,1)S(1)} %bitcast.1), channel_id=1, source_target_pairs={{384,0},{512,128},{640,256},{768,384},{896,512},{0,640},{128,768},... | collective-permute-start | bytes 589832 | tf_op jit(solution)/shard_map/ppermute | solution.py:271
  27.0 19.8 %collective-permute-start.1 = (bf16[16,24,256]{2,1,0:T(8,128)(2,1)S(1)}, bf16[16,24,256]{2,1,0:T(8,128)(2,1)S(1)}, u32[]{:S(2)}, u32[]{:S(2)}) collective-permute-start(bf16[16,24,256]{2,1,0:T(8,128)(2,1)S(1)} %bitcast.2), channel_id=1, source_target_pairs={{640,0},{768,128},{896,256},{0,384},{128,512},{256,640},{384,768},... | collective-permute-start | bytes 589832 | tf_op jit(solution)/shard_map/ppermute | solution.py:271
  33.3 23.6 %all-to-all-start.1 = ((f32[64,1,128]{2,1,0:T(1,128)}), f32[64,1,128]{2,1,0:T(1,128)S(1)}, u32[]{:S(2)}, u32[]{:S(2)}) async-start(f32[64,1,128]{2,1,0:T(1,128)} %get-tuple-element.16), calls=%async_computation.1 | async-start | bytes 65536 | tf_op jit(solution)/shard_map/all_to_all | solution.py:300
  46.8 24.8 %collective-permute-start.2 = (bf16[40,24,256]{2,1,0:T(8,128)(2,1)S(1)}, bf16[40,24,256]{2,1,0:T(8,128)(2,1)S(1)}, u32[]{:S(2)}, u32[]{:S(2)}) collective-permute-start(bf16[40,24,256]{2,1,0:T(8,128)(2,1)S(1)} %get-tuple-element.21), channel_id=1, source_target_pairs={{128,0},{256,128},{384,256},{512,384},{640,512},{768,640},{896,768... | collective-permute-start | bytes 1474568 | tf_op jit(solution)/shard_map/ppermute | solution.py:271
  50.6 21.0 %collective-permute-start.3 = (bf16[40,24,256]{2,1,0:T(8,128)(2,1)S(1)}, bf16[40,24,256]{2,1,0:T(8,128)(2,1)S(1)}, u32[]{:S(2)}, u32[]{:S(2)}) collective-permute-start(bf16[40,24,256]{2,1,0:T(8,128)(2,1)S(1)} %get-tuple-element.22), channel_id=1, source_target_pairs={{896,0},{0,128},{128,256},{256,384},{384,512},{512,640},{640,768},... | collective-permute-start | bytes 1474568 | tf_op jit(solution)/shard_map/ppermute | solution.py:271
  56.9 14.8 %copy-start.1 = (bf16[16,24,256]{2,1,0:T(8,128)(2,1)S(1)}, bf16[16,24,256]{2,1,0:T(8,128)(2,1)}, u32[]{:S(2)}) copy-start(bf16[16,24,256]{2,1,0:T(8,128)(2,1)} %obs_ref.1) | copy-start | bytes 589828

commit v7 on v6

--- a/solution.py
+++ b/solution.py
@@ -15,6 +15,8 @@
 C, M, LAT, LON = 16, 8, 768, 1024
 ROWS, COLS = 24, 256
 CELLS = C * ROWS
+FIRST = 8
+INV = 16
 PIECES = 4
 PARTS = 8
 GROUP = 32
@@ -66,9 +68,11 @@
     return (flat >= part * (CELLS // M)) & (flat < (part + 1) * (CELLS // M))
 
 
-def pack_kernel(scales_ref, own_hbm, obs_hbm, pay_ref, aux_ref, own_ref, obs_ref, sems):
+def pack_kernel(scales_hbm, own_hbm, obs_hbm, pay_ref, aux_ref, scales_ref, own_ref, obs_ref, sems):
     me = lax.axis_index("y")
     per = C // PIECES
+    get_scales = pltpu.make_async_copy(scales_hbm, scales_ref, sems.at[2 * PIECES])
+    get_scales.start()
     copies = []
     for i in range(PIECES):
         part = pl.ds(i * per, per)
@@ -86,8 +90,11 @@
     channel = lax.shift_right_logical(flat * 2731, 16)
     weight = row_weight(lat_index() * ROWS + flat - channel * ROWS)
     inv = jnp.zeros((8, 128), F32)
+    get_scales.wait()
     for c in range(C):
-        inv = jnp.where(channel == c, inverse_square(scales_ref, c), inv)
+        one = inverse_square(scales_ref, c)
+        aux_ref[INV + c : INV + c + 1] = one[0:1]
+        inv = jnp.where(channel == c, one, inv)
     aux_ref[8:16] = weight * inv * np.float32(1.0 / (C * SUMW * GROUP))
 
     total = jnp.zeros((ROWS, 128), F32)
@@ -127,10 +134,10 @@
         pay_ref[d, 16:32] = last.astype(BF16)
 
 
-def distance_kernel(scales_ref, recv_ref, aux_ref, msg_ref, zall_ref, token_ref, rows_ref):
+def distance_kernel(recv_ref, aux_ref, msg_ref, zall_ref, token_ref, rows_ref):
     token_ref[...] = jnp.zeros((8, 128), F32)
     me = lax.axis_index("y")
-    inv = inverse_square(scales_ref, me * 2 + lax.axis_index("xl"), ROWS)
+    inv = aux_ref[pl.ds(INV + me * 2 + lax.axis_index("xl"), 1)]
     w = tile_weights((ROWS, 128)) * (inv * np.float32(1.0 / (C * LON * SUMW)))
     row, lane = iota((8, 128), 0), iota((8, 128), 1)
     got = [recv_ref[s].astype(F32) for s in range(GROUP)]
@@ -186,16 +193,15 @@
 
 
 def stack_kernel(own_ref, up_ref, down_ref, token_ref, ups_ref, downs_ref):
-    half = C // 2
-    ups_ref[0:C] = own_ref[0]
+    ups_ref[0:C] = up_ref[...]
     ups_ref[C : 2 * C] = down_ref[...]
-    ups_ref[2 * C :] = up_ref[0:half]
+    ups_ref[2 * C :] = own_ref[0, 0:FIRST]
     downs_ref[0:C] = own_ref[0]
-    downs_ref[C : 2 * C] = up_ref[...]
-    downs_ref[2 * C :] = down_ref[half:]
-
-
-def coefficient_kernel(msg_ref, zall_ref, coef_ref, zcol_ref):
+    downs_ref[C : 2 * C] = down_ref[...]
+    downs_ref[2 * C :] = up_ref[FIRST:]
+
+
+def coefficient_kernel(msg_ref, zall_ref, obs_ref, own_ref, up_ref, down_ref, coef_ref, begun_ref, zcol_ref):
     me = lax.axis_index("y")
     dist = jnp.sum(msg_ref[...], axis=0)
     row, lane = iota((16, 128), 0), iota((16, 128), 1)
@@ -218,17 +224,21 @@
         z = z + coef[7 + k : 8 + k] * (zall_ref[(me + k) & 7] - zme)
     for b in range(3):
         zcol_ref[b * 128 : (b + 1) * 128] = jnp.broadcast_to(z[b : b + 1], (128, 128)).T
-
-
-def mix_kernel(
-    scales_ref, coef_ref, zcol_ref, obs_ref, own_ref, up_ref, down_ref, ups_ref, downs_ref, out_hbm, out_ref, sems
-):
+    coef = jnp.concatenate([coef, coef], axis=1)
+    for c in range(C):
+        xm = own_ref[0, c].astype(F32)
+        acc = coef[7:8] * (xm - obs_ref[c].astype(F32))
+        acc = acc + coef[1:2] * (up_ref[c].astype(F32) - xm)
+        acc = acc + coef[4:5] * (down_ref[c].astype(F32) - xm)
+        z = zcol_ref[c * ROWS : (c + 1) * ROWS]
+        begun_ref[c] = acc + jnp.concatenate([z, z], axis=1)
+
+
+def mix_kernel(aux_ref, coef_ref, begun_ref, own_ref, ups_ref, downs_ref, out_hbm, out_ref, sems):
     def tile(k, c):
-        if k == 4:
-            return ups_ref[2 * C + c] if c < C // 2 else downs_ref[2 * C + c - C // 2]
-        return {
-            1: ups_ref, 6: ups_ref, 7: downs_ref, 2: downs_ref, 3: up_ref, 5: down_ref
-        }[k][c + (C if k in (6, 2) else 0)]
+        if k == 1:
+            return ups_ref[2 * C + c] if c < FIRST else downs_ref[2 * C + c - FIRST]
+        return {3: ups_ref, 6: ups_ref, 7: downs_ref, 4: downs_ref}[k][c + (C if k in (6, 4) else 0)]
 
     fac = tile_weights((ROWS, 128)) * np.float32(LAT / SUMW)
     coef = coef_ref[...]
@@ -237,12 +247,10 @@
     copies = []
     for c in range(C):
         xm = own_ref[0, c].astype(F32)
-        acc = coef[7:8] * (xm - obs_ref[c].astype(F32))
-        for k in range(1, M):
+        acc = begun_ref[c]
+        for k in (1, 3, 4, 6, 7):
             acc = acc + coef[k - 1 : k] * (tile(k, c).astype(F32) - xm)
-        z = zcol_ref[c * ROWS : (c + 1) * ROWS]
-        acc = acc + jnp.concatenate([z, z], axis=1)
-        f = fac * inverse_square(scales_ref, c, ROWS)
+        f = fac * aux_ref[INV + c : INV + c + 1]
         out_ref[c] = acc * jnp.concatenate([f, f], axis=1)
         if c % per == per - 1:
             part = pl.ds(c + 1 - per, per)
@@ -276,50 +284,52 @@
     hbm = pl.BlockSpec(memory_space=pltpu.HBM)
     pay, aux = call(
         pack_kernel,
-        (shape((GROUP, 32, 128), BF16), shape((16, 128), F32)),
-        [SMEM, hbm, hbm],
+        (shape((GROUP, 32, 128), BF16), shape((INV + C, 128), F32)),
+        [hbm] * 3,
         1 << 20,
         vmem=60,
         out_specs=(VMEM, VMEM),
         scratch_shapes=[
+            pltpu.SMEM((C,), F32),
             pltpu.VMEM((C, ROWS, COLS), BF16),
             pltpu.VMEM((C, ROWS, COLS), BF16),
-            pltpu.SemaphoreType.DMA((2 * PIECES,)),
+            pltpu.SemaphoreType.DMA((2 * PIECES + 1,)),
         ],
     )(scales, members, observed)
     recv = lax.all_to_all(pay, ("y", "xl", "core"), 0, 0, tiled=True)
-    up, down = from_ahead(members[0], 3), from_ahead(members[0], -3)
+    up, down = from_ahead(members[0], 2), from_ahead(members[0], -3)
     msg, zall, token = call(
         distance_kernel,
         (shape((64, 1, 128), F32), shape((16, 8, 128), F32), shape((8, 128), F32)),
-        [SMEM, VMEM, VMEM],
+        [VMEM, VMEM],
         LONG,
         out_specs=(VMEM, VMEM, VMEM),
         scratch_shapes=[pltpu.VMEM((128, 128), F32)],
-    )(scales, recv, aux)
+    )(recv, aux)
     msg = lax.all_to_all(msg, ("y", "z"), 0, 0, tiled=True)
-    stack = shape((5 * C // 2, ROWS, COLS), BF16)
-    ups, downs = call(stack_kernel, (stack, stack), [VMEM] * 4, 1 << 22, out_specs=(VMEM,) * 2)(
+    stacks = tuple(shape((2 * C + n, ROWS, COLS), BF16) for n in (FIRST, C - FIRST))
+    ups, downs = call(stack_kernel, stacks, [VMEM] * 4, 1 << 22, out_specs=(VMEM,) * 2)(
         members, up, down, token
     )
     ups, downs = from_ahead(ups, 1), from_ahead(downs, -1)
     msg = call(relay_kernel, shape((16, 1, 128), F32), [VMEM], LONG, out_specs=VMEM)(msg)
     msg = lax.all_to_all(msg, ("xh", "xl", "core"), 0, 0, tiled=True)
-    coef, zcol = call(
+    coef, begun = call(
         coefficient_kernel,
-        (shape((16, 128), F32), shape((CELLS, 128), F32)),
-        [VMEM] * 2,
+        (shape((16, 128), F32), shape((C, ROWS, COLS), F32)),
+        [VMEM] * 6,
         1 << 16,
         out_specs=(VMEM, VMEM),
-    )(msg, zall)
+        scratch_shapes=[pltpu.VMEM((CELLS, 128), F32)],
+    )(msg, zall, observed, members, up, down)
     return call(
         mix_kernel,
         shape((1, C, ROWS, COLS), F32),
-        [SMEM] + [VMEM] * 8,
+        [VMEM] * 6,
         1 << 22,
         out_specs=hbm,
         scratch_shapes=[pltpu.VMEM((C, ROWS, COLS), F32), pltpu.SemaphoreType.DMA((PARTS,))],
-    )(scales, coef, zcol, observed, members, up, down, ups, downs)
+    )(aux, coef, begun, members, ups, downs)
 
 
 def solution(mesh):

time: 73.9 us -> 72.3 us (0.978)
  Pallas kernels: 6.43 us -> 4.58 us
  blocking collectives: 14.4 us -> 16 us
  waiting for transfers between devices: 7.68 us -> 6.76 us
    all_to_all x1, blocking collectives: 14.4 us -> 16 us  [per_device(): msg = lax.all_to_all(msg, ('xh', 'xl', 'core'), 0, 0, tiled=True)]
    all_to_all x1, starting transfers between devices: 12.8 us -> 11.5 us  [per_device(): msg = lax.all_to_all(msg, ('y', 'z'), 0, 0, tiled=True)]
    pallas_call x4, Pallas kernels: 4.66 us -> 3.35 us  [the longest x1 1.98 us: per_device(): call(pack_kernel, (shape((GROUP, 32, 128), BF16), shape((INV + C, 128), F...]
    ppermute x4, starting transfers between devices: 14 us -> 15 us  [from_ahead(): return lax.ppermute(tile, 'y', [((i + k) % M, i) for i in range(M)])]
  transfers between devices with their start and end apart: 6 -> 6, of which waited for: 3 -> 2; matrix products, arithmetic and copies ran while one was open for 0% -> 0% of each run, Pallas kernels for 3% -> 2%
where the time goes in v7:
time: 72.3 us; the launch traced here: 71.8 us
  starting transfers between devices  44.3 us (61%)
  blocking collectives  16 us (22%)
  waiting for transfers between devices  6.76 us (9%)
  Pallas kernels  4.58 us (6%)
    all_to_all x1, starting transfers between devices, per_device(): recv = lax.all_to_all(pay, ('y', 'xl', 'core'), 0, 0, tiled=True)  17.8 us
    all_to_all x1, blocking collectives, per_device(): msg = lax.all_to_all(msg, ('xh', 'xl', 'core'), 0, 0, tiled=True)  16 us
    ppermute x4, starting transfers between devices, from_ahead(): return lax.ppermute(tile, 'y', [((i + k) % M, i) for i in range(M)])  15 us
    all_to_all x1, starting transfers between devices, per_device(): msg = lax.all_to_all(msg, ('y', 'z'), 0, 0, tiled=True)  11.5 us
    all_to_all x1, waiting for transfers between devices, per_device(): msg = lax.all_to_all(msg, ('y', 'z'), 0, 0, tiled=True)  4.2 us
    all_to_all x1, waiting for transfers between devices, per_device(): recv = lax.all_to_all(pay, ('y', 'xl', 'core'), 0, 0, tiled=True)  2.54 us
    pallas_call x1, Pallas kernels, per_device(): call(pack_kernel, (shape((GROUP, 32, 128), BF16), shape((INV + C, 128), F...  1.98 us
  transfers between devices with their start and end apart: 6, of which 2 were waited for; matrix products, arithmetic and copies ran while one was open for 0% of the time, Pallas kernels for 2%

profile of v7, /device:TPU:1, one launch (start us, length us, event | category | flops | bytes accessed | tf_op | source)
XLA Modules:
  0.0 71.8 jit_solution(18122002450539521935)
XLA Ops:
  0.0 2.0 %shard_map.37 = (bf16[32,32,128]{2,1,0:T(8,128)(2,1)}, f32[32,128]{1,0:T(8,128)}) custom-call(f32[16]{0:T(128)} %scales_hbm.1, bf16[1,16,24,256]{3,2,1,0:T(8,128)(2,1)} %own_ref.5, bf16[16,24,256]{2,1,0:T(8,128)(2,1)} %obs_ref.1), custom_call_target="tpu_custom_call" | custom-call | flops 1048576 | bytes 1048576 | tf_op jit(solution)/shard_map/pallas_call | solution.py:285
  2.0 0.0 copy-start
  2.0 0.0 copy-start.2
  2.0 17.8 %all-to-all-start = ((bf16[32,32,128]{2,1,0:T(8,128)(2,1)}), bf16[32,32,128]{2,1,0:T(8,128)(2,1)S(1)}, u32[]{:S(2)}, u32[]{:S(2)}) async-start(bf16[32,32,128]{2,1,0:T(8,128)(2,1)} %get-tuple-element.15), calls=%async_computation | async-start | bytes 524288 | tf_op jit(solution)/shard_map/all_to_all | solution.py:299
  19.8 0.0 copy-done
  19.9 5.2 %collective-permute-start.1 = (bf16[16,24,256]{2,1,0:T(8,128)(2,1)S(1)}, bf16[16,24,256]{2,1,0:T(8,128)(2,1)S(1)}, u32[]{:S(2)}, u32[]{:S(2)}) collective-permute-start(bf16[16,24,256]{2,1,0:T(8,128)(2,1)S(1)} %bitcast.1), channel_id=1, source_target_pairs={{640,0},{768,128},{896,256},{0,384},{128,512},{256,640},{384,768},... | collective-permute-start | bytes 589832 | tf_op jit(solution)/shard_map/ppermute | solution.py:279
  25.0 3.3 %collective-permute-start = (bf16[16,24,256]{2,1,0:T(8,128)(2,1)S(1)}, bf16[16,24,256]{2,1,0:T(8,128)(2,1)S(1)}, u32[]{:S(2)}, u32[]{:S(2)}) collective-permute-start(bf16[16,24,256]{2,1,0:T(8,128)(2,1)S(1)} %bitcast.2), channel_id=1, source_target_pairs={{256,0},{384,128},{512,256},{640,384},{768,512},{896,640},{0,768},... | collective-permute-start | bytes 589832 | tf_op jit(solution)/shard_map/ppermute | solution.py:279
  28.4 2.5 %all-to-all-done.recv_ref = bf16[32,32,128]{2,1,0:T(8,128)(2,1)S(1)} async-done(((bf16[32,32,128]{2,1,0:T(8,128)(2,1)}), bf16[32,32,128]{2,1,0:T(8,128)(2,1)S(1)}, u32[]{:S(2)}, u32[]{:S(2)}) %all-to-all-start) | async-done | bytes 262176 | tf_op jit(solution)/shard_map/all_to_all | solution.py:299
  30.9 1.2 %shard_map.38 = (f32[64,1,128]{2,1,0:T(1,128)}, f32[16,8,128]{2,1,0:T(8,128)S(1)}, f32[8,128]{1,0:T(8,128)S(1)}) custom-call(bf16[32,32,128]{2,1,0:T(8,128)(2,1)S(1)} %all-to-all-done.recv_ref, f32[32,128]{1,0:T(8,128)S(1)} %copy-done.2), custom_call_target="tpu_custom_call" | custom-call | flops 68719476736 | bytes 68719476736 | tf_op jit(solution)/shard_map/pallas_call | solution.py:301
  32.1 11.5 %all-to-all-start.1 = ((f32[64,1,128]{2,1,0:T(1,128)}), f32[64,1,128]{2,1,0:T(1,128)S(1)}, u32[]{:S(2)}, u32[]{:S(2)}) async-start(f32[64,1,128]{2,1,0:T(1,128)} %get-tuple-element.16), calls=%async_computation.1 | async-start | bytes 65536 | tf_op jit(solution)/shard_map/all_to_all | solution.py:309
  43.6 0.0 collective-permute-done.1.down_ref
  43.6 0.0 collective-permute-done.up_ref
  43.6 0.1 shard_map.41
  43.7 4.4 %collective-permute-start.2 = (bf16[40,24,256]{2,1,0:T(8,128)(2,1)S(1)}, bf16[40,24,256]{2,1,0:T(8,128)(2,1)S(1)}, u32[]{:S(2)}, u32[]{:S(2)}) collective-permute-start(bf16[40,24,256]{2,1,0:T(8,128)(2,1)S(1)} %get-tuple-element.21), channel_id=1, source_target_pairs={{128,0},{256,128},{384,256},{512,384},{640,512},{768,640},{896,768... | collective-permute-start | bytes 1474568 | tf_op jit(solution)/shard_map/ppermute | solution.py:279
  48.1 0.0 copy-start.1
  48.1 2.1 %collective-permute-start.3 = (bf16[40,24,256]{2,1,0:T(8,128)(2,1)S(1)}, bf16[40,24,256]{2,1,0:T(8,128)(2,1)S(1)}, u32[]{:S(2)}, u32[]{:S(2)}) collective-permute-start(bf16[40,24,256]{2,1,0:T(8,128)(2,1)S(1)} %get-tuple-element.22), channel_id=1, source_target_pairs={{896,0},{0,128},{128,256},{256,384},{384,512},{512,640},{640,768},... | collective-permute-start | bytes 1474568 | tf_op jit(solution)/shard_map/ppermute | solution.py:279
  50.2 4.2 %all-to-all-done.1.in_ref = f32[64,1,128]{2,1,0:T(1,128)S(1)} async-done(((f32[64,1,128]{2,1,0:T(1,128)}), f32[64,1,128]{2,1,0:T(1,128)S(1)}, u32[]{:S(2)}, u32[]{:S(2)}) %all-to-all-start.1) | async-done | bytes 32800 | tf_op jit(solution)/shard_map/all_to_all | solution.py:309
  54.4 0.1 shard_map.39
  54.4 16.0 %all_to_all.15.msg_ref = f32[16,1,128]{2,1,0:T(1,128)S(1)} all-to-all(f32[16,1,128]{2,1,0:T(1,128)S(1)} %shard_map.39), channel_id=1, replica_groups=mesh['y'=8,'z'=8,'xh'=4,'xl'=2,'core'=2] {'xh','xl','core'}, dimensions={0} | all-to-all | bytes 16384 | tf_op jit(solution)/shard_map/all_to_all | solution.py:316
  70.5 0.0 copy-done.1
  70.5 0.3 shard_map.40
  70.8 0.0 collective-permute-done.2.ups_ref
  70.8 0.0 collective-permute-done.3.downs_ref
  70.8 1.0 %shard_map.42 = f32[1,16,24,256]{3,2,1,0:T(8,128)} custom-call(f32[32,128]{1,0:T(8,128)S(1)} %copy-done.2, f32[16,128]{1,0:T(8,128)S(1)} %get-tuple-element.18.coef_ref, f32[16,24,256]{2,1,0:T(8,128)S(1)} %get-tuple-element.19.begun_ref, bf16[1,16,24,256]{3,2,1,0:T(8,128)(2,1)S(1)} %copy-done, bf16[40,24,256]{2,1,0:T(8,128)(2,1)S(1)} %collective-permute-done.2.ups_ref, ...), custom_call_target="tpu_custom_call" | custom-call | flops 4194304 | bytes 4194304 | tf_op jit(solution)/shard_map/pallas_call | solution.py:325
  (1 shorter events, 0.0 us)
Async XLA Ops:
  2.0 17.9 %copy-start = (bf16[1,16,24,256]{3,2,1,0:T(8,128)(2,1)S(1)}, bf16[1,16,24,256]{3,2,1,0:T(8,128)(2,1)}, u32[]{:S(2)}) copy-start(bf16[1,16,24,256]{3,2,1,0:T(8,128)(2,1)} %own_ref.5) | copy-start | bytes 589828
  2.0 28.9 %copy-start.2 = (f32[32,128]{1,0:T(8,128)S(1)}, f32[32,128]{1,0:T(8,128)}, u32[]{:S(2)}) copy-start(f32[32,128]{1,0:T(8,128)} %get-tuple-element.14.aux_ref) | copy-start | bytes 49156
  2.0 28.9 %all-to-all-start = ((bf16[32,32,128]{2,1,0:T(8,128)(2,1)}), bf16[32,32,128]{2,1,0:T(8,128)(2,1)S(1)}, u32[]{:S(2)}, u32[]{:S(2)}) async-start(bf16[32,32,128]{2,1,0:T(8,128)(2,1)} %get-tuple-element.15), calls=%async_computation | async-start | bytes 524288 | tf_op jit(solution)/shard_map/all_to_all | solution.py:299
  19.9 23.7 %collective-permute-start.1 = (bf16[16,24,256]{2,1,0:T(8,128)(2,1)S(1)}, bf16[16,24,256]{2,1,0:T(8,128)(2,1)S(1)}, u32[]{:S(2)}, u32[]{:S(2)}) collective-permute-start(bf16[16,24,256]{2,1,0:T(8,128)(2,1)S(1)} %bitcast.1), channel_id=1, source_target_pairs={{640,0},{768,128},{896,256},{0,384},{128,512},{256,640},{384,768},... | collective-permute-start | bytes 589832 | tf_op jit(solution)/shard_map/ppermute | solution.py:279
  25.0 18.6 %collective-permute-start = (bf16[16,24,256]{2,1,0:T(8,128)(2,1)S(1)}, bf16[16,24,256]{2,1,0:T(8,128)(2,1)S(1)}, u32[]{:S(2)}, u32[]{:S(2)}) collective-permute-start(bf16[16,24,256]{2,1,0:T(8,128)(2,1)S(1)} %bitcast.2), channel_id=1, source_target_pairs={{256,0},{384,128},{512,256},{640,384},{768,512},{896,640},{0,768},... | collective-permute-start | bytes 589832 | tf_op jit(solution)/shard_map/ppermute | solution.py:279
  32.1 22.3 %all-to-all-start.1 = ((f32[64,1,128]{2,1,0:T(1,128)}), f32[64,1,128]{2,1,0:T(1,128)S(1)}, u32[]{:S(2)}, u32[]{:S(2)}) async-start(f32[64,1,128]{2,1,0:T(1,128)} %get-tuple-element.16), calls=%async_computation.1 | async-start | bytes 65536 | tf_op jit(solution)/shard_map/all_to_all | solution.py:309
  43.7 27.1 %collective-permute-start.2 = (bf16[40,24,256]{2,1,0:T(8,128)(2,1)S(1)}, bf16[40,24,256]{2,1,0:T(8,128)(2,1)S(1)}, u32[]{:S(2)}, u32[]{:S(2)}) collective-permute-start(bf16[40,24,256]{2,1,0:T(8,128)(2,1)S(1)} %get-tuple-element.21), channel_id=1, source_target_pairs={{128,0},{256,128},{384,256},{512,384},{640,512},{768,640},{896,768... | collective-permute-start | bytes 1474568 | tf_op jit(solution)/shard_map/ppermute | solution.py:279
  48.1 22.4 %copy-start.1 = (bf16[16,24,256]{2,1,0:T(8,128)(2,1)S(1)}, bf16[16,24,256]{2,1,0:T(8,128)(2,1)}, u32[]{:S(2)}) copy-start(bf16[16,24,256]{2,1,0:T(8,128)(2,1)} %obs_ref.1) | copy-start | bytes 589828
  48.1 22.7 %collective-permute-start.3 = (bf16[40,24,256]{2,1,0:T(8,128)(2,1)S(1)}, bf16[40,24,256]{2,1,0:T(8,128)(2,1)S(1)}, u32[]{:S(2)}, u32[]{:S(2)}) collective-permute-start(bf16[40,24,256]{2,1,0:T(8,128)(2,1)S(1)} %get-tuple-element.22), channel_id=1, source_target_pairs={{896,0},{0,128},{128,256},{256,384},{384,512},{512,640},{640,768},... | collective-permute-start | bytes 1474568 | tf_op jit(solution)/shard_map/ppermute | solution.py:279

commit v8 on v7

--- a/solution.py
+++ b/solution.py
@@ -183,8 +183,7 @@
     sums = lax.dot_general(
         ones, rows_ref[...], (((1,), (1,)), ((), ())), precision=HIGHEST, preferred_element_type=F32
     )
-    for i in range(msg_ref.shape[0]):
-        msg_ref[i] = sums[0:1]
+    msg_ref[...] = jnp.broadcast_to(sums[0:1][None], msg_ref.shape)
 
 
 def relay_kernel(in_ref, out_ref):
@@ -201,7 +200,7 @@
     downs_ref[2 * C :] = up_ref[FIRST:]
 
 
-def coefficient_kernel(msg_ref, zall_ref, obs_ref, own_ref, up_ref, down_ref, coef_ref, begun_ref, zcol_ref):
+def coefficient_kernel(msg_ref, zall_ref, obs_ref, own_ref, down_ref, up_ref, coef_ref, begun_ref, zcol_ref):
     me = lax.axis_index("y")
     dist = jnp.sum(msg_ref[...], axis=0)
     row, lane = iota((16, 128), 0), iota((16, 128), 1)
@@ -300,20 +299,20 @@
     up, down = from_ahead(members[0], 2), from_ahead(members[0], -3)
     msg, zall, token = call(
         distance_kernel,
-        (shape((64, 1, 128), F32), shape((16, 8, 128), F32), shape((8, 128), F32)),
+        (shape((128, 1, 128), F32), shape((16, 8, 128), F32), shape((8, 128), F32)),
         [VMEM, VMEM],
         LONG,
         out_specs=(VMEM, VMEM, VMEM),
         scratch_shapes=[pltpu.VMEM((128, 128), F32)],
     )(recv, aux)
-    msg = lax.all_to_all(msg, ("y", "z"), 0, 0, tiled=True)
+    msg = lax.all_to_all(msg, ("y", "xh", "xl", "core"), 0, 0, tiled=True)
     stacks = tuple(shape((2 * C + n, ROWS, COLS), BF16) for n in (FIRST, C - FIRST))
     ups, downs = call(stack_kernel, stacks, [VMEM] * 4, 1 << 22, out_specs=(VMEM,) * 2)(
         members, up, down, token
     )
     ups, downs = from_ahead(ups, 1), from_ahead(downs, -1)
-    msg = call(relay_kernel, shape((16, 1, 128), F32), [VMEM], LONG, out_specs=VMEM)(msg)
-    msg = lax.all_to_all(msg, ("xh", "xl", "core"), 0, 0, tiled=True)
+    msg = call(relay_kernel, shape((8, 1, 128), F32), [VMEM], LONG, out_specs=VMEM)(msg)
+    msg = lax.all_to_all(msg, "z", 0, 0, tiled=True)
     coef, begun = call(
         coefficient_kernel,
         (shape((16, 128), F32), shape((C, ROWS, COLS), F32)),
@@ -321,7 +320,7 @@
         1 << 16,
         out_specs=(VMEM, VMEM),
         scratch_shapes=[pltpu.VMEM((CELLS, 128), F32)],
-    )(msg, zall, observed, members, up, down)
+    )(msg, zall, observed, members, down, up)
     return call(
         mix_kernel,
         shape((1, C, ROWS, COLS), F32),

time: 72.3 us -> 70 us (0.968)
  starting transfers between devices: 44.3 us -> 40 us
  blocking collectives: 16 us -> 17.7 us
    all_to_all x1, starting transfers between devices: 11.5 us -> 6.78 us  [per_device(): msg = lax.all_to_all(msg, ('y', 'xh', 'xl', 'core'), 0, 0, tiled=True)]
    all_to_all x1, waiting for transfers between devices: 4.2 us -> 2.41 us  [per_device(): msg = lax.all_to_all(msg, ('y', 'xh', 'xl', 'core'), 0, 0, tiled=True)]
    all_to_all x1, blocking collectives: 16 us -> 17.7 us  [per_device(): msg = lax.all_to_all(msg, 'z', 0, 0, tiled=True)]
    ppermute x4, waiting for transfers between devices: 0.01 us -> 1.06 us  [from_ahead(): return lax.ppermute(tile, 'y', [((i + k) % M, i) for i in range(M)])]
    all_to_all x1, waiting for transfers between devices: 2.54 us -> 3.57 us  [per_device(): recv = lax.all_to_all(pay, ('y', 'xl', 'core'), 0, 0, tiled=True)]
  transfers between devices with their start and end apart: 6 -> 6, of which waited for: 2 -> 3; matrix products, arithmetic and copies ran while one was open for 0% -> 0% of each run, Pallas kernels for 2% -> 2%
where the time goes in v8:
time: 70 us; the launch traced here: 69.6 us
  starting transfers between devices  40 us (57%)
  blocking collectives  17.7 us (25%)
  waiting for transfers between devices  7.04 us (10%)
  Pallas kernels  4.66 us (7%)
    all_to_all x1, starting transfers between devices, per_device(): recv = lax.all_to_all(pay, ('y', 'xl', 'core'), 0, 0, tiled=True)  17.8 us
    all_to_all x1, blocking collectives, per_device(): msg = lax.all_to_all(msg, 'z', 0, 0, tiled=True)  17.7 us
    ppermute x4, starting transfers between devices, from_ahead(): return lax.ppermute(tile, 'y', [((i + k) % M, i) for i in range(M)])  15.4 us
    all_to_all x1, starting transfers between devices, per_device(): msg = lax.all_to_all(msg, ('y', 'xh', 'xl', 'core'), 0, 0, tiled=True)  6.78 us
    all_to_all x1, waiting for transfers between devices, per_device(): recv = lax.all_to_all(pay, ('y', 'xl', 'core'), 0, 0, tiled=True)  3.57 us
    all_to_all x1, waiting for transfers between devices, per_device(): msg = lax.all_to_all(msg, ('y', 'xh', 'xl', 'core'), 0, 0, tiled=True)  2.41 us
    pallas_call x1, Pallas kernels, per_device(): call(pack_kernel, (shape((GROUP, 32, 128), BF16), shape((INV + C, 128), F...  1.98 us
  transfers between devices with their start and end apart: 6, of which 3 were waited for; matrix products, arithmetic and copies ran while one was open for 0% of the time, Pallas kernels for 2%

profile of v8, /device:TPU:1, one launch (start us, length us, event | category | flops | bytes accessed | tf_op | source)
XLA Modules:
  0.0 69.6 jit_solution(12912305208442235062)
XLA Ops:
  0.0 2.0 %shard_map.37 = (bf16[32,32,128]{2,1,0:T(8,128)(2,1)}, f32[32,128]{1,0:T(8,128)}) custom-call(f32[16]{0:T(128)} %scales_hbm.1, bf16[1,16,24,256]{3,2,1,0:T(8,128)(2,1)} %own_ref.5, bf16[16,24,256]{2,1,0:T(8,128)(2,1)} %obs_ref.1), custom_call_target="tpu_custom_call" | custom-call | flops 1048576 | bytes 1048576 | tf_op jit(solution)/shard_map/pallas_call | solution.py:284
  2.0 0.0 copy-start
  2.0 0.0 copy-start.2
  2.0 17.8 %all-to-all-start = ((bf16[32,32,128]{2,1,0:T(8,128)(2,1)}), bf16[32,32,128]{2,1,0:T(8,128)(2,1)S(1)}, u32[]{:S(2)}, u32[]{:S(2)}) async-start(bf16[32,32,128]{2,1,0:T(8,128)(2,1)} %get-tuple-element.15), calls=%async_computation | async-start | bytes 524288 | tf_op jit(solution)/shard_map/all_to_all | solution.py:298
  19.8 0.0 copy-done
  19.9 5.6 %collective-permute-start.1 = (bf16[16,24,256]{2,1,0:T(8,128)(2,1)S(1)}, bf16[16,24,256]{2,1,0:T(8,128)(2,1)S(1)}, u32[]{:S(2)}, u32[]{:S(2)}) collective-permute-start(bf16[16,24,256]{2,1,0:T(8,128)(2,1)S(1)} %bitcast.1), channel_id=1, source_target_pairs={{256,0},{384,128},{512,256},{640,384},{768,512},{896,640},{0,768},... | collective-permute-start | bytes 589832 | tf_op jit(solution)/shard_map/ppermute | solution.py:278
  25.4 1.9 %collective-permute-start = (bf16[16,24,256]{2,1,0:T(8,128)(2,1)S(1)}, bf16[16,24,256]{2,1,0:T(8,128)(2,1)S(1)}, u32[]{:S(2)}, u32[]{:S(2)}) collective-permute-start(bf16[16,24,256]{2,1,0:T(8,128)(2,1)S(1)} %bitcast.2), channel_id=1, source_target_pairs={{640,0},{768,128},{896,256},{0,384},{128,512},{256,640},{384,768},... | collective-permute-start | bytes 589832 | tf_op jit(solution)/shard_map/ppermute | solution.py:278
  27.3 3.6 %all-to-all-done.recv_ref = bf16[32,32,128]{2,1,0:T(8,128)(2,1)S(1)} async-done(((bf16[32,32,128]{2,1,0:T(8,128)(2,1)}), bf16[32,32,128]{2,1,0:T(8,128)(2,1)S(1)}, u32[]{:S(2)}, u32[]{:S(2)}) %all-to-all-start) | async-done | bytes 262176 | tf_op jit(solution)/shard_map/all_to_all | solution.py:298
  30.9 1.2 %shard_map.38 = (f32[128,1,128]{2,1,0:T(1,128)}, f32[16,8,128]{2,1,0:T(8,128)S(1)}, f32[8,128]{1,0:T(8,128)S(1)}) custom-call(bf16[32,32,128]{2,1,0:T(8,128)(2,1)S(1)} %all-to-all-done.recv_ref, f32[32,128]{1,0:T(8,128)S(1)} %copy-done.2), custom_call_target="tpu_custom_call" | custom-call | flops 68719476736 | bytes 68719476736 | tf_op jit(solution)/shard_map/pallas_call | solution.py:300
  32.1 6.8 %all-to-all-start.1 = ((f32[128,1,128]{2,1,0:T(1,128)}), f32[128,1,128]{2,1,0:T(1,128)S(1)}, u32[]{:S(2)}, u32[]{:S(2)}) async-start(f32[128,1,128]{2,1,0:T(1,128)} %get-tuple-element.16), calls=%async_computation.1 | async-start | bytes 131072 | tf_op jit(solution)/shard_map/all_to_all | solution.py:308
  38.9 0.0 collective-permute-done.1.up_ref
  38.9 1.1 %collective-permute-done.down_ref = bf16[16,24,256]{2,1,0:T(8,128)(2,1)S(1)} collective-permute-done((bf16[16,24,256]{2,1,0:T(8,128)(2,1)S(1)}, bf16[16,24,256]{2,1,0:T(8,128)(2,1)S(1)}, u32[]{:S(2)}, u32[]{:S(2)}) %collective-permute-start) | collective-permute-done | bytes 196640 | tf_op jit(solution)/shard_map/ppermute | solution.py:278
  40.0 0.1 shard_map.41
  40.0 5.7 %collective-permute-start.2 = (bf16[40,24,256]{2,1,0:T(8,128)(2,1)S(1)}, bf16[40,24,256]{2,1,0:T(8,128)(2,1)S(1)}, u32[]{:S(2)}, u32[]{:S(2)}) collective-permute-start(bf16[40,24,256]{2,1,0:T(8,128)(2,1)S(1)} %get-tuple-element.21), channel_id=1, source_target_pairs={{128,0},{256,128},{384,256},{512,384},{640,512},{768,640},{896,768... | collective-permute-start | bytes 1474568 | tf_op jit(solution)/shard_map/ppermute | solution.py:278
  45.8 0.0 copy-start.1
  45.8 2.2 %collective-permute-start.3 = (bf16[40,24,256]{2,1,0:T(8,128)(2,1)S(1)}, bf16[40,24,256]{2,1,0:T(8,128)(2,1)S(1)}, u32[]{:S(2)}, u32[]{:S(2)}) collective-permute-start(bf16[40,24,256]{2,1,0:T(8,128)(2,1)S(1)} %get-tuple-element.22), channel_id=1, source_target_pairs={{896,0},{0,128},{128,256},{256,384},{384,512},{512,640},{640,768},... | collective-permute-start | bytes 1474568 | tf_op jit(solution)/shard_map/ppermute | solution.py:278
  48.0 2.4 %all-to-all-done.1.in_ref = f32[128,1,128]{2,1,0:T(1,128)S(1)} async-done(((f32[128,1,128]{2,1,0:T(1,128)}), f32[128,1,128]{2,1,0:T(1,128)S(1)}, u32[]{:S(2)}, u32[]{:S(2)}) %all-to-all-start.1) | async-done | bytes 65568 | tf_op jit(solution)/shard_map/all_to_all | solution.py:308
  50.4 0.1 shard_map.39
  50.5 17.7 %all_to_all.15.msg_ref = f32[8,1,128]{2,1,0:T(1,128)S(1)} all-to-all(f32[8,1,128]{2,1,0:T(1,128)S(1)} %shard_map.39), channel_id=1, replica_groups=mesh['y'=8,'z'=8,'xh'=4,'xl'=2,'core'=2] {'z'}, dimensions={0} | all-to-all | bytes 8192 | tf_op jit(solution)/shard_map/all_to_all | solution.py:315
  68.3 0.0 copy-done.1
  68.3 0.3 shard_map.40
  68.5 0.0 collective-permute-done.2.ups_ref
  68.5 0.0 collective-permute-done.3.downs_ref
  68.5 1.0 %shard_map.42 = f32[1,16,24,256]{3,2,1,0:T(8,128)} custom-call(f32[32,128]{1,0:T(8,128)S(1)} %copy-done.2, f32[16,128]{1,0:T(8,128)S(1)} %get-tuple-element.18.coef_ref, f32[16,24,256]{2,1,0:T(8,128)S(1)} %get-tuple-element.19.begun_ref, bf16[1,16,24,256]{3,2,1,0:T(8,128)(2,1)S(1)} %copy-done, bf16[40,24,256]{2,1,0:T(8,128)(2,1)S(1)} %collective-permute-done.2.ups_ref, ...), custom_call_target="tpu_custom_call" | custom-call | flops 4194304 | bytes 4194304 | tf_op jit(solution)/shard_map/pallas_call | solution.py:324
  (1 shorter events, 0.0 us)
Async XLA Ops:
  2.0 17.9 %copy-start = (bf16[1,16,24,256]{3,2,1,0:T(8,128)(2,1)S(1)}, bf16[1,16,24,256]{3,2,1,0:T(8,128)(2,1)}, u32[]{:S(2)}) copy-start(bf16[1,16,24,256]{3,2,1,0:T(8,128)(2,1)} %own_ref.5) | copy-start | bytes 589828
  2.0 28.9 %copy-start.2 = (f32[32,128]{1,0:T(8,128)S(1)}, f32[32,128]{1,0:T(8,128)}, u32[]{:S(2)}) copy-start(f32[32,128]{1,0:T(8,128)} %get-tuple-element.14.aux_ref) | copy-start | bytes 49156
  2.0 28.9 %all-to-all-start = ((bf16[32,32,128]{2,1,0:T(8,128)(2,1)}), bf16[32,32,128]{2,1,0:T(8,128)(2,1)S(1)}, u32[]{:S(2)}, u32[]{:S(2)}) async-start(bf16[32,32,128]{2,1,0:T(8,128)(2,1)} %get-tuple-element.15), calls=%async_computation | async-start | bytes 524288 | tf_op jit(solution)/shard_map/all_to_all | solution.py:298
  19.9 19.0 %collective-permute-start.1 = (bf16[16,24,256]{2,1,0:T(8,128)(2,1)S(1)}, bf16[16,24,256]{2,1,0:T(8,128)(2,1)S(1)}, u32[]{:S(2)}, u32[]{:S(2)}) collective-permute-start(bf16[16,24,256]{2,1,0:T(8,128)(2,1)S(1)} %bitcast.1), channel_id=1, source_target_pairs={{256,0},{384,128},{512,256},{640,384},{768,512},{896,640},{0,768},... | collective-permute-start | bytes 589832 | tf_op jit(solution)/shard_map/ppermute | solution.py:278
  25.4 14.5 %collective-permute-start = (bf16[16,24,256]{2,1,0:T(8,128)(2,1)S(1)}, bf16[16,24,256]{2,1,0:T(8,128)(2,1)S(1)}, u32[]{:S(2)}, u32[]{:S(2)}) collective-permute-start(bf16[16,24,256]{2,1,0:T(8,128)(2,1)S(1)} %bitcast.2), channel_id=1, source_target_pairs={{640,0},{768,128},{896,256},{0,384},{128,512},{256,640},{384,768},... | collective-permute-start | bytes 589832 | tf_op jit(solution)/shard_map/ppermute | solution.py:278
  32.1 18.3 %all-to-all-start.1 = ((f32[128,1,128]{2,1,0:T(1,128)}), f32[128,1,128]{2,1,0:T(1,128)S(1)}, u32[]{:S(2)}, u32[]{:S(2)}) async-start(f32[128,1,128]{2,1,0:T(1,128)} %get-tuple-element.16), calls=%async_computation.1 | async-start | bytes 131072 | tf_op jit(solution)/shard_map/all_to_all | solution.py:308
  40.0 28.5 %collective-permute-start.2 = (bf16[40,24,256]{2,1,0:T(8,128)(2,1)S(1)}, bf16[40,24,256]{2,1,0:T(8,128)(2,1)S(1)}, u32[]{:S(2)}, u32[]{:S(2)}) collective-permute-start(bf16[40,24,256]{2,1,0:T(8,128)(2,1)S(1)} %get-tuple-element.21), channel_id=1, source_target_pairs={{128,0},{256,128},{384,256},{512,384},{640,512},{768,640},{896,768... | collective-permute-start | bytes 1474568 | tf_op jit(solution)/shard_map/ppermute | solution.py:278
  45.8 22.5 %copy-start.1 = (bf16[16,24,256]{2,1,0:T(8,128)(2,1)S(1)}, bf16[16,24,256]{2,1,0:T(8,128)(2,1)}, u32[]{:S(2)}) copy-start(bf16[16,24,256]{2,1,0:T(8,128)(2,1)} %obs_ref.1) | copy-start | bytes 589828
  45.8 22.8 %collective-permute-start.3 = (bf16[40,24,256]{2,1,0:T(8,128)(2,1)S(1)}, bf16[40,24,256]{2,1,0:T(8,128)(2,1)S(1)}, u32[]{:S(2)}, u32[]{:S(2)}) collective-permute-start(bf16[40,24,256]{2,1,0:T(8,128)(2,1)S(1)} %get-tuple-element.22), channel_id=1, source_target_pairs={{896,0},{0,128},{128,256},{256,384},{384,512},{512,640},{640,768},... | collective-permute-start | bytes 1474568 | tf_op jit(solution)/shard_map/ppermute | solution.py:278

commit v9 on v8

--- a/solution.py
+++ b/solution.py
@@ -299,20 +299,20 @@
     up, down = from_ahead(members[0], 2), from_ahead(members[0], -3)
     msg, zall, token = call(
         distance_kernel,
-        (shape((128, 1, 128), F32), shape((16, 8, 128), F32), shape((8, 128), F32)),
+        (shape((64, 1, 128), F32), shape((16, 8, 128), F32), shape((8, 128), F32)),
         [VMEM, VMEM],
         LONG,
         out_specs=(VMEM, VMEM, VMEM),
         scratch_shapes=[pltpu.VMEM((128, 128), F32)],
     )(recv, aux)
-    msg = lax.all_to_all(msg, ("y", "xh", "xl", "core"), 0, 0, tiled=True)
+    msg = lax.all_to_all(msg, ("y", "xh", "xl"), 0, 0, tiled=True)
     stacks = tuple(shape((2 * C + n, ROWS, COLS), BF16) for n in (FIRST, C - FIRST))
     ups, downs = call(stack_kernel, stacks, [VMEM] * 4, 1 << 22, out_specs=(VMEM,) * 2)(
         members, up, down, token
     )
     ups, downs = from_ahead(ups, 1), from_ahead(downs, -1)
-    msg = call(relay_kernel, shape((8, 1, 128), F32), [VMEM], LONG, out_specs=VMEM)(msg)
-    msg = lax.all_to_all(msg, "z", 0, 0, tiled=True)
+    msg = call(relay_kernel, shape((16, 1, 128), F32), [VMEM], LONG, out_specs=VMEM)(msg)
+    msg = lax.all_to_all(msg, ("z", "core"), 0, 0, tiled=True)
     coef, begun = call(
         coefficient_kernel,
         (shape((16, 128), F32), shape((C, ROWS, COLS), F32)),

time: 70 us -> 70.9 us (1.013)
  blocking collectives: 17.7 us -> 21.1 us
  starting transfers between devices: 40 us -> 38.4 us
  waiting for transfers between devices: 7.04 us -> 6.32 us
    all_to_all x1, blocking collectives: 17.7 us -> 21.1 us  [per_device(): msg = lax.all_to_all(msg, ('z', 'core'), 0, 0, tiled=True)]
    all_to_all x1, waiting for transfers between devices: 2.41 us -> 0.01 us  [per_device(): msg = lax.all_to_all(msg, ('y', 'xh', 'xl'), 0, 0, tiled=True)]
    ppermute x4, waiting for transfers between devices: 1.06 us -> 2.75 us  [from_ahead(): return lax.ppermute(tile, 'y', [((i + k) % M, i) for i in range(M)])]
    all_to_all x1, starting transfers between devices: 6.78 us -> 5.13 us  [per_device(): msg = lax.all_to_all(msg, ('y', 'xh', 'xl'), 0, 0, tiled=True)]
where the time goes in v9:
time: 70.9 us; the launch traced here: 70.5 us
  starting transfers between devices  38.4 us (54%)
  blocking collectives  21.1 us (30%)
  waiting for transfers between devices  6.32 us (9%)
  Pallas kernels  4.57 us (6%)
    all_to_all x1, blocking collectives, per_device(): msg = lax.all_to_all(msg, ('z', 'core'), 0, 0, tiled=True)  21.1 us
    all_to_all x1, starting transfers between devices, per_device(): recv = lax.all_to_all(pay, ('y', 'xl', 'core'), 0, 0, tiled=True)  17.8 us
    ppermute x4, starting transfers between devices, from_ahead(): return lax.ppermute(tile, 'y', [((i + k) % M, i) for i in range(M)])  15.4 us
    all_to_all x1, starting transfers between devices, per_device(): msg = lax.all_to_all(msg, ('y', 'xh', 'xl'), 0, 0, tiled=True)  5.13 us
    all_to_all x1, waiting for transfers between devices, per_device(): recv = lax.all_to_all(pay, ('y', 'xl', 'core'), 0, 0, tiled=True)  3.57 us
    ppermute x4, waiting for transfers between devices, from_ahead(): return lax.ppermute(tile, 'y', [((i + k) % M, i) for i in range(M)])  2.75 us
    pallas_call x1, Pallas kernels, per_device(): call(pack_kernel, (shape((GROUP, 32, 128), BF16), shape((INV + C, 128), F...  1.98 us
  transfers between devices with their start and end apart: 6, of which 3 were waited for; matrix products, arithmetic and copies ran while one was open for 0% of the time, Pallas kernels for 2%

profile of v9, /device:TPU:1, one launch (start us, length us, event | category | flops | bytes accessed | tf_op | source)
XLA Modules:
  0.0 70.5 jit_solution(6545229142878734281)
XLA Ops:
  0.0 2.0 %shard_map.37 = (bf16[32,32,128]{2,1,0:T(8,128)(2,1)}, f32[32,128]{1,0:T(8,128)}) custom-call(f32[16]{0:T(128)} %scales_hbm.1, bf16[1,16,24,256]{3,2,1,0:T(8,128)(2,1)} %own_ref.5, bf16[16,24,256]{2,1,0:T(8,128)(2,1)} %obs_ref.1), custom_call_target="tpu_custom_call" | custom-call | flops 1048576 | bytes 1048576 | tf_op jit(solution)/shard_map/pallas_call | solution.py:284
  2.0 0.0 copy-start
  2.0 0.0 copy-start.2
  2.0 17.8 %all-to-all-start = ((bf16[32,32,128]{2,1,0:T(8,128)(2,1)}), bf16[32,32,128]{2,1,0:T(8,128)(2,1)S(1)}, u32[]{:S(2)}, u32[]{:S(2)}) async-start(bf16[32,32,128]{2,1,0:T(8,128)(2,1)} %get-tuple-element.15), calls=%async_computation | async-start | bytes 524288 | tf_op jit(solution)/shard_map/all_to_all | solution.py:298
  19.8 0.0 copy-done
  19.9 5.6 %collective-permute-start.1 = (bf16[16,24,256]{2,1,0:T(8,128)(2,1)S(1)}, bf16[16,24,256]{2,1,0:T(8,128)(2,1)S(1)}, u32[]{:S(2)}, u32[]{:S(2)}) collective-permute-start(bf16[16,24,256]{2,1,0:T(8,128)(2,1)S(1)} %bitcast.1), channel_id=1, source_target_pairs={{256,0},{384,128},{512,256},{640,384},{768,512},{896,640},{0,768},... | collective-permute-start | bytes 589832 | tf_op jit(solution)/shard_map/ppermute | solution.py:278
  25.4 1.9 %collective-permute-start = (bf16[16,24,256]{2,1,0:T(8,128)(2,1)S(1)}, bf16[16,24,256]{2,1,0:T(8,128)(2,1)S(1)}, u32[]{:S(2)}, u32[]{:S(2)}) collective-permute-start(bf16[16,24,256]{2,1,0:T(8,128)(2,1)S(1)} %bitcast.2), channel_id=1, source_target_pairs={{640,0},{768,128},{896,256},{0,384},{128,512},{256,640},{384,768},... | collective-permute-start | bytes 589832 | tf_op jit(solution)/shard_map/ppermute | solution.py:278
  27.3 3.6 %all-to-all-done.recv_ref = bf16[32,32,128]{2,1,0:T(8,128)(2,1)S(1)} async-done(((bf16[32,32,128]{2,1,0:T(8,128)(2,1)}), bf16[32,32,128]{2,1,0:T(8,128)(2,1)S(1)}, u32[]{:S(2)}, u32[]{:S(2)}) %all-to-all-start) | async-done | bytes 262176 | tf_op jit(solution)/shard_map/all_to_all | solution.py:298
  30.9 0.0 copy-done.2
  30.9 1.2 %shard_map.38 = (f32[64,1,128]{2,1,0:T(1,128)}, f32[16,8,128]{2,1,0:T(8,128)S(1)}, f32[8,128]{1,0:T(8,128)S(1)}) custom-call(bf16[32,32,128]{2,1,0:T(8,128)(2,1)S(1)} %all-to-all-done.recv_ref, f32[32,128]{1,0:T(8,128)S(1)} %copy-done.2), custom_call_target="tpu_custom_call" | custom-call | flops 68719476736 | bytes 68719476736 | tf_op jit(solution)/shard_map/pallas_call | solution.py:300
  32.1 5.1 %all-to-all-start.1 = ((f32[64,1,128]{2,1,0:T(1,128)}), f32[64,1,128]{2,1,0:T(1,128)S(1)}, u32[]{:S(2)}, u32[]{:S(2)}) async-start(f32[64,1,128]{2,1,0:T(1,128)} %get-tuple-element.16), calls=%async_computation.1 | async-start | bytes 65536 | tf_op jit(solution)/shard_map/all_to_all | solution.py:308
  37.2 0.4 collective-permute-done.1.up_ref
  37.6 2.4 %collective-permute-done.down_ref = bf16[16,24,256]{2,1,0:T(8,128)(2,1)S(1)} collective-permute-done((bf16[16,24,256]{2,1,0:T(8,128)(2,1)S(1)}, bf16[16,24,256]{2,1,0:T(8,128)(2,1)S(1)}, u32[]{:S(2)}, u32[]{:S(2)}) %collective-permute-start) | collective-permute-done | bytes 196640 | tf_op jit(solution)/shard_map/ppermute | solution.py:278
  40.0 0.1 shard_map.41
  40.0 5.7 %collective-permute-start.2 = (bf16[40,24,256]{2,1,0:T(8,128)(2,1)S(1)}, bf16[40,24,256]{2,1,0:T(8,128)(2,1)S(1)}, u32[]{:S(2)}, u32[]{:S(2)}) collective-permute-start(bf16[40,24,256]{2,1,0:T(8,128)(2,1)S(1)} %get-tuple-element.21), channel_id=1, source_target_pairs={{128,0},{256,128},{384,256},{512,384},{640,512},{768,640},{896,768... | collective-permute-start | bytes 1474568 | tf_op jit(solution)/shard_map/ppermute | solution.py:278
  45.8 0.0 copy-start.1
  45.8 2.2 %collective-permute-start.3 = (bf16[40,24,256]{2,1,0:T(8,128)(2,1)S(1)}, bf16[40,24,256]{2,1,0:T(8,128)(2,1)S(1)}, u32[]{:S(2)}, u32[]{:S(2)}) collective-permute-start(bf16[40,24,256]{2,1,0:T(8,128)(2,1)S(1)} %get-tuple-element.22), channel_id=1, source_target_pairs={{896,0},{0,128},{128,256},{256,384},{384,512},{512,640},{640,768},... | collective-permute-start | bytes 1474568 | tf_op jit(solution)/shard_map/ppermute | solution.py:278
  48.0 0.0 all-to-all-done.1.in_ref
  48.0 0.1 shard_map.39
  48.1 21.1 %all_to_all.15.msg_ref = f32[16,1,128]{2,1,0:T(1,128)S(1)} all-to-all(f32[16,1,128]{2,1,0:T(1,128)S(1)} %shard_map.39), channel_id=1, replica_groups=mesh['y'=8,'z'=8,'xh'=4,'xl'=2,'core'=2] {'z','core'}, dimensions={0} | all-to-all | bytes 16384 | tf_op jit(solution)/shard_map/all_to_all | solution.py:315
  69.1 0.3 shard_map.40
  69.4 0.0 collective-permute-done.2.ups_ref
  69.4 0.0 collective-permute-done.3.downs_ref
  69.5 1.0 %shard_map.42 = f32[1,16,24,256]{3,2,1,0:T(8,128)} custom-call(f32[32,128]{1,0:T(8,128)S(1)} %copy-done.2, f32[16,128]{1,0:T(8,128)S(1)} %get-tuple-element.18.coef_ref, f32[16,24,256]{2,1,0:T(8,128)S(1)} %get-tuple-element.19.begun_ref, bf16[1,16,24,256]{3,2,1,0:T(8,128)(2,1)S(1)} %copy-done, bf16[40,24,256]{2,1,0:T(8,128)(2,1)S(1)} %collective-permute-done.2.ups_ref, ...), custom_call_target="tpu_custom_call" | custom-call | flops 4194304 | bytes 4194304 | tf_op jit(solution)/shard_map/pallas_call | solution.py:324
  (1 shorter events, 0.0 us)
Async XLA Ops:
  2.0 17.9 %copy-start = (bf16[1,16,24,256]{3,2,1,0:T(8,128)(2,1)S(1)}, bf16[1,16,24,256]{3,2,1,0:T(8,128)(2,1)}, u32[]{:S(2)}) copy-start(bf16[1,16,24,256]{3,2,1,0:T(8,128)(2,1)} %own_ref.5) | copy-start | bytes 589828
  2.0 28.9 %copy-start.2 = (f32[32,128]{1,0:T(8,128)S(1)}, f32[32,128]{1,0:T(8,128)}, u32[]{:S(2)}) copy-start(f32[32,128]{1,0:T(8,128)} %get-tuple-element.14.aux_ref) | copy-start | bytes 49156
  2.0 28.9 %all-to-all-start = ((bf16[32,32,128]{2,1,0:T(8,128)(2,1)}), bf16[32,32,128]{2,1,0:T(8,128)(2,1)S(1)}, u32[]{:S(2)}, u32[]{:S(2)}) async-start(bf16[32,32,128]{2,1,0:T(8,128)(2,1)} %get-tuple-element.15), calls=%async_computation | async-start | bytes 524288 | tf_op jit(solution)/shard_map/all_to_all | solution.py:298
  19.9 17.7 %collective-permute-start.1 = (bf16[16,24,256]{2,1,0:T(8,128)(2,1)S(1)}, bf16[16,24,256]{2,1,0:T(8,128)(2,1)S(1)}, u32[]{:S(2)}, u32[]{:S(2)}) collective-permute-start(bf16[16,24,256]{2,1,0:T(8,128)(2,1)S(1)} %bitcast.1), channel_id=1, source_target_pairs={{256,0},{384,128},{512,256},{640,384},{768,512},{896,640},{0,768},... | collective-permute-start | bytes 589832 | tf_op jit(solution)/shard_map/ppermute | solution.py:278
  25.4 14.5 %collective-permute-start = (bf16[16,24,256]{2,1,0:T(8,128)(2,1)S(1)}, bf16[16,24,256]{2,1,0:T(8,128)(2,1)S(1)}, u32[]{:S(2)}, u32[]{:S(2)}) collective-permute-start(bf16[16,24,256]{2,1,0:T(8,128)(2,1)S(1)} %bitcast.2), channel_id=1, source_target_pairs={{640,0},{768,128},{896,256},{0,384},{128,512},{256,640},{384,768},... | collective-permute-start | bytes 589832 | tf_op jit(solution)/shard_map/ppermute | solution.py:278
  32.1 15.9 %all-to-all-start.1 = ((f32[64,1,128]{2,1,0:T(1,128)}), f32[64,1,128]{2,1,0:T(1,128)S(1)}, u32[]{:S(2)}, u32[]{:S(2)}) async-start(f32[64,1,128]{2,1,0:T(1,128)} %get-tuple-element.16), calls=%async_computation.1 | async-start | bytes 65536 | tf_op jit(solution)/shard_map/all_to_all | solution.py:308
  40.0 29.4 %collective-permute-start.2 = (bf16[40,24,256]{2,1,0:T(8,128)(2,1)S(1)}, bf16[40,24,256]{2,1,0:T(8,128)(2,1)S(1)}, u32[]{:S(2)}, u32[]{:S(2)}) collective-permute-start(bf16[40,24,256]{2,1,0:T(8,128)(2,1)S(1)} %get-tuple-element.21), channel_id=1, source_target_pairs={{128,0},{256,128},{384,256},{512,384},{640,512},{768,640},{896,768... | collective-permute-start | bytes 1474568 | tf_op jit(solution)/shard_map/ppermute | solution.py:278
  45.8 23.4 %copy-start.1 = (bf16[16,24,256]{2,1,0:T(8,128)(2,1)S(1)}, bf16[16,24,256]{2,1,0:T(8,128)(2,1)}, u32[]{:S(2)}) copy-start(bf16[16,24,256]{2,1,0:T(8,128)(2,1)} %obs_ref.1) | copy-start | bytes 589828
  45.8 23.7 %collective-permute-start.3 = (bf16[40,24,256]{2,1,0:T(8,128)(2,1)S(1)}, bf16[40,24,256]{2,1,0:T(8,128)(2,1)S(1)}, u32[]{:S(2)}, u32[]{:S(2)}) collective-permute-start(bf16[40,24,256]{2,1,0:T(8,128)(2,1)S(1)} %get-tuple-element.22), channel_id=1, source_target_pairs={{896,0},{0,128},{128,256},{256,384},{384,512},{512,640},{640,768},... | collective-permute-start | bytes 1474568 | tf_op jit(solution)/shard_map/ppermute | solution.py:278

commit v10 on v8

--- a/solution.py
+++ b/solution.py
@@ -63,13 +63,7 @@
     return lax.dot_general(ones, flat, (((1,), (1,)), ((), ())), preferred_element_type=F32)
 
 
-def part_of(part, block, lane):
-    flat = block * 128 + lane
-    return (flat >= part * (CELLS // M)) & (flat < (part + 1) * (CELLS // M))
-
-
 def pack_kernel(scales_hbm, own_hbm, obs_hbm, pay_ref, aux_ref, scales_ref, own_ref, obs_ref, sems):
-    me = lax.axis_index("y")
     per = C // PIECES
     get_scales = pltpu.make_async_copy(scales_hbm, scales_ref, sems.at[2 * PIECES])
     get_scales.start()
@@ -112,22 +106,13 @@
     aux_ref[0:8] = (total[0:8] + total[8:16] + total[16:24]) * np.float32(1.0 / (C * LON * SUMW))
 
     x = own_ref[...].astype(F32)
-    zx = lanes_sum(x)
-    zy = lanes_sum(obs_ref[...].astype(F32))
-    row, lane = iota((8, 128), 0), iota((8, 128), 1)
-
-    def high(v):
-        return v.astype(BF16).astype(F32)
-
-    part = jnp.zeros((8, 128), F32)
+    above = lanes_sum(x) - lanes_sum(obs_ref[...].astype(F32))
+    row = iota((8, 128), 0)
     extra = jnp.zeros((8, 128), F32)
     for k in range(3):
-        part = jnp.where(part_of(me, k, lane), zy[:, k * 128 : (k + 1) * 128], part)
-        zk = zx[:, k * 128 : (k + 1) * 128]
-        extra = jnp.where(row == k, high(zk), extra)
-        extra = jnp.where(row == k + 3, zk - high(zk), extra)
-    extra = jnp.where(row == 6, high(part), extra)
-    extra = jnp.where(row == 7, part - high(part), extra)
+        z = above[:, k * 128 : (k + 1) * 128]
+        high = z.astype(BF16).astype(F32)
+        extra = jnp.where(row == k, high, jnp.where(row == k + 3, z - high, extra))
     for d in range(GROUP):
         h = d % 2
         last = jnp.concatenate([x[d // 2, 16:24, h * 128 : (h + 1) * 128], extra], axis=0)
@@ -139,7 +124,7 @@
     me = lax.axis_index("y")
     inv = aux_ref[pl.ds(INV + me * 2 + lax.axis_index("xl"), 1)]
     w = tile_weights((ROWS, 128)) * (inv * np.float32(1.0 / (C * LON * SUMW)))
-    row, lane = iota((8, 128), 0), iota((8, 128), 1)
+    row = iota((8, 128), 0)
     got = [recv_ref[s].astype(F32) for s in range(GROUP)]
     rows_ref[...] = jnp.zeros((128, 128), F32)
     pairs = [(k, m, (m - k) % M) for k in (1, 2, 3, 4) for m in range(M) if k < 4 or m < 4]
@@ -162,23 +147,17 @@
 
     zw = aux_ref[8:16]
     real = row < 3
-    zobs = jnp.zeros((8, 128), F32)
     zonal = []
     for m in range(M):
         s = sum(got[m * 4 + l][24:32] for l in range(4))
         z = jnp.where(real, s + jnp.concatenate([s[3:8], s[0:3]], axis=0), 0.0) * np.float32(1.0 / LON)
         zonal.append(z)
         zall_ref[m] = z
-        part = s[6:7] + s[7:8]
-        zobs = jnp.where(real & part_of(m, row, lane), part, zobs)
-    zobs = zobs * np.float32(1.0 / LON)
-    zall_ref[M] = zobs
     for k, m, n in pairs:
         d = zonal[m] - zonal[n]
         put(40 + (k - 1) * 8 + m, zw * d * d)
     for m in range(M):
-        d = zonal[m] - zobs
-        put(72 + m, zw * d * d)
+        put(72 + m, zw * zonal[m] * zonal[m])
     ones = jnp.ones((8, 128), F32)
     sums = lax.dot_general(
         ones, rows_ref[...], (((1,), (1,)), ((), ())), precision=HIGHEST, preferred_element_type=F32
@@ -218,7 +197,7 @@
     coef = jnp.broadcast_to(picked, (16, 128)) * norm
     coef_ref[...] = coef
     zme = zall_ref[me]
-    z = coef[15:16] * (zme - zall_ref[M])
+    z = coef[15:16] * zme
     for k in range(1, M):
         z = z + coef[7 + k : 8 + k] * (zall_ref[(me + k) & 7] - zme)
     for b in range(3):
@@ -299,7 +278,7 @@
     up, down = from_ahead(members[0], 2), from_ahead(members[0], -3)
     msg, zall, token = call(
         distance_kernel,
-        (shape((128, 1, 128), F32), shape((16, 8, 128), F32), shape((8, 128), F32)),
+        (shape((128, 1, 128), F32), shape((M, 8, 128), F32), shape((8, 128), F32)),
         [VMEM, VMEM],
         LONG,
         out_specs=(VMEM, VMEM, VMEM),

time: 70 us -> 70 us (level)
  no operation moved by 1% of the time
where the time goes in v10:
time: 70 us; the launch traced here: 69.6 us
  starting transfers between devices  40 us (57%)
  blocking collectives  17.7 us (25%)
  waiting for transfers between devices  7.04 us (10%)
  Pallas kernels  4.65 us (7%)
    all_to_all x1, starting transfers between devices, per_device(): recv = lax.all_to_all(pay, ('y', 'xl', 'core'), 0, 0, tiled=True)  17.8 us
    all_to_all x1, blocking collectives, per_device(): msg = lax.all_to_all(msg, 'z', 0, 0, tiled=True)  17.7 us
    ppermute x4, starting transfers between devices, from_ahead(): return lax.ppermute(tile, 'y', [((i + k) % M, i) for i in range(M)])  15.4 us
    all_to_all x1, starting transfers between devices, per_device(): msg = lax.all_to_all(msg, ('y', 'xh', 'xl', 'core'), 0, 0, tiled=True)  6.78 us
    all_to_all x1, waiting for transfers between devices, per_device(): recv = lax.all_to_all(pay, ('y', 'xl', 'core'), 0, 0, tiled=True)  3.57 us
    all_to_all x1, waiting for transfers between devices, per_device(): msg = lax.all_to_all(msg, ('y', 'xh', 'xl', 'core'), 0, 0, tiled=True)  2.4 us
    pallas_call x1, Pallas kernels, per_device(): call(pack_kernel, (shape((GROUP, 32, 128), BF16), shape((INV + C, 128), F...  1.98 us
  transfers between devices with their start and end apart: 6, of which 3 were waited for; matrix products, arithmetic and copies ran while one was open for 0% of the time, Pallas kernels for 2%

profile of v10, /device:TPU:1, one launch (start us, length us, event | category | flops | bytes accessed | tf_op | source)
XLA Modules:
  0.0 69.6 jit_solution(10378539384786843277)
XLA Ops:
  0.0 2.0 %shard_map.37 = (bf16[32,32,128]{2,1,0:T(8,128)(2,1)}, f32[32,128]{1,0:T(8,128)}) custom-call(f32[16]{0:T(128)} %scales_hbm.1, bf16[1,16,24,256]{3,2,1,0:T(8,128)(2,1)} %own_ref.5, bf16[16,24,256]{2,1,0:T(8,128)(2,1)} %obs_ref.1), custom_call_target="tpu_custom_call" | custom-call | flops 1048576 | bytes 1048576 | tf_op jit(solution)/shard_map/pallas_call | solution.py:263
  2.0 0.0 copy-start
  2.0 0.0 copy-start.2
  2.0 17.8 %all-to-all-start = ((bf16[32,32,128]{2,1,0:T(8,128)(2,1)}), bf16[32,32,128]{2,1,0:T(8,128)(2,1)S(1)}, u32[]{:S(2)}, u32[]{:S(2)}) async-start(bf16[32,32,128]{2,1,0:T(8,128)(2,1)} %get-tuple-element.15), calls=%async_computation | async-start | bytes 524288 | tf_op jit(solution)/shard_map/all_to_all | solution.py:277
  19.8 0.0 copy-done
  19.9 5.6 %collective-permute-start.1 = (bf16[16,24,256]{2,1,0:T(8,128)(2,1)S(1)}, bf16[16,24,256]{2,1,0:T(8,128)(2,1)S(1)}, u32[]{:S(2)}, u32[]{:S(2)}) collective-permute-start(bf16[16,24,256]{2,1,0:T(8,128)(2,1)S(1)} %bitcast.1), channel_id=1, source_target_pairs={{256,0},{384,128},{512,256},{640,384},{768,512},{896,640},{0,768},... | collective-permute-start | bytes 589832 | tf_op jit(solution)/shard_map/ppermute | solution.py:257
  25.4 1.9 %collective-permute-start = (bf16[16,24,256]{2,1,0:T(8,128)(2,1)S(1)}, bf16[16,24,256]{2,1,0:T(8,128)(2,1)S(1)}, u32[]{:S(2)}, u32[]{:S(2)}) collective-permute-start(bf16[16,24,256]{2,1,0:T(8,128)(2,1)S(1)} %bitcast.2), channel_id=1, source_target_pairs={{640,0},{768,128},{896,256},{0,384},{128,512},{256,640},{384,768},... | collective-permute-start | bytes 589832 | tf_op jit(solution)/shard_map/ppermute | solution.py:257
  27.3 3.6 %all-to-all-done.recv_ref = bf16[32,32,128]{2,1,0:T(8,128)(2,1)S(1)} async-done(((bf16[32,32,128]{2,1,0:T(8,128)(2,1)}), bf16[32,32,128]{2,1,0:T(8,128)(2,1)S(1)}, u32[]{:S(2)}, u32[]{:S(2)}) %all-to-all-start) | async-done | bytes 262176 | tf_op jit(solution)/shard_map/all_to_all | solution.py:277
  30.9 0.0 copy-done.2
  30.9 1.2 %shard_map.38 = (f32[128,1,128]{2,1,0:T(1,128)}, f32[8,8,128]{2,1,0:T(8,128)S(1)}, f32[8,128]{1,0:T(8,128)S(1)}) custom-call(bf16[32,32,128]{2,1,0:T(8,128)(2,1)S(1)} %all-to-all-done.recv_ref, f32[32,128]{1,0:T(8,128)S(1)} %copy-done.2), custom_call_target="tpu_custom_call" | custom-call | flops 68719476736 | bytes 68719476736 | tf_op jit(solution)/shard_map/pallas_call | solution.py:279
  32.1 6.8 %all-to-all-start.1 = ((f32[128,1,128]{2,1,0:T(1,128)}), f32[128,1,128]{2,1,0:T(1,128)S(1)}, u32[]{:S(2)}, u32[]{:S(2)}) async-start(f32[128,1,128]{2,1,0:T(1,128)} %get-tuple-element.16), calls=%async_computation.1 | async-start | bytes 131072 | tf_op jit(solution)/shard_map/all_to_all | solution.py:287
  38.9 0.0 collective-permute-done.1.up_ref
  38.9 1.1 %collective-permute-done.down_ref = bf16[16,24,256]{2,1,0:T(8,128)(2,1)S(1)} collective-permute-done((bf16[16,24,256]{2,1,0:T(8,128)(2,1)S(1)}, bf16[16,24,256]{2,1,0:T(8,128)(2,1)S(1)}, u32[]{:S(2)}, u32[]{:S(2)}) %collective-permute-start) | collective-permute-done | bytes 196640 | tf_op jit(solution)/shard_map/ppermute | solution.py:257
  40.0 0.1 shard_map.41
  40.0 5.7 %collective-permute-start.2 = (bf16[40,24,256]{2,1,0:T(8,128)(2,1)S(1)}, bf16[40,24,256]{2,1,0:T(8,128)(2,1)S(1)}, u32[]{:S(2)}, u32[]{:S(2)}) collective-permute-start(bf16[40,24,256]{2,1,0:T(8,128)(2,1)S(1)} %get-tuple-element.21), channel_id=1, source_target_pairs={{128,0},{256,128},{384,256},{512,384},{640,512},{768,640},{896,768... | collective-permute-start | bytes 1474568 | tf_op jit(solution)/shard_map/ppermute | solution.py:257
  45.8 0.0 copy-start.1
  45.8 2.2 %collective-permute-start.3 = (bf16[40,24,256]{2,1,0:T(8,128)(2,1)S(1)}, bf16[40,24,256]{2,1,0:T(8,128)(2,1)S(1)}, u32[]{:S(2)}, u32[]{:S(2)}) collective-permute-start(bf16[40,24,256]{2,1,0:T(8,128)(2,1)S(1)} %get-tuple-element.22), channel_id=1, source_target_pairs={{896,0},{0,128},{128,256},{256,384},{384,512},{512,640},{640,768},... | collective-permute-start | bytes 1474568 | tf_op jit(solution)/shard_map/ppermute | solution.py:257
  48.0 2.4 %all-to-all-done.1.in_ref = f32[128,1,128]{2,1,0:T(1,128)S(1)} async-done(((f32[128,1,128]{2,1,0:T(1,128)}), f32[128,1,128]{2,1,0:T(1,128)S(1)}, u32[]{:S(2)}, u32[]{:S(2)}) %all-to-all-start.1) | async-done | bytes 65568 | tf_op jit(solution)/shard_map/all_to_all | solution.py:287
  50.4 0.1 shard_map.39
  50.5 17.7 %all_to_all.15.msg_ref = f32[8,1,128]{2,1,0:T(1,128)S(1)} all-to-all(f32[8,1,128]{2,1,0:T(1,128)S(1)} %shard_map.39), channel_id=1, replica_groups=mesh['y'=8,'z'=8,'xh'=4,'xl'=2,'core'=2] {'z'}, dimensions={0} | all-to-all | bytes 8192 | tf_op jit(solution)/shard_map/all_to_all | solution.py:294
  68.2 0.3 shard_map.40
  68.5 0.0 collective-permute-done.2.ups_ref
  68.5 0.0 collective-permute-done.3.downs_ref
  68.5 1.0 %shard_map.42 = f32[1,16,24,256]{3,2,1,0:T(8,128)} custom-call(f32[32,128]{1,0:T(8,128)S(1)} %copy-done.2, f32[16,128]{1,0:T(8,128)S(1)} %get-tuple-element.18.coef_ref, f32[16,24,256]{2,1,0:T(8,128)S(1)} %get-tuple-element.19.begun_ref, bf16[1,16,24,256]{3,2,1,0:T(8,128)(2,1)S(1)} %copy-done, bf16[40,24,256]{2,1,0:T(8,128)(2,1)S(1)} %collective-permute-done.2.ups_ref, ...), custom_call_target="tpu_custom_call" | custom-call | flops 4194304 | bytes 4194304 | tf_op jit(solution)/shard_map/pallas_call | solution.py:303
  (1 shorter events, 0.0 us)
Async XLA Ops:
  2.0 17.9 %copy-start = (bf16[1,16,24,256]{3,2,1,0:T(8,128)(2,1)S(1)}, bf16[1,16,24,256]{3,2,1,0:T(8,128)(2,1)}, u32[]{:S(2)}) copy-start(bf16[1,16,24,256]{3,2,1,0:T(8,128)(2,1)} %own_ref.5) | copy-start | bytes 589828
  2.0 28.9 %copy-start.2 = (f32[32,128]{1,0:T(8,128)S(1)}, f32[32,128]{1,0:T(8,128)}, u32[]{:S(2)}) copy-start(f32[32,128]{1,0:T(8,128)} %get-tuple-element.14.aux_ref) | copy-start | bytes 49156
  2.0 28.9 %all-to-all-start = ((bf16[32,32,128]{2,1,0:T(8,128)(2,1)}), bf16[32,32,128]{2,1,0:T(8,128)(2,1)S(1)}, u32[]{:S(2)}, u32[]{:S(2)}) async-start(bf16[32,32,128]{2,1,0:T(8,128)(2,1)} %get-tuple-element.15), calls=%async_computation | async-start | bytes 524288 | tf_op jit(solution)/shard_map/all_to_all | solution.py:277
  19.9 19.0 %collective-permute-start.1 = (bf16[16,24,256]{2,1,0:T(8,128)(2,1)S(1)}, bf16[16,24,256]{2,1,0:T(8,128)(2,1)S(1)}, u32[]{:S(2)}, u32[]{:S(2)}) collective-permute-start(bf16[16,24,256]{2,1,0:T(8,128)(2,1)S(1)} %bitcast.1), channel_id=1, source_target_pairs={{256,0},{384,128},{512,256},{640,384},{768,512},{896,640},{0,768},... | collective-permute-start | bytes 589832 | tf_op jit(solution)/shard_map/ppermute | solution.py:257
  25.4 14.5 %collective-permute-start = (bf16[16,24,256]{2,1,0:T(8,128)(2,1)S(1)}, bf16[16,24,256]{2,1,0:T(8,128)(2,1)S(1)}, u32[]{:S(2)}, u32[]{:S(2)}) collective-permute-start(bf16[16,24,256]{2,1,0:T(8,128)(2,1)S(1)} %bitcast.2), channel_id=1, source_target_pairs={{640,0},{768,128},{896,256},{0,384},{128,512},{256,640},{384,768},... | collective-permute-start | bytes 589832 | tf_op jit(solution)/shard_map/ppermute | solution.py:257
  32.1 18.3 %all-to-all-start.1 = ((f32[128,1,128]{2,1,0:T(1,128)}), f32[128,1,128]{2,1,0:T(1,128)S(1)}, u32[]{:S(2)}, u32[]{:S(2)}) async-start(f32[128,1,128]{2,1,0:T(1,128)} %get-tuple-element.16), calls=%async_computation.1 | async-start | bytes 131072 | tf_op jit(solution)/shard_map/all_to_all | solution.py:287
  40.0 28.5 %collective-permute-start.2 = (bf16[40,24,256]{2,1,0:T(8,128)(2,1)S(1)}, bf16[40,24,256]{2,1,0:T(8,128)(2,1)S(1)}, u32[]{:S(2)}, u32[]{:S(2)}) collective-permute-start(bf16[40,24,256]{2,1,0:T(8,128)(2,1)S(1)} %get-tuple-element.21), channel_id=1, source_target_pairs={{128,0},{256,128},{384,256},{512,384},{640,512},{768,640},{896,768... | collective-permute-start | bytes 1474568 | tf_op jit(solution)/shard_map/ppermute | solution.py:257
  45.8 22.5 %copy-start.1 = (bf16[16,24,256]{2,1,0:T(8,128)(2,1)S(1)}, bf16[16,24,256]{2,1,0:T(8,128)(2,1)}, u32[]{:S(2)}) copy-start(bf16[16,24,256]{2,1,0:T(8,128)(2,1)} %obs_ref.1) | copy-start | bytes 589828
  45.8 22.8 %collective-permute-start.3 = (bf16[40,24,256]{2,1,0:T(8,128)(2,1)S(1)}, bf16[40,24,256]{2,1,0:T(8,128)(2,1)S(1)}, u32[]{:S(2)}, u32[]{:S(2)}) collective-permute-start(bf16[40,24,256]{2,1,0:T(8,128)(2,1)S(1)} %get-tuple-element.22), channel_id=1, source_target_pairs={{896,0},{0,128},{128,256},{256,384},{384,512},{512,640},{640,768},... | collective-permute-start | bytes 1474568 | tf_op jit(solution)/shard_map/ppermute | solution.py:257

commit v11 on v10

--- a/solution.py
+++ b/solution.py
@@ -15,7 +15,6 @@
 C, M, LAT, LON = 16, 8, 768, 1024
 ROWS, COLS = 24, 256
 CELLS = C * ROWS
-FIRST = 8
 INV = 16
 PIECES = 4
 PARTS = 8
@@ -170,13 +169,12 @@
     out_ref[...] = jnp.broadcast_to(total[None], out_ref.shape)
 
 
-def stack_kernel(own_ref, up_ref, down_ref, token_ref, ups_ref, downs_ref):
-    ups_ref[0:C] = up_ref[...]
-    ups_ref[C : 2 * C] = down_ref[...]
-    ups_ref[2 * C :] = own_ref[0, 0:FIRST]
+def stack_kernel(own_ref, up_ref, down_ref, token_ref, ups_ref, downs_ref, again_ref):
+    ups_ref[0:C] = own_ref[0]
+    ups_ref[C : 2 * C] = up_ref[...]
     downs_ref[0:C] = own_ref[0]
     downs_ref[C : 2 * C] = down_ref[...]
-    downs_ref[2 * C :] = up_ref[FIRST:]
+    again_ref[...] = up_ref[...]
 
 
 def coefficient_kernel(msg_ref, zall_ref, obs_ref, own_ref, down_ref, up_ref, coef_ref, begun_ref, zcol_ref):
@@ -207,16 +205,14 @@
         xm = own_ref[0, c].astype(F32)
         acc = coef[7:8] * (xm - obs_ref[c].astype(F32))
         acc = acc + coef[1:2] * (up_ref[c].astype(F32) - xm)
-        acc = acc + coef[4:5] * (down_ref[c].astype(F32) - xm)
+        acc = acc + coef[5:6] * (down_ref[c].astype(F32) - xm)
         z = zcol_ref[c * ROWS : (c + 1) * ROWS]
         begun_ref[c] = acc + jnp.concatenate([z, z], axis=1)
 
 
-def mix_kernel(aux_ref, coef_ref, begun_ref, own_ref, ups_ref, downs_ref, out_hbm, out_ref, sems):
+def mix_kernel(aux_ref, coef_ref, begun_ref, own_ref, ups_ref, downs_ref, again_ref, out_hbm, out_ref, sems):
     def tile(k, c):
-        if k == 1:
-            return ups_ref[2 * C + c] if c < FIRST else downs_ref[2 * C + c - FIRST]
-        return {3: ups_ref, 6: ups_ref, 7: downs_ref, 4: downs_ref}[k][c + (C if k in (6, 4) else 0)]
+        return {1: ups_ref, 3: ups_ref, 7: downs_ref, 5: downs_ref, 4: again_ref}[k][c + (C if k in (3, 5) else 0)]
 
     fac = tile_weights((ROWS, 128)) * np.float32(LAT / SUMW)
     coef = coef_ref[...]
@@ -226,7 +222,7 @@
     for c in range(C):
         xm = own_ref[0, c].astype(F32)
         acc = begun_ref[c]
-        for k in (1, 3, 4, 6, 7):
+        for k in (1, 3, 4, 5, 7):
             acc = acc + coef[k - 1 : k] * (tile(k, c).astype(F32) - xm)
         f = fac * aux_ref[INV + c : INV + c + 1]
         out_ref[c] = acc * jnp.concatenate([f, f], axis=1)
@@ -275,7 +271,7 @@
         ],
     )(scales, members, observed)
     recv = lax.all_to_all(pay, ("y", "xl", "core"), 0, 0, tiled=True)
-    up, down = from_ahead(members[0], 2), from_ahead(members[0], -3)
+    up, down = from_ahead(members[0], 2), from_ahead(members[0], -2)
     msg, zall, token = call(
         distance_kernel,
         (shape((128, 1, 128), F32), shape((M, 8, 128), F32), shape((8, 128), F32)),
@@ -285,11 +281,11 @@
         scratch_shapes=[pltpu.VMEM((128, 128), F32)],
     )(recv, aux)
     msg = lax.all_to_all(msg, ("y", "xh", "xl", "core"), 0, 0, tiled=True)
-    stacks = tuple(shape((2 * C + n, ROWS, COLS), BF16) for n in (FIRST, C - FIRST))
-    ups, downs = call(stack_kernel, stacks, [VMEM] * 4, 1 << 22, out_specs=(VMEM,) * 2)(
+    stack, tile = shape((2 * C, ROWS, COLS), BF16), shape((C, ROWS, COLS), BF16)
+    ups, downs, again = call(stack_kernel, (stack, stack, tile), [VMEM] * 4, 1 << 22, out_specs=(VMEM,) * 3)(
         members, up, down, token
     )
-    ups, downs = from_ahead(ups, 1), from_ahead(downs, -1)
+    ups, downs, again = from_ahead(ups, 1), from_ahead(downs, -1), from_ahead(again, 2)
     msg = call(relay_kernel, shape((8, 1, 128), F32), [VMEM], LONG, out_specs=VMEM)(msg)
     msg = lax.all_to_all(msg, "z", 0, 0, tiled=True)
     coef, begun = call(
@@ -303,11 +299,11 @@
     return call(
         mix_kernel,
         shape((1, C, ROWS, COLS), F32),
-        [VMEM] * 6,
+        [VMEM] * 7,
         1 << 22,
         out_specs=hbm,
         scratch_shapes=[pltpu.VMEM((C, ROWS, COLS), F32), pltpu.SemaphoreType.DMA((PARTS,))],
-    )(aux, coef, begun, members, ups, downs)
+    )(aux, coef, begun, members, ups, downs, again)
 
 
 def solution(mesh):

time: 70 us -> 71.3 us (1.019)
  the two profiles are of different devices: /device:TPU:1 before, /device:TPU:2 now
where the time goes in v11:
time: 71.3 us; the launch traced here: 70.8 us
  starting transfers between devices  42.2 us (59%)
  blocking collectives  19.2 us (27%)
  Pallas kernels  4.65 us (7%)
  waiting for transfers between devices  4.6 us (6%)
    ppermute x5, starting transfers between devices, from_ahead(): return lax.ppermute(tile, 'y', [((i + k) % M, i) for i in range(M)])  19.7 us
    all_to_all x1, blocking collectives, per_device(): msg = lax.all_to_all(msg, 'z', 0, 0, tiled=True)  19.2 us
    all_to_all x1, starting transfers between devices, per_device(): recv = lax.all_to_all(pay, ('y', 'xl', 'core'), 0, 0, tiled=True)  16.9 us
    all_to_all x1, starting transfers between devices, per_device(): msg = lax.all_to_all(msg, ('y', 'xh', 'xl', 'core'), 0, 0, tiled=True)  5.68 us
    all_to_all x1, waiting for transfers between devices, per_device(): recv = lax.all_to_all(pay, ('y', 'xl', 'core'), 0, 0, tiled=True)  4.59 us
    pallas_call x1, Pallas kernels, per_device(): call(pack_kernel, (shape((GROUP, 32, 128), BF16), shape((INV + C, 128), F...  1.98 us
  transfers between devices with their start and end apart: 7, of which 1 were waited for; matrix products, arithmetic and copies ran while one was open for 0% of the time, Pallas kernels for 2%

profile of v11, /device:TPU:2, one launch (start us, length us, event | category | flops | bytes accessed | tf_op | source)
XLA Modules:
  0.0 70.8 jit_solution(15182789049719801104)
XLA Ops:
  0.0 2.0 %shard_map.37 = (bf16[32,32,128]{2,1,0:T(8,128)(2,1)}, f32[32,128]{1,0:T(8,128)}) custom-call(f32[16]{0:T(128)} %scales_hbm.1, bf16[1,16,24,256]{3,2,1,0:T(8,128)(2,1)} %own_ref.5, bf16[16,24,256]{2,1,0:T(8,128)(2,1)} %obs_ref.1), custom_call_target="tpu_custom_call" | custom-call | flops 1048576 | bytes 1048576 | tf_op jit(solution)/shard_map/pallas_call | solution.py:259
  2.0 0.0 copy-start
  2.0 0.0 copy-start.2
  2.0 16.9 %all-to-all-start = ((bf16[32,32,128]{2,1,0:T(8,128)(2,1)}), bf16[32,32,128]{2,1,0:T(8,128)(2,1)S(1)}, u32[]{:S(2)}, u32[]{:S(2)}) async-start(bf16[32,32,128]{2,1,0:T(8,128)(2,1)} %get-tuple-element.16), calls=%async_computation | async-start | bytes 524288 | tf_op jit(solution)/shard_map/all_to_all | solution.py:273
  18.9 5.6 %collective-permute-start.1 = (bf16[16,24,256]{2,1,0:T(8,128)(2,1)S(1)}, bf16[16,24,256]{2,1,0:T(8,128)(2,1)S(1)}, u32[]{:S(2)}, u32[]{:S(2)}) collective-permute-start(bf16[16,24,256]{2,1,0:T(8,128)(2,1)S(1)} %bitcast.1), channel_id=1, source_target_pairs={{256,0},{384,128},{512,256},{640,384},{768,512},{896,640},{0,768},... | collective-permute-start | bytes 589832 | tf_op jit(solution)/shard_map/ppermute | solution.py:253
  24.5 1.9 %collective-permute-start = (bf16[16,24,256]{2,1,0:T(8,128)(2,1)S(1)}, bf16[16,24,256]{2,1,0:T(8,128)(2,1)S(1)}, u32[]{:S(2)}, u32[]{:S(2)}) collective-permute-start(bf16[16,24,256]{2,1,0:T(8,128)(2,1)S(1)} %bitcast.2), channel_id=1, source_target_pairs={{768,0},{896,128},{0,256},{128,384},{256,512},{384,640},{512,768},... | collective-permute-start | bytes 589832 | tf_op jit(solution)/shard_map/ppermute | solution.py:253
  26.5 4.6 %all-to-all-done.recv_ref = bf16[32,32,128]{2,1,0:T(8,128)(2,1)S(1)} async-done(((bf16[32,32,128]{2,1,0:T(8,128)(2,1)}), bf16[32,32,128]{2,1,0:T(8,128)(2,1)S(1)}, u32[]{:S(2)}, u32[]{:S(2)}) %all-to-all-start) | async-done | bytes 262176 | tf_op jit(solution)/shard_map/all_to_all | solution.py:273
  31.1 1.2 %shard_map.38 = (f32[128,1,128]{2,1,0:T(1,128)}, f32[8,8,128]{2,1,0:T(8,128)S(1)}, f32[8,128]{1,0:T(8,128)S(1)}) custom-call(bf16[32,32,128]{2,1,0:T(8,128)(2,1)S(1)} %all-to-all-done.recv_ref, f32[32,128]{1,0:T(8,128)S(1)} %copy-done.2), custom_call_target="tpu_custom_call" | custom-call | flops 68719476736 | bytes 68719476736 | tf_op jit(solution)/shard_map/pallas_call | solution.py:275
  32.2 5.7 %all-to-all-start.1 = ((f32[128,1,128]{2,1,0:T(1,128)}), f32[128,1,128]{2,1,0:T(1,128)S(1)}, u32[]{:S(2)}, u32[]{:S(2)}) async-start(f32[128,1,128]{2,1,0:T(1,128)} %get-tuple-element.17), calls=%async_computation.1 | async-start | bytes 131072 | tf_op jit(solution)/shard_map/all_to_all | solution.py:283
  37.9 0.0 collective-permute-done.1.up_ref
  37.9 0.0 collective-permute-done.down_ref
  37.9 0.1 shard_map.41
  38.0 6.1 %collective-permute-start.4 = (bf16[16,24,256]{2,1,0:T(8,128)(2,1)S(1)}, bf16[16,24,256]{2,1,0:T(8,128)(2,1)S(1)}, u32[]{:S(2)}, u32[]{:S(2)}) collective-permute-start(bf16[16,24,256]{2,1,0:T(8,128)(2,1)S(1)} %get-tuple-element.24), channel_id=1, source_target_pairs={{256,0},{384,128},{512,256},{640,384},{768,512},{896,640},{0,768},... | collective-permute-start | bytes 589832 | tf_op jit(solution)/shard_map/ppermute | solution.py:253
  44.2 3.3 %collective-permute-start.2 = (bf16[32,24,256]{2,1,0:T(8,128)(2,1)S(1)}, bf16[32,24,256]{2,1,0:T(8,128)(2,1)S(1)}, u32[]{:S(2)}, u32[]{:S(2)}) collective-permute-start(bf16[32,24,256]{2,1,0:T(8,128)(2,1)S(1)} %get-tuple-element.22), channel_id=1, source_target_pairs={{128,0},{256,128},{384,256},{512,384},{640,512},{768,640},{896,768... | collective-permute-start | bytes 1179656 | tf_op jit(solution)/shard_map/ppermute | solution.py:253
  47.4 0.0 copy-start.1
  47.4 2.7 %collective-permute-start.3 = (bf16[32,24,256]{2,1,0:T(8,128)(2,1)S(1)}, bf16[32,24,256]{2,1,0:T(8,128)(2,1)S(1)}, u32[]{:S(2)}, u32[]{:S(2)}) collective-permute-start(bf16[32,24,256]{2,1,0:T(8,128)(2,1)S(1)} %get-tuple-element.23), channel_id=1, source_target_pairs={{896,0},{0,128},{128,256},{256,384},{384,512},{512,640},{640,768},... | collective-permute-start | bytes 1179656 | tf_op jit(solution)/shard_map/ppermute | solution.py:253
  50.2 0.0 all-to-all-done.1.in_ref
  50.2 0.1 shard_map.39
  50.3 19.2 %all_to_all.15.msg_ref = f32[8,1,128]{2,1,0:T(1,128)S(1)} all-to-all(f32[8,1,128]{2,1,0:T(1,128)S(1)} %shard_map.39), channel_id=1, replica_groups=mesh['y'=8,'z'=8,'xh'=4,'xl'=2,'core'=2] {'z'}, dimensions={0} | all-to-all | bytes 8192 | tf_op jit(solution)/shard_map/all_to_all | solution.py:290
  69.5 0.3 shard_map.40
  69.7 0.0 collective-permute-done.4.again_ref
  69.8 0.0 collective-permute-done.2.ups_ref
  69.8 0.0 collective-permute-done.3.downs_ref
  69.8 1.0 %shard_map.42 = f32[1,16,24,256]{3,2,1,0:T(8,128)} custom-call(f32[32,128]{1,0:T(8,128)S(1)} %copy-done.2, f32[16,128]{1,0:T(8,128)S(1)} %get-tuple-element.19.coef_ref, f32[16,24,256]{2,1,0:T(8,128)S(1)} %get-tuple-element.20.begun_ref, bf16[1,16,24,256]{3,2,1,0:T(8,128)(2,1)S(1)} %copy-done, bf16[32,24,256]{2,1,0:T(8,128)(2,1)S(1)} %collective-permute-done.2.ups_ref, ...), custom_call_target="tpu_custom_call" | custom-call | flops 4194304 | bytes 4194304 | tf_op jit(solution)/shard_map/pallas_call | solution.py:299
  (3 shorter events, 0.0 us)
Async XLA Ops:
  2.0 16.9 %copy-start = (bf16[1,16,24,256]{3,2,1,0:T(8,128)(2,1)S(1)}, bf16[1,16,24,256]{3,2,1,0:T(8,128)(2,1)}, u32[]{:S(2)}) copy-start(bf16[1,16,24,256]{3,2,1,0:T(8,128)(2,1)} %own_ref.5) | copy-start | bytes 589828
  2.0 29.1 %copy-start.2 = (f32[32,128]{1,0:T(8,128)S(1)}, f32[32,128]{1,0:T(8,128)}, u32[]{:S(2)}) copy-start(f32[32,128]{1,0:T(8,128)} %get-tuple-element.15.aux_ref) | copy-start | bytes 49156
  2.0 29.0 %all-to-all-start = ((bf16[32,32,128]{2,1,0:T(8,128)(2,1)}), bf16[32,32,128]{2,1,0:T(8,128)(2,1)S(1)}, u32[]{:S(2)}, u32[]{:S(2)}) async-start(bf16[32,32,128]{2,1,0:T(8,128)(2,1)} %get-tuple-element.16), calls=%async_computation | async-start | bytes 524288 | tf_op jit(solution)/shard_map/all_to_all | solution.py:273
  18.9 19.0 %collective-permute-start.1 = (bf16[16,24,256]{2,1,0:T(8,128)(2,1)S(1)}, bf16[16,24,256]{2,1,0:T(8,128)(2,1)S(1)}, u32[]{:S(2)}, u32[]{:S(2)}) collective-permute-start(bf16[16,24,256]{2,1,0:T(8,128)(2,1)S(1)} %bitcast.1), channel_id=1, source_target_pairs={{256,0},{384,128},{512,256},{640,384},{768,512},{896,640},{0,768},... | collective-permute-start | bytes 589832 | tf_op jit(solution)/shard_map/ppermute | solution.py:253
  24.5 13.4 %collective-permute-start = (bf16[16,24,256]{2,1,0:T(8,128)(2,1)S(1)}, bf16[16,24,256]{2,1,0:T(8,128)(2,1)S(1)}, u32[]{:S(2)}, u32[]{:S(2)}) collective-permute-start(bf16[16,24,256]{2,1,0:T(8,128)(2,1)S(1)} %bitcast.2), channel_id=1, source_target_pairs={{768,0},{896,128},{0,256},{128,384},{256,512},{384,640},{512,768},... | collective-permute-start | bytes 589832 | tf_op jit(solution)/shard_map/ppermute | solution.py:253
  32.2 17.9 %all-to-all-start.1 = ((f32[128,1,128]{2,1,0:T(1,128)}), f32[128,1,128]{2,1,0:T(1,128)S(1)}, u32[]{:S(2)}, u32[]{:S(2)}) async-start(f32[128,1,128]{2,1,0:T(1,128)} %get-tuple-element.17), calls=%async_computation.1 | async-start | bytes 131072 | tf_op jit(solution)/shard_map/all_to_all | solution.py:283
  38.0 31.7 %collective-permute-start.4 = (bf16[16,24,256]{2,1,0:T(8,128)(2,1)S(1)}, bf16[16,24,256]{2,1,0:T(8,128)(2,1)S(1)}, u32[]{:S(2)}, u32[]{:S(2)}) collective-permute-start(bf16[16,24,256]{2,1,0:T(8,128)(2,1)S(1)} %get-tuple-element.24), channel_id=1, source_target_pairs={{256,0},{384,128},{512,256},{640,384},{768,512},{896,640},{0,768},... | collective-permute-start | bytes 589832 | tf_op jit(solution)/shard_map/ppermute | solution.py:253
  44.2 25.6 %collective-permute-start.2 = (bf16[32,24,256]{2,1,0:T(8,128)(2,1)S(1)}, bf16[32,24,256]{2,1,0:T(8,128)(2,1)S(1)}, u32[]{:S(2)}, u32[]{:S(2)}) collective-permute-start(bf16[32,24,256]{2,1,0:T(8,128)(2,1)S(1)} %get-tuple-element.22), channel_id=1, source_target_pairs={{128,0},{256,128},{384,256},{512,384},{640,512},{768,640},{896,768... | collective-permute-start | bytes 1179656 | tf_op jit(solution)/shard_map/ppermute | solution.py:253
  47.4 22.0 %copy-start.1 = (bf16[16,24,256]{2,1,0:T(8,128)(2,1)S(1)}, bf16[16,24,256]{2,1,0:T(8,128)(2,1)}, u32[]{:S(2)}) copy-start(bf16[16,24,256]{2,1,0:T(8,128)(2,1)} %obs_ref.1) | copy-start | bytes 589828
  47.4 22.3 %collective-permute-start.3 = (bf16[32,24,256]{2,1,0:T(8,128)(2,1)S(1)}, bf16[32,24,256]{2,1,0:T(8,128)(2,1)S(1)}, u32[]{:S(2)}, u32[]{:S(2)}) collective-permute-start(bf16[32,24,256]{2,1,0:T(8,128)(2,1)S(1)} %get-tuple-element.23), channel_id=1, source_target_pairs={{896,0},{0,128},{128,256},{256,384},{384,512},{512,640},{640,768},... | collective-permute-start | bytes 1179656 | tf_op jit(solution)/shard_map/ppermute | solution.py:253

commit v12 on v10

--- a/solution.py
+++ b/solution.py
@@ -18,7 +18,7 @@
 FIRST = 8
 INV = 16
 PIECES = 4
-PARTS = 8
+PARTS = 16
 GROUP = 32
 LONG = 1 << 36
 HIGHEST = lax.Precision.HIGHEST

time: 70 us -> 70.1 us (level)
  no operation moved by 1% of the time
where the time goes in v12:
time: 70.1 us; the launch traced here: 69.6 us
  starting transfers between devices  40 us (57%)
  blocking collectives  17.7 us (25%)
  waiting for transfers between devices  7.04 us (10%)
  Pallas kernels  4.71 us (7%)
    all_to_all x1, starting transfers between devices, per_device(): recv = lax.all_to_all(pay, ('y', 'xl', 'core'), 0, 0, tiled=True)  17.8 us
    all_to_all x1, blocking collectives, per_device(): msg = lax.all_to_all(msg, 'z', 0, 0, tiled=True)  17.7 us
    ppermute x4, starting transfers between devices, from_ahead(): return lax.ppermute(tile, 'y', [((i + k) % M, i) for i in range(M)])  15.4 us
    all_to_all x1, starting transfers between devices, per_device(): msg = lax.all_to_all(msg, ('y', 'xh', 'xl', 'core'), 0, 0, tiled=True)  6.78 us
    all_to_all x1, waiting for transfers between devices, per_device(): recv = lax.all_to_all(pay, ('y', 'xl', 'core'), 0, 0, tiled=True)  3.57 us
    all_to_all x1, waiting for transfers between devices, per_device(): msg = lax.all_to_all(msg, ('y', 'xh', 'xl', 'core'), 0, 0, tiled=True)  2.4 us
    pallas_call x1, Pallas kernels, per_device(): call(pack_kernel, (shape((GROUP, 32, 128), BF16), shape((INV + C, 128), F...  1.98 us
  transfers between devices with their start and end apart: 6, of which 3 were waited for; matrix products, arithmetic and copies ran while one was open for 0% of the time, Pallas kernels for 2%

profile of v12, /device:TPU:1, one launch (start us, length us, event | category | flops | bytes accessed | tf_op | source)
XLA Modules:
  0.0 69.6 jit_solution(7909639164770269369)
XLA Ops:
  0.0 2.0 %shard_map.37 = (bf16[32,32,128]{2,1,0:T(8,128)(2,1)}, f32[32,128]{1,0:T(8,128)}) custom-call(f32[16]{0:T(128)} %scales_hbm.1, bf16[1,16,24,256]{3,2,1,0:T(8,128)(2,1)} %own_ref.5, bf16[16,24,256]{2,1,0:T(8,128)(2,1)} %obs_ref.1), custom_call_target="tpu_custom_call" | custom-call | flops 1048576 | bytes 1048576 | tf_op jit(solution)/shard_map/pallas_call | solution.py:263
  2.0 0.0 copy-start
  2.0 0.0 copy-start.2
  2.0 17.8 %all-to-all-start = ((bf16[32,32,128]{2,1,0:T(8,128)(2,1)}), bf16[32,32,128]{2,1,0:T(8,128)(2,1)S(1)}, u32[]{:S(2)}, u32[]{:S(2)}) async-start(bf16[32,32,128]{2,1,0:T(8,128)(2,1)} %get-tuple-element.15), calls=%async_computation | async-start | bytes 524288 | tf_op jit(solution)/shard_map/all_to_all | solution.py:277
  19.8 0.0 copy-done
  19.9 5.6 %collective-permute-start.1 = (bf16[16,24,256]{2,1,0:T(8,128)(2,1)S(1)}, bf16[16,24,256]{2,1,0:T(8,128)(2,1)S(1)}, u32[]{:S(2)}, u32[]{:S(2)}) collective-permute-start(bf16[16,24,256]{2,1,0:T(8,128)(2,1)S(1)} %bitcast.1), channel_id=1, source_target_pairs={{256,0},{384,128},{512,256},{640,384},{768,512},{896,640},{0,768},... | collective-permute-start | bytes 589832 | tf_op jit(solution)/shard_map/ppermute | solution.py:257
  25.4 1.9 %collective-permute-start = (bf16[16,24,256]{2,1,0:T(8,128)(2,1)S(1)}, bf16[16,24,256]{2,1,0:T(8,128)(2,1)S(1)}, u32[]{:S(2)}, u32[]{:S(2)}) collective-permute-start(bf16[16,24,256]{2,1,0:T(8,128)(2,1)S(1)} %bitcast.2), channel_id=1, source_target_pairs={{640,0},{768,128},{896,256},{0,384},{128,512},{256,640},{384,768},... | collective-permute-start | bytes 589832 | tf_op jit(solution)/shard_map/ppermute | solution.py:257
  27.3 3.6 %all-to-all-done.recv_ref = bf16[32,32,128]{2,1,0:T(8,128)(2,1)S(1)} async-done(((bf16[32,32,128]{2,1,0:T(8,128)(2,1)}), bf16[32,32,128]{2,1,0:T(8,128)(2,1)S(1)}, u32[]{:S(2)}, u32[]{:S(2)}) %all-to-all-start) | async-done | bytes 262176 | tf_op jit(solution)/shard_map/all_to_all | solution.py:277
  30.9 0.0 copy-done.2
  30.9 1.2 %shard_map.38 = (f32[128,1,128]{2,1,0:T(1,128)}, f32[8,8,128]{2,1,0:T(8,128)S(1)}, f32[8,128]{1,0:T(8,128)S(1)}) custom-call(bf16[32,32,128]{2,1,0:T(8,128)(2,1)S(1)} %all-to-all-done.recv_ref, f32[32,128]{1,0:T(8,128)S(1)} %copy-done.2), custom_call_target="tpu_custom_call" | custom-call | flops 68719476736 | bytes 68719476736 | tf_op jit(solution)/shard_map/pallas_call | solution.py:279
  32.1 6.8 %all-to-all-start.1 = ((f32[128,1,128]{2,1,0:T(1,128)}), f32[128,1,128]{2,1,0:T(1,128)S(1)}, u32[]{:S(2)}, u32[]{:S(2)}) async-start(f32[128,1,128]{2,1,0:T(1,128)} %get-tuple-element.16), calls=%async_computation.1 | async-start | bytes 131072 | tf_op jit(solution)/shard_map/all_to_all | solution.py:287
  38.9 0.0 collective-permute-done.1.up_ref
  38.9 1.1 %collective-permute-done.down_ref = bf16[16,24,256]{2,1,0:T(8,128)(2,1)S(1)} collective-permute-done((bf16[16,24,256]{2,1,0:T(8,128)(2,1)S(1)}, bf16[16,24,256]{2,1,0:T(8,128)(2,1)S(1)}, u32[]{:S(2)}, u32[]{:S(2)}) %collective-permute-start) | collective-permute-done | bytes 196640 | tf_op jit(solution)/shard_map/ppermute | solution.py:257
  40.0 0.1 shard_map.41
  40.0 5.7 %collective-permute-start.2 = (bf16[40,24,256]{2,1,0:T(8,128)(2,1)S(1)}, bf16[40,24,256]{2,1,0:T(8,128)(2,1)S(1)}, u32[]{:S(2)}, u32[]{:S(2)}) collective-permute-start(bf16[40,24,256]{2,1,0:T(8,128)(2,1)S(1)} %get-tuple-element.21), channel_id=1, source_target_pairs={{128,0},{256,128},{384,256},{512,384},{640,512},{768,640},{896,768... | collective-permute-start | bytes 1474568 | tf_op jit(solution)/shard_map/ppermute | solution.py:257
  45.8 0.0 copy-start.1
  45.8 2.2 %collective-permute-start.3 = (bf16[40,24,256]{2,1,0:T(8,128)(2,1)S(1)}, bf16[40,24,256]{2,1,0:T(8,128)(2,1)S(1)}, u32[]{:S(2)}, u32[]{:S(2)}) collective-permute-start(bf16[40,24,256]{2,1,0:T(8,128)(2,1)S(1)} %get-tuple-element.22), channel_id=1, source_target_pairs={{896,0},{0,128},{128,256},{256,384},{384,512},{512,640},{640,768},... | collective-permute-start | bytes 1474568 | tf_op jit(solution)/shard_map/ppermute | solution.py:257
  48.0 2.4 %all-to-all-done.1.in_ref = f32[128,1,128]{2,1,0:T(1,128)S(1)} async-done(((f32[128,1,128]{2,1,0:T(1,128)}), f32[128,1,128]{2,1,0:T(1,128)S(1)}, u32[]{:S(2)}, u32[]{:S(2)}) %all-to-all-start.1) | async-done | bytes 65568 | tf_op jit(solution)/shard_map/all_to_all | solution.py:287
  50.4 0.1 shard_map.39
  50.5 17.7 %all_to_all.15.msg_ref = f32[8,1,128]{2,1,0:T(1,128)S(1)} all-to-all(f32[8,1,128]{2,1,0:T(1,128)S(1)} %shard_map.39), channel_id=1, replica_groups=mesh['y'=8,'z'=8,'xh'=4,'xl'=2,'core'=2] {'z'}, dimensions={0} | all-to-all | bytes 8192 | tf_op jit(solution)/shard_map/all_to_all | solution.py:294
  68.2 0.3 shard_map.40
  68.5 0.0 collective-permute-done.2.ups_ref
  68.5 0.0 collective-permute-done.3.downs_ref
  68.5 1.1 %shard_map.42 = f32[1,16,24,256]{3,2,1,0:T(8,128)} custom-call(f32[32,128]{1,0:T(8,128)S(1)} %copy-done.2, f32[16,128]{1,0:T(8,128)S(1)} %get-tuple-element.18.coef_ref, f32[16,24,256]{2,1,0:T(8,128)S(1)} %get-tuple-element.19.begun_ref, bf16[1,16,24,256]{3,2,1,0:T(8,128)(2,1)S(1)} %copy-done, bf16[40,24,256]{2,1,0:T(8,128)(2,1)S(1)} %collective-permute-done.2.ups_ref, ...), custom_call_target="tpu_custom_call" | custom-call | flops 4194304 | bytes 4194304 | tf_op jit(solution)/shard_map/pallas_call | solution.py:303
  (1 shorter events, 0.0 us)
Async XLA Ops:
  2.0 17.9 %copy-start = (bf16[1,16,24,256]{3,2,1,0:T(8,128)(2,1)S(1)}, bf16[1,16,24,256]{3,2,1,0:T(8,128)(2,1)}, u32[]{:S(2)}) copy-start(bf16[1,16,24,256]{3,2,1,0:T(8,128)(2,1)} %own_ref.5) | copy-start | bytes 589828
  2.0 28.9 %copy-start.2 = (f32[32,128]{1,0:T(8,128)S(1)}, f32[32,128]{1,0:T(8,128)}, u32[]{:S(2)}) copy-start(f32[32,128]{1,0:T(8,128)} %get-tuple-element.14.aux_ref) | copy-start | bytes 49156
  2.0 28.9 %all-to-all-start = ((bf16[32,32,128]{2,1,0:T(8,128)(2,1)}), bf16[32,32,128]{2,1,0:T(8,128)(2,1)S(1)}, u32[]{:S(2)}, u32[]{:S(2)}) async-start(bf16[32,32,128]{2,1,0:T(8,128)(2,1)} %get-tuple-element.15), calls=%async_computation | async-start | bytes 524288 | tf_op jit(solution)/shard_map/all_to_all | solution.py:277
  19.9 19.0 %collective-permute-start.1 = (bf16[16,24,256]{2,1,0:T(8,128)(2,1)S(1)}, bf16[16,24,256]{2,1,0:T(8,128)(2,1)S(1)}, u32[]{:S(2)}, u32[]{:S(2)}) collective-permute-start(bf16[16,24,256]{2,1,0:T(8,128)(2,1)S(1)} %bitcast.1), channel_id=1, source_target_pairs={{256,0},{384,128},{512,256},{640,384},{768,512},{896,640},{0,768},... | collective-permute-start | bytes 589832 | tf_op jit(solution)/shard_map/ppermute | solution.py:257
  25.4 14.5 %collective-permute-start = (bf16[16,24,256]{2,1,0:T(8,128)(2,1)S(1)}, bf16[16,24,256]{2,1,0:T(8,128)(2,1)S(1)}, u32[]{:S(2)}, u32[]{:S(2)}) collective-permute-start(bf16[16,24,256]{2,1,0:T(8,128)(2,1)S(1)} %bitcast.2), channel_id=1, source_target_pairs={{640,0},{768,128},{896,256},{0,384},{128,512},{256,640},{384,768},... | collective-permute-start | bytes 589832 | tf_op jit(solution)/shard_map/ppermute | solution.py:257
  32.1 18.3 %all-to-all-start.1 = ((f32[128,1,128]{2,1,0:T(1,128)}), f32[128,1,128]{2,1,0:T(1,128)S(1)}, u32[]{:S(2)}, u32[]{:S(2)}) async-start(f32[128,1,128]{2,1,0:T(1,128)} %get-tuple-element.16), calls=%async_computation.1 | async-start | bytes 131072 | tf_op jit(solution)/shard_map/all_to_all | solution.py:287
  40.0 28.5 %collective-permute-start.2 = (bf16[40,24,256]{2,1,0:T(8,128)(2,1)S(1)}, bf16[40,24,256]{2,1,0:T(8,128)(2,1)S(1)}, u32[]{:S(2)}, u32[]{:S(2)}) collective-permute-start(bf16[40,24,256]{2,1,0:T(8,128)(2,1)S(1)} %get-tuple-element.21), channel_id=1, source_target_pairs={{128,0},{256,128},{384,256},{512,384},{640,512},{768,640},{896,768... | collective-permute-start | bytes 1474568 | tf_op jit(solution)/shard_map/ppermute | solution.py:257
  45.8 22.5 %copy-start.1 = (bf16[16,24,256]{2,1,0:T(8,128)(2,1)S(1)}, bf16[16,24,256]{2,1,0:T(8,128)(2,1)}, u32[]{:S(2)}) copy-start(bf16[16,24,256]{2,1,0:T(8,128)(2,1)} %obs_ref.1) | copy-start | bytes 589828
  45.8 22.8 %collective-permute-start.3 = (bf16[40,24,256]{2,1,0:T(8,128)(2,1)S(1)}, bf16[40,24,256]{2,1,0:T(8,128)(2,1)S(1)}, u32[]{:S(2)}, u32[]{:S(2)}) collective-permute-start(bf16[40,24,256]{2,1,0:T(8,128)(2,1)S(1)} %get-tuple-element.22), channel_id=1, source_target_pairs={{896,0},{0,128},{128,256},{256,384},{384,512},{512,640},{640,768},... | collective-permute-start | bytes 1474568 | tf_op jit(solution)/shard_map/ppermute | solution.py:257
